TPU v7x, 32 devices: a whole 2x2x4 slice. The times are simulated.
32 devices in a mesh: groups: 2 (over y), adapter: 4 (over z), tensor: 4 (over x, core).
Axes of the slice: x: 2, y: 2, z: 4, core: 2. Of those that a mesh axis runs over, the one named last changes fastest.
Arguments:
- hidden: bfloat16 [256, 8192], P(('groups', 'adapter'), 'tensor'), parts along dimension 0, may hold values from -6 to 6
- base_queries: bfloat16 [256, 8192], P(('groups', 'adapter'), 'tensor'), parts along dimension 0, may hold values from -6 to 6
- base_keys: bfloat16 [256, 1024], P(('groups', 'adapter'), 'tensor'), parts along dimension 0, may hold values from -6 to 6
- base_values: bfloat16 [256, 1024], P(('groups', 'adapter'), 'tensor'), parts along dimension 0, may hold values from -6 to 6
- adapter_down_weight: bfloat16 [32, 96, 8192], P('adapter', None, 'tensor'), may hold values from -0.0625 to 0.0625
- adapter_up_query: bfloat16 [32, 32, 8192], P(None, None, ('adapter', 'tensor')), may hold values from -1 to 1
- adapter_up_key_value: bfloat16 [32, 2, 32, 1024], P(None, None, None, ('adapter', 'tensor')), may hold values from -1 to 1
- cached_keys: bfloat16 [256, 8, 128, 128], P(('groups', 'adapter'), 'tensor'), parts along dimension 0, may hold values from -400 to 400
- cached_values: bfloat16 [256, 8, 128, 128], P(('groups', 'adapter'), 'tensor'), parts along dimension 0, may hold values from -6 to 6
- request_adapter: int32 [256], P(('groups', 'adapter')), parts along dimension 0, may hold values from 0 to 31
- lengths: int32 [256], P(('groups', 'adapter')), parts along dimension 0, may hold values from 1 to 128, 8192 in all
Outputs:
- attention: bfloat16 [256, 8192], P(('groups', 'adapter'), 'tensor'), parts along dimension 0
- fresh_keys: bfloat16 [256, 1024], P(('groups', 'adapter'), 'tensor'), parts along dimension 0
- fresh_values: bfloat16 [256, 1024], P(('groups', 'adapter'), 'tensor'), parts along dimension 0
There are 2 independent parts, one for each index of `groups`. A program takes and returns all parts, laid end to end along the dimension named above; an argument that names none is the same for every part. Nothing has to cross between parts.
Inputs may be any that keep to these rules, and one draw needn't show every extreme that they name: The lengths of the 128 requests of ONE part (one serving replica) sum to 8192, and some request of each part has exactly 128; over an array that lays several parts end to end the total is that sum times the number of parts.
All inputs are finite; a program needn't handle non-finite values. No bound on the sum of `lengths` on one device may be relied on, other than what follows from the above.
Results may differ from a plain program's by a relative error of at most 0.0088.
Values may be sent and summed in bfloat16 or wider, within the bound.
No kernel may reach another device: no remote copies, remote signals or barrier semaphores. Data moves between devices by JAX's collectives and lax.ppermute only.
A program may use at most 64 MiB of HBM per device.

v0:
```python
import math

import jax
import jax.numpy as jnp
from jax import lax
from jax.sharding import PartitionSpec as P

ADAPTER_SCALE = 0.5
ROPE_BASE = 500000.0


def rotate_pairs(vectors, positions):
    half_dim = vectors.shape[-1] // 2
    inv_freq = jnp.exp(
        -jnp.arange(half_dim, dtype=jnp.float32) * (2.0 / vectors.shape[-1]) * math.log(ROPE_BASE)
    )
    angles = positions.astype(jnp.float32)[:, None, None] * inv_freq[None, None, :]
    cosine = jnp.cos(angles)
    sine_part = jnp.sin(angles)
    front_half = vectors[..., :half_dim]
    back_half = vectors[..., half_dim:]
    return jnp.concatenate(
        [front_half * cosine - back_half * sine_part, front_half * sine_part + back_half * cosine],
        axis=-1,
    )


def attend_cache(query_vector, key_new, value_new, cached_keys, cached_values, lengths):
    local_requests, query_heads, head_dim = query_vector.shape
    kv_heads = key_new.shape[1]
    grouped = query_vector.reshape(local_requests, kv_heads, query_heads // kv_heads, head_dim)
    inv_sqrt = 1.0 / math.sqrt(head_dim)
    cache_scores = (
        jnp.einsum("rkge,rkpe->rkgp", grouped, cached_keys, preferred_element_type=jnp.float32)
        * inv_sqrt
    )
    in_cache = jnp.arange(cached_keys.shape[2], dtype=jnp.int32)[None, :] < lengths[:, None]
    cache_scores = jnp.where(in_cache[:, None, None, :], cache_scores, -jnp.inf)
    new_score = (
        jnp.einsum("rkge,rke->rkg", grouped, key_new, preferred_element_type=jnp.float32) * inv_sqrt
    )
    row_max = jnp.maximum(jnp.max(cache_scores, axis=-1), new_score)
    cache_weights = jnp.exp(cache_scores - row_max[..., None])
    new_weight = jnp.exp(new_score - row_max)
    softmax_sum = jnp.sum(cache_weights, axis=-1) + new_weight
    cache_weights = (cache_weights / softmax_sum[..., None]).astype(jnp.bfloat16)
    new_weight = (new_weight / softmax_sum).astype(jnp.bfloat16)
    mixed = jnp.einsum(
        "rkgp,rkpe->rkge", cache_weights, cached_values, preferred_element_type=jnp.float32
    )
    mixed = (
        mixed
        + new_weight.astype(jnp.float32)[..., None] * value_new.astype(jnp.float32)[:, :, None, :]
    )
    return mixed.reshape(local_requests, query_heads * head_dim).astype(jnp.bfloat16)


def body(
    hidden,
    base_queries,
    base_keys,
    base_values,
    adapter_down_weight,
    adapter_up_query,
    adapter_up_key_value,
    cached_keys,
    cached_values,
    request_adapter,
    lengths,
):
    owner_index = lax.axis_index("adapter")
    owning_requests = lax.axis_size("adapter")
    holding_count = adapter_down_weight.shape[0]
    rank_width = adapter_up_query.shape[1]
    local_requests = hidden.shape[0]
    everyone, every_id = (
        lax.all_gather(hidden, "adapter", axis=0, tiled=True),
        lax.all_gather(request_adapter, "adapter", axis=0, tiled=True),
    )
    every_row = everyone.shape[0]
    slot_of = every_id - owner_index * holding_count
    picked = slot_of[:, None] == jnp.arange(holding_count, dtype=jnp.int32)[None, :]
    picked_float = picked.astype(jnp.float32)
    flattened_lowered = adapter_down_weight.reshape(
        holding_count * 3 * rank_width, adapter_down_weight.shape[2]
    )
    partial_value = lax.dot_general(
        everyone, flattened_lowered, (((1,), (1,)), ((), ())), preferred_element_type=jnp.float32
    )
    summed = lax.psum(partial_value, "tensor")
    mine = jnp.sum(
        summed.reshape(every_row, holding_count, 3 * rank_width) * picked_float[:, :, None], axis=1
    )
    shrink_rank = lax.psum(mine.astype(jnp.bfloat16), "adapter").astype(jnp.float32)
    shrink_rank = shrink_rank.astype(jnp.bfloat16)

    def expand_rank(segment, factors):
        rows_used = jnp.take(factors, every_id, axis=0)
        rank_product = jnp.einsum(
            "rj,rjc->rc", segment, rows_used, preferred_element_type=jnp.float32
        )
        column_width = rank_product.shape[1]
        return (ADAPTER_SCALE * rank_product).reshape(
            owning_requests, every_row // owning_requests, 1, column_width
        )

    query_portion = expand_rank(shrink_rank[:, :rank_width], adapter_up_query)
    key_portion = expand_rank(
        shrink_rank[:, rank_width : 2 * rank_width], adapter_up_key_value[:, 0]
    )
    value_portion = expand_rank(shrink_rank[:, 2 * rank_width :], adapter_up_key_value[:, 1])
    arrived = (
        lax.all_to_all(
            lax.all_to_all(query_portion, "adapter", split_axis=0, concat_axis=2, tiled=True),
            "tensor",
            split_axis=2,
            concat_axis=0,
            tiled=True,
        ),
        lax.all_to_all(
            lax.all_to_all(key_portion, "adapter", split_axis=0, concat_axis=2, tiled=True),
            "tensor",
            split_axis=2,
            concat_axis=0,
            tiled=True,
        ),
        lax.all_to_all(
            lax.all_to_all(value_portion, "adapter", split_axis=0, concat_axis=2, tiled=True),
            "tensor",
            split_axis=2,
            concat_axis=0,
            tiled=True,
        ),
    )

    def columns(values):
        return jnp.transpose(values, (1, 2, 0, 3)).reshape(local_requests, -1)

    query_update = columns(arrived[0])
    key_update = columns(arrived[1])
    value_update = columns(arrived[2])
    head_dim = cached_keys.shape[3]
    kv_heads = cached_keys.shape[1]
    query_heads = base_queries.shape[1] // head_dim
    query_vector = rotate_pairs(
        (base_queries.astype(jnp.float32) + query_update).reshape(
            local_requests, query_heads, head_dim
        ),
        lengths,
    ).astype(jnp.bfloat16)
    fresh_keys = rotate_pairs(
        (base_keys.astype(jnp.float32) + key_update).reshape(local_requests, kv_heads, head_dim),
        lengths,
    ).astype(jnp.bfloat16)
    fresh_values = (base_values.astype(jnp.float32) + value_update).astype(jnp.bfloat16)
    attention = attend_cache(
        query_vector,
        fresh_keys,
        fresh_values.reshape(local_requests, kv_heads, head_dim),
        cached_keys,
        cached_values,
        lengths,
    )
    return (attention, fresh_keys.reshape(local_requests, kv_heads * head_dim), fresh_values)


def solution(mesh):
    return jax.shard_map(
        body,
        mesh=mesh,
        in_specs=(
            P(("groups", "adapter"), "tensor"),
            P(("groups", "adapter"), "tensor"),
            P(("groups", "adapter"), "tensor"),
            P(("groups", "adapter"), "tensor"),
            P("adapter", None, "tensor"),
            P(None, None, ("adapter", "tensor")),
            P(None, None, None, ("adapter", "tensor")),
            P(("groups", "adapter"), "tensor", None, None),
            P(("groups", "adapter"), "tensor", None, None),
            P(("groups", "adapter")),
            P(("groups", "adapter")),
        ),
        out_specs=(
            P(("groups", "adapter"), "tensor"),
            P(("groups", "adapter"), "tensor"),
            P(("groups", "adapter"), "tensor"),
        ),
        check_vma=False,
    )
```

profile of v0, /device:TPU:0, one launch (start us, length us, event | category | flops | bytes accessed | tf_op | source)
XLA Modules:
  0.0 161.3 jit_solution(11653606395352310396)
XLA Ops:
  7.3 17.7 %all_gather.6 = bf16[128,2048]{1,0:T(8,128)(2,1)S(1)} all-gather(bf16[32,2048]{1,0:T(8,128)(2,1)} %param.13), channel_id=1, replica_groups=mesh['groups'=2,'adapter'=4,'tensor'=4] {'adapter'}, dimensions={0}, use_global_device_ids=true | all-gather | bytes 655360 | tf_op jit(solution)/shard_map/all_gather | solution.py:77
  25.0 1.7 %fusion.33 = f32[128,768]{0,1:T(8,128)} fusion(bf16[128,2048]{1,0:T(8,128)(2,1)S(1)} %all_gather.6, bf16[768,2048]{1,0:T(8,128)(2,1)S(1)} %bitcast.145), kind=kOutput, calls=%fused_computation.76 | convolution fusion | flops 402653184 | bytes 4063232 | tf_op jit(solution)/shard_map/dot_general | solution.py:87
  28.9 8.5 %all-reduce = s32[128]{0:T(128)S(1)} all-reduce(s32[128]{0:T(128)S(1)} %dynamic-update-slice), channel_id=1, replica_groups=mesh['groups'=2,'adapter'=4,'tensor'=4] {'adapter'}, use_global_device_ids=true, to_apply=%add | all-reduce | flops 128 | bytes 1024
  37.5 1.8 %slice_bitcast_fusion.1 = (bf16[32,32,64]{2,1,0:T(8,128)(2,1)S(1)}, bf16[32,32,64]{2,1,0:T(8,128)(2,1)}) fusion(bf16[32,2,32,64]{3,2,1,0:T(8,128)(2,1)} %param.19), kind=kLoop, calls=%fused_computation.24 | loop fusion | bytes 524288 | tf_op jit(solution)/shard_map/squeeze | solution.py:109
  39.3 4.0 %gather_fusion = bf16[128,32,512]{2,1,0:T(8,128)(2,1)} fusion(bf16[32,32,512]{2,1,0:T(8,128)(2,1)} %param.18, s32[1024]{0:T(1024)S(1)} %pad_clamp_fusion), kind=kCustom, calls=%fused_computation.2 | custom fusion | bytes 8389120 | tf_op jit(solution)/shard_map/jit(_take)/gather | solution.py:98
  43.2 2.6 %gather_fusion.2 = bf16[128,32,64]{2,1,0:T(8,128)(2,1)} fusion(bf16[32,32,64]{2,1,0:T(8,128)(2,1)} %get-tuple-element.5, s32[1024]{0:T(1024)S(1)} %pad_clamp_fusion), kind=kCustom, calls=%fused_computation.1.clone | custom fusion | bytes 1049088 | tf_op jit(solution)/shard_map/jit(_take)/gather | solution.py:98
  47.7 13.5 %all-reduce.3.cloned.1.call-done = f32[128,8,96]{0,2,1:T(8,128)} async-done(((f32[128,8,96]{0,2,1:T(8,128)}), f32[128,8,96]{0,2,1:T(8,128)}) %all-reduce.3.cloned.1.call-update) | async-done | bytes 393232 | tf_op jit(solution)/shard_map/psum | solution.py:90
  62.3 19.0 %psum.15 = bf16[128,96]{0,1:T(8,128)(2,1)S(1)} all-reduce(bf16[128,96]{0,1:T(8,128)(2,1)S(1)} %multiply_reduce_fusion), channel_id=1, replica_groups=mesh['groups'=2,'adapter'=4,'tensor'=4] {'adapter'}, use_global_device_ids=true, to_apply=%region_2.0 | all-reduce | flops 12288 | bytes 49152 | tf_op jit(solution)/shard_map/psum | solution.py:94
  81.4 2.9 %fusion = f32[128,1,512]{2,1,0:T(1,128)S(1)} fusion(bf16[128,32,1]{1,2,0:T(2,128)(2,1)S(1)} %copy.58, bf16[128,32,512]{2,1,0:T(8,128)(2,1)} %gather_fusion, pred[128]{0:T(512)(128)(4,1)S(1)} %compare_and_fusion), kind=kOutput, calls=%fused_computation.3 | convolution fusion | flops 6291456 | bytes 4464768 | tf_op jit(solution)/shard_map/rj,rjc->rc/dot_general | solution.py:99
  87.6 3.3 %all-to-all-start.4 = ((f32[4,1,2048]{2,1,0:T(1,128)}), f32[4,1,2048]{2,1,0:T(1,128)S(1)}, u32[]{:S(2)}, u32[]{:S(2)}) async-start(f32[4,1,2048]{2,1,0:T(1,128)} %reshape.221), calls=%async_computation.4 | async-start | bytes 65536 | tf_op jit(solution)/shard_map/all_to_all | solution.py:128
  93.4 3.1 %all-to-all-done.4 = f32[4,1,2048]{2,1,0:T(1,128)S(1)} async-done(((f32[4,1,2048]{2,1,0:T(1,128)}), f32[4,1,2048]{2,1,0:T(1,128)S(1)}, u32[]{:S(2)}, u32[]{:S(2)}) %all-to-all-start.4) | async-done | bytes 32800 | tf_op jit(solution)/shard_map/all_to_all | solution.py:128
  96.5 3.3 %all-to-all-start.2 = ((f32[4,1,2048]{2,1,0:T(1,128)}), f32[4,1,2048]{2,1,0:T(1,128)S(1)}, u32[]{:S(2)}, u32[]{:S(2)}) async-start(f32[4,1,2048]{2,1,0:T(1,128)} %reshape.225), calls=%async_computation.2 | async-start | bytes 65536 | tf_op jit(solution)/shard_map/all_to_all | solution.py:121
  101.9 3.6 %all-to-all-done.2 = f32[4,1,2048]{2,1,0:T(1,128)S(1)} async-done(((f32[4,1,2048]{2,1,0:T(1,128)}), f32[4,1,2048]{2,1,0:T(1,128)S(1)}, u32[]{:S(2)}, u32[]{:S(2)}) %all-to-all-start.2) | async-done | bytes 32800 | tf_op jit(solution)/shard_map/all_to_all | solution.py:121
  105.4 3.3 %all-to-all-start.5 = ((f32[4,1,2048]{2,1,0:T(1,128)}), f32[4,1,2048]{2,1,0:T(1,128)S(1)}, u32[]{:S(2)}, u32[]{:S(2)}) async-start(f32[4,1,2048]{2,1,0:T(1,128)} %reshape.223), calls=%async_computation.5 | async-start | bytes 65536 | tf_op jit(solution)/shard_map/all_to_all | solution.py:127
  110.2 2.4 %all-to-all-done.5 = f32[4,1,2048]{2,1,0:T(1,128)S(1)} async-done(((f32[4,1,2048]{2,1,0:T(1,128)}), f32[4,1,2048]{2,1,0:T(1,128)S(1)}, u32[]{:S(2)}, u32[]{:S(2)}) %all-to-all-start.5) | async-done | bytes 32800 | tf_op jit(solution)/shard_map/all_to_all | solution.py:127
  112.6 3.3 %all-to-all-start.3 = ((f32[4,1,2048]{2,1,0:T(1,128)}), f32[4,1,2048]{2,1,0:T(1,128)S(1)}, u32[]{:S(2)}, u32[]{:S(2)}) async-start(f32[4,1,2048]{2,1,0:T(1,128)} %reshape.227), calls=%async_computation.3 | async-start | bytes 65536 | tf_op jit(solution)/shard_map/all_to_all | solution.py:120
  117.5 2.3 %all-to-all-done.3 = f32[4,1,2048]{2,1,0:T(1,128)S(1)} async-done(((f32[4,1,2048]{2,1,0:T(1,128)}), f32[4,1,2048]{2,1,0:T(1,128)S(1)}, u32[]{:S(2)}, u32[]{:S(2)}) %all-to-all-start.3) | async-done | bytes 32800 | tf_op jit(solution)/shard_map/all_to_all | solution.py:120
  119.8 4.0 %all-to-all-start = ((f32[4,32,1,512]{3,1,2,0:T(8,128)}), f32[4,32,1,512]{3,1,2,0:T(8,128)}, u32[]{:S(2)}, u32[]{:S(2)}) async-start(f32[4,32,1,512]{3,1,2,0:T(8,128)} %bitcast.6), calls=%async_computation | async-start | bytes 524288 | tf_op jit(solution)/shard_map/all_to_all | solution.py:114
  125.0 8.0 %all-to-all-done = f32[4,32,1,512]{3,1,2,0:T(8,128)} async-done(((f32[4,32,1,512]{3,1,2,0:T(8,128)}), f32[4,32,1,512]{3,1,2,0:T(8,128)}, u32[]{:S(2)}, u32[]{:S(2)}) %all-to-all-start) | async-done | bytes 262176 | tf_op jit(solution)/shard_map/all_to_all | solution.py:114
  133.0 3.4 %all-to-all-start.1 = ((f32[1,32,4,512]{3,1,0,2:T(8,128)}), f32[1,32,4,512]{3,1,0,2:T(8,128)S(1)}, u32[]{:S(2)}, u32[]{:S(2)}) async-start(f32[1,32,4,512]{3,1,0,2:T(8,128)} %bitcast.10), calls=%async_computation.1 | async-start | bytes 524288 | tf_op jit(solution)/shard_map/all_to_all | solution.py:113
  137.8 4.6 %all-to-all-done.1 = f32[1,32,4,512]{3,1,0,2:T(8,128)S(1)} async-done(((f32[1,32,4,512]{3,1,0,2:T(8,128)}), f32[1,32,4,512]{3,1,0,2:T(8,128)S(1)}, u32[]{:S(2)}, u32[]{:S(2)}) %all-to-all-start.1) | async-done | bytes 262176 | tf_op jit(solution)/shard_map/all_to_all | solution.py:113
  144.7 2.6 %fusion.30 = (f32[32,2,8]{2,1,0:T(2,128)}, f32[32,2,8,128]{3,2,1,0:T(8,128)S(1)}) fusion(bf16[32,2,128,128]{3,2,1,0:T(8,128)(2,1)S(1)} %copy-done.1, bf16[32,2,8,64]{3,2,1,0:T(8,128)(2,1)S(1)} %get-tuple-element.7, bf16[32,2,8,64]{3,2,1,0:T(8,128)(2,1)S(1)} %get-tuple-element.6, pred[32,128]{1,0:T(8,128)(4,1)} %iota_compare_fusion), kind=kOutput, calls=%fused_computation.69 | convolution fusion | flops 17235456 | bytes 2496512 | tf_op jit(solution)/shard_map/rkge,rkpe->rkgp/dot_general | solution.py:34
  148.2 1.8 %fusion.19 = f32[32,2,1,8]{3,2,1,0:T(1,128)} fusion(bf16[32,2,128,1]{2,1,0,3:T(2,128)(2,1)} %fusion.41, bf16[32,2,8,64]{3,2,1,0:T(8,128)(2,1)} %copy-done.2, bf16[32,2,8,64]{3,2,1,0:T(8,128)(2,1)S(1)} %get-tuple-element.6), kind=kOutput, calls=%fused_computation.42 | convolution fusion | flops 393216 | bytes 149504 | tf_op jit(solution)/shard_map/rkge,rke->rkg/dot_general | solution.py:40
  151.4 2.3 %fusion.5 = bf16[32,2,8,128]{3,2,1,0:T(8,128)(2,1)S(1)} fusion(bf16[32,2,128,128]{3,2,1,0:T(8,128)(2,1)} %param.21, f32[32,2,8,128]{3,2,1,0:T(8,128)S(1)} %get-tuple-element.20, f32[32,2,128]{2,1,0:T(2,128)} %reshape.176, f32[32,2,8]{2,1,0:T(2,128)S(1)} %copy.53, f32[32,2,8]{2,1,0:T(2,128)S(1)} %copy.52, f32[32,2,8]{2,1,0:T(2,128)S(1)} %copy.50), kind=kOutput, calls=%fused_computation.10 | convolution fusion | flops 17170432 | bytes 2529280 | tf_op jit(solution)/shard_map/rkgp,rkpe->rkge/dot_general | solution.py:48
  (88 shorter events, 23.3 us)
Async XLA Ops:
  7.2 17.8 %copy-start = (bf16[8,96,2048]{2,1,0:T(8,128)(2,1)S(1)}, bf16[8,96,2048]{2,1,0:T(8,128)(2,1)}, u32[]{:S(2)}) copy-start(bf16[8,96,2048]{2,1,0:T(8,128)(2,1)} %param.17) | copy-start | bytes 9437188
  7.2 20.3 %copy-start.9 = (u32[32]{0:T(128)S(1)}, u32[32]{0:T(128)}, u32[]{:S(2)}) copy-start(u32[32]{0:T(128)} %constant.51) | copy-start | bytes 388
  7.2 19.6 %copy-start.7 = (s32[32]{0:T(128)S(1)}, s32[32]{0:T(128)}, u32[]{:S(2)}) copy-start(s32[32]{0:T(128)} %param.23) | copy-start | bytes 388
  7.2 21.5 %copy-start.8 = (s32[32]{0:T(128)S(1)}, s32[32]{0:T(128)}, u32[]{:S(2)}) copy-start(s32[32]{0:T(128)} %param.22) | copy-start | bytes 388
  7.2 54.0 %all-reduce.3.cloned.1.call-start = ((), (), s32[]{:S(2)}) async-start(), calls=%async_computation.6 | async-start | bytes 786432 | tf_op jit(solution)/shard_map/psum | solution.py:90
  47.7 77.2 %copy-start.3 = (f32[32,64]{1,0:T(8,128)}, f32[32,64]{1,0:T(8,128)S(1)}, u32[]{:S(2)}) copy-start(f32[32,64]{1,0:T(8,128)S(1)} %get-tuple-element.16) | copy-start | bytes 24580
  84.3 32.6 %copy-start.6 = (bf16[32,256]{1,0:T(8,128)(2,1)S(1)}, bf16[32,256]{1,0:T(8,128)(2,1)}, u32[]{:S(2)}) copy-start(bf16[32,256]{1,0:T(8,128)(2,1)} %param.16) | copy-start | bytes 49156
  85.1 39.7 %copy-start.5 = (bf16[32,256]{1,0:T(8,128)(2,1)S(1)}, bf16[32,256]{1,0:T(8,128)(2,1)}, u32[]{:S(2)}) copy-start(bf16[32,256]{1,0:T(8,128)(2,1)} %param.15) | copy-start | bytes 49156
  87.6 8.9 %all-to-all-start.4 = ((f32[4,1,2048]{2,1,0:T(1,128)}), f32[4,1,2048]{2,1,0:T(1,128)S(1)}, u32[]{:S(2)}, u32[]{:S(2)}) async-start(f32[4,1,2048]{2,1,0:T(1,128)} %reshape.221), calls=%async_computation.4 | async-start | bytes 65536 | tf_op jit(solution)/shard_map/all_to_all | solution.py:128
  96.5 8.9 %all-to-all-start.2 = ((f32[4,1,2048]{2,1,0:T(1,128)}), f32[4,1,2048]{2,1,0:T(1,128)S(1)}, u32[]{:S(2)}, u32[]{:S(2)}) async-start(f32[4,1,2048]{2,1,0:T(1,128)} %reshape.225), calls=%async_computation.2 | async-start | bytes 65536 | tf_op jit(solution)/shard_map/all_to_all | solution.py:121
  105.4 7.2 %all-to-all-start.5 = ((f32[4,1,2048]{2,1,0:T(1,128)}), f32[4,1,2048]{2,1,0:T(1,128)S(1)}, u32[]{:S(2)}, u32[]{:S(2)}) async-start(f32[4,1,2048]{2,1,0:T(1,128)} %reshape.223), calls=%async_computation.5 | async-start | bytes 65536 | tf_op jit(solution)/shard_map/all_to_all | solution.py:127
  112.6 7.2 %all-to-all-start.3 = ((f32[4,1,2048]{2,1,0:T(1,128)}), f32[4,1,2048]{2,1,0:T(1,128)S(1)}, u32[]{:S(2)}, u32[]{:S(2)}) async-start(f32[4,1,2048]{2,1,0:T(1,128)} %reshape.227), calls=%async_computation.3 | async-start | bytes 65536 | tf_op jit(solution)/shard_map/all_to_all | solution.py:120
  116.9 26.9 %copy-start.4 = (bf16[32,256]{1,0:T(8,128)(2,1)}, bf16[32,256]{1,0:T(8,128)(2,1)S(1)}, u32[]{:S(2)}) copy-start(bf16[32,256]{1,0:T(8,128)(2,1)S(1)} %add_convert_fusion.1) | copy-start | bytes 49156
  119.8 13.2 %all-to-all-start = ((f32[4,32,1,512]{3,1,2,0:T(8,128)}), f32[4,32,1,512]{3,1,2,0:T(8,128)}, u32[]{:S(2)}, u32[]{:S(2)}) async-start(f32[4,32,1,512]{3,1,2,0:T(8,128)} %bitcast.6), calls=%async_computation | async-start | bytes 524288 | tf_op jit(solution)/shard_map/all_to_all | solution.py:114
  133.0 9.4 %all-to-all-start.1 = ((f32[1,32,4,512]{3,1,0,2:T(8,128)}), f32[1,32,4,512]{3,1,0,2:T(8,128)S(1)}, u32[]{:S(2)}, u32[]{:S(2)}) async-start(f32[1,32,4,512]{3,1,0,2:T(8,128)} %bitcast.10), calls=%async_computation.1 | async-start | bytes 524288 | tf_op jit(solution)/shard_map/all_to_all | solution.py:113
  142.4 2.3 %copy-start.1 = (bf16[32,2,128,128]{3,2,1,0:T(8,128)(2,1)S(1)}, bf16[32,2,128,128]{3,2,1,0:T(8,128)(2,1)}, u32[]{:S(2)}) copy-start(bf16[32,2,128,128]{3,2,1,0:T(8,128)(2,1)} %param.20) | copy-start | bytes 6291460
  144.7 2.6 %copy-start.2 = (bf16[32,2,8,64]{3,2,1,0:T(8,128)(2,1)}, bf16[32,2,8,64]{3,2,1,0:T(8,128)(2,1)S(1)}, u32[]{:S(2)}) copy-start(bf16[32,2,8,64]{3,2,1,0:T(8,128)(2,1)S(1)} %get-tuple-element.7) | copy-start | bytes 196612
Sparse Core Ops, SparseCore 0:
  26.8 34.3 all-reduce.2
where the time goes:
time: 162 us; the launch traced here: 161 us
  blocking collectives  45.2 us (28%)
  waiting for transfers between devices  37.5 us (23%)
  starting transfers between devices  20.5 us (13%)
  local copies, waits for them, and re-layouts  19.6 us (12%)
  between operations  15.1 us (9%)
  matrix products  14.8 us (9%)
  other arithmetic  8.66 us (5%)
    psum x1, blocking collectives, body(): lax.psum(mine.astype(jnp.bfloat16), 'adapter').astype(jnp.float32)  19 us
    all_gather x1, blocking collectives, body(): lax.all_gather(hidden, 'adapter', axis=0, tiled=True)  17.7 us
    psum x1, waiting for transfers between devices, body(): summed = lax.psum(partial_value, 'tensor')  13.5 us
    unnamed x1, blocking collectives  8.53 us
    gather x3, local copies, waits for them, and re-layouts, expand_rank(): rows_used = jnp.take(factors, every_id, axis=0)  8.29 us
    all_to_all x1, waiting for transfers between devices, body(): lax.all_to_all(query_portion, 'adapter', split_axis=0, concat_axis=2, til...  7.99 us
    dot_general x3, matrix products, expand_rank(): jnp.einsum('rj,rjc->rc', segment, rows_used, preferred_element_type=jnp.f...  6.29 us
    unnamed x37, local copies, waits for them, and re-layouts  5.59 us
  transfers between devices with their start and end apart: 7, of which 7 were waited for; matrix products, arithmetic and copies ran while one was open for 14% of the time, Pallas kernels for 0%

commit v1 on v0

--- a/solution.py
+++ b/solution.py
@@ -1,12 +1,352 @@
+import functools
 import math
 
 import jax
 import jax.numpy as jnp
 from jax import lax
+from jax.experimental import pallas as pl
+from jax.experimental.pallas import tpu as pltpu
 from jax.sharding import PartitionSpec as P
 
 ADAPTER_SCALE = 0.5
 ROPE_BASE = 500000.0
+LANES = 128
+VMEM_BYTES = 16 * 1024 * 1024
+
+
+def rotation_factors(positions, head_dim):
+    half_dim = head_dim // 2
+    inv_freq = jnp.exp(
+        -jnp.arange(half_dim, dtype=jnp.float32) * (2.0 / head_dim) * math.log(ROPE_BASE)
+    )
+    angles = positions.astype(jnp.float32)[:, None] * inv_freq[None, :]
+    return jnp.cos(angles), jnp.sin(angles)
+
+
+def swap_blocks(row, place, block):
+    lane = lax.broadcasted_iota(jnp.int32, row.shape, 1)
+    far = pltpu.roll(row, 2 * block, 1)
+    row = jnp.where((place & 2) != 0, far, row)
+    up, down = pltpu.roll(row, block, 1), pltpu.roll(row, LANES - block, 1)
+    near = jnp.where((lane // block) % 2 == 0, down, up)
+    return jnp.where((place & 1) != 0, near, row)
+
+
+def down_kernel(place_ref, ids_ref, *refs):
+    *hidden_refs, down_ref, out_ref, ids_out_ref, rows_ref = refs
+    place = place_ref[0]
+    block = hidden_refs[0].shape[0]
+    for k, hidden_ref in enumerate(hidden_refs):
+        start = pl.multiple_of((place ^ k) * block, block)
+        rows_ref[pl.ds(start, block), :] = hidden_ref[...]
+    held = down_ref.shape[0]
+    ids = swap_blocks(jnp.broadcast_to(ids_ref[...], (8, LANES)), place, block)[0:1]
+    ids_out_ref[...] = ids
+    product = lax.dot_general(
+        down_ref[...].reshape(held * down_ref.shape[1], down_ref.shape[2]),
+        rows_ref[...],
+        (((1,), (1,)), ((), ())),
+        preferred_element_type=jnp.float32,
+    )
+    slot = ids - place * held
+    rank = down_ref.shape[1]
+    total = jnp.zeros(out_ref.shape, jnp.float32)
+    for s in range(held):
+        total += jnp.where(slot == s, product[s * rank : (s + 1) * rank], 0.0)
+    out_ref[...] = total
+
+
+def up_kernel(place_ref, ids_ref, *refs):
+    shrink_refs = refs[:4]
+    up_query_ref, up_kv_ref, *out_refs, terms_ref = refs[4:]
+    shrink = shrink_refs[0][...].astype(jnp.float32)
+    for ref in shrink_refs[1:]:
+        shrink += ref[...].astype(jnp.float32)
+    rank = shrink.shape[0] // 3
+    rows = shrink.shape[1]
+    shrink = jnp.concatenate([shrink, jnp.zeros((LANES - 3 * rank, rows), jnp.float32)], axis=0)
+    shrink = jnp.transpose(shrink)
+    ids = jnp.transpose(jnp.broadcast_to(ids_ref[...].astype(jnp.float32), (LANES, rows)))
+    lane = lax.broadcasted_iota(jnp.int32, (rows, LANES), 1)
+    count = up_query_ref.shape[0]
+    query = jnp.concatenate([shrink[:, :rank]] * (LANES // rank), axis=1)
+    lane_slot = (lane // rank).astype(jnp.float32)
+    step = LANES // rank
+    spread = jnp.concatenate(
+        [
+            jnp.where(ids - c * step == lane_slot, query, 0.0).astype(jnp.bfloat16)
+            for c in range(count // step)
+        ],
+        axis=1,
+    )
+    terms_ref[:, : up_query_ref.shape[2]] = ADAPTER_SCALE * jnp.dot(
+        spread,
+        up_query_ref[...].reshape(count * rank, up_query_ref.shape[2]),
+        preferred_element_type=jnp.float32,
+    )
+    pair = jnp.concatenate([shrink[:, rank : 3 * rank]] * (LANES // (2 * rank)), axis=1)
+    lane_slot = (lane // (2 * rank)).astype(jnp.float32)
+    is_key = (lane // rank) % 2 == 0
+    key, value = jnp.where(is_key, pair, 0.0), jnp.where(is_key, 0.0, pair)
+    step = LANES // (2 * rank)
+    both = []
+    for part in (key, value):
+        both.append(
+            jnp.concatenate(
+                [
+                    jnp.where(ids - c * step == lane_slot, part, 0.0).astype(jnp.bfloat16)
+                    for c in range(count // step)
+                ],
+                axis=1,
+            )
+        )
+    kv_width = up_kv_ref.shape[3]
+    kv = ADAPTER_SCALE * jnp.dot(
+        jnp.concatenate(both, axis=0),
+        up_kv_ref[...].reshape(count * 2 * rank, kv_width),
+        preferred_element_type=jnp.float32,
+    )
+    terms_ref[:, up_query_ref.shape[2] :] = jnp.concatenate([kv[:rows], kv[rows:]], axis=1)
+    block = out_refs[0].shape[0]
+    for k, out_ref in enumerate(out_refs):
+        start = pl.multiple_of((place_ref[1] ^ k) * block, block)
+        out_ref[...] = terms_ref[pl.ds(start, block), :]
+
+
+def attend_kernel(place_ref, lengths_ref, *refs):
+    term_refs = refs[:4]
+    (
+        base_query_ref,
+        base_key_ref,
+        base_value_ref,
+        cosine_ref,
+        sine_ref,
+        keys_ref,
+        values_ref,
+        out_ref,
+        fresh_key_ref,
+        fresh_value_ref,
+        terms_ref,
+        query_ref,
+        key_ref,
+        value_ref,
+        score_ref,
+        weight_ref,
+        new_weight_ref,
+    ) = refs[4:]
+    place = place_ref[0]
+    for k, term_ref in enumerate(term_refs):
+        terms_ref[place ^ k] = term_ref[...]
+    requests = base_query_ref.shape[0]
+    kv_heads = keys_ref.shape[1]
+    slots, head = keys_ref.shape[2], keys_ref.shape[3]
+    half = head // 2
+    heads = base_query_ref.shape[1] // head
+    group = heads // kv_heads
+    each = terms_ref.shape[2] // head - 1
+    cosine, sine = cosine_ref[...], sine_ref[...]
+    lane = lax.broadcasted_iota(jnp.int32, (requests, head), 1)
+    cosine = jnp.concatenate([cosine, cosine], axis=1)
+    sine = jnp.concatenate([-sine, sine], axis=1)
+
+    def rotate(u):
+        return (u * cosine + pltpu.roll(u, half, 1) * sine).astype(jnp.bfloat16)
+
+    for h in range(heads):
+        c = (h % each) * head
+        u = base_query_ref[:, h * head : (h + 1) * head].astype(jnp.float32)
+        u += terms_ref[h // each, :, c : c + head]
+        query_ref[pl.ds(h, requests, stride=heads), :] = rotate(u).astype(jnp.float32)
+    for g in range(kv_heads):
+        low = terms_ref[2 * g, :, each * head :]
+        high = terms_ref[2 * g + 1, :, each * head :]
+        u = base_key_ref[:, g * head : (g + 1) * head].astype(jnp.float32)
+        u += jnp.where(lane < half, low, pltpu.roll(high, half, 1))
+        key = rotate(u)
+        fresh_key_ref[:, g * head : (g + 1) * head] = key
+        key_ref[pl.ds(g, requests, stride=kv_heads), :] = key.astype(jnp.float32)
+        u = base_value_ref[:, g * head : (g + 1) * head].astype(jnp.float32)
+        u += jnp.where(lane < half, pltpu.roll(low, half, 1), high)
+        value = u.astype(jnp.bfloat16)
+        fresh_value_ref[:, g * head : (g + 1) * head] = value
+        value_ref[pl.ds(g, requests, stride=kv_heads), :] = value.astype(jnp.float32)
+
+    inv_sqrt = 1.0 / math.sqrt(head)
+    for r in range(requests):
+        query = query_ref[r * heads : (r + 1) * heads, :].astype(jnp.bfloat16)
+        scores = lax.dot_general(
+            query,
+            keys_ref[r].reshape(kv_heads * slots, head),
+            (((1,), (1,)), ((), ())),
+            preferred_element_type=jnp.float32,
+        )
+        for g in range(kv_heads):
+            score_ref[r * heads + g * group : r * heads + (g + 1) * group, :] = scores[
+                g * group : (g + 1) * group, g * slots : (g + 1) * slots
+            ]
+    slot = lax.broadcasted_iota(jnp.int32, (heads, slots), 1)
+    for r in range(requests):
+        rows = slice(r * heads, (r + 1) * heads)
+        query = query_ref[rows, :]
+        new_key = jnp.concatenate(
+            [
+                jnp.broadcast_to(key_ref[r * kv_heads + g : r * kv_heads + g + 1, :], (group, head))
+                for g in range(kv_heads)
+            ],
+            axis=0,
+        )
+        new_score = jnp.sum(query * new_key, axis=1, keepdims=True) * inv_sqrt
+        scores = jnp.where(slot < lengths_ref[r], score_ref[rows, :] * inv_sqrt, -jnp.inf)
+        row_max = jnp.maximum(jnp.max(scores, axis=1, keepdims=True), new_score)
+        weights = jnp.exp(scores - row_max)
+        new_weight = jnp.exp(new_score - row_max)
+        total = jnp.sum(weights, axis=1, keepdims=True) + new_weight
+        weight_ref[rows, :] = weights / total
+        new_weight_ref[rows, :] = jnp.broadcast_to(new_weight / total, (heads, head))
+    for r in range(requests):
+        rows = slice(r * heads, (r + 1) * heads)
+        weights = weight_ref[rows, :].astype(jnp.bfloat16)
+        zero = jnp.zeros((group, slots), jnp.float32)
+        wide = jnp.concatenate(
+            [
+                jnp.concatenate(
+                    [
+                        weight_ref[r * heads + g * group : r * heads + (g + 1) * group, :]
+                        if o == g
+                        else zero
+                        for o in range(kv_heads)
+                    ],
+                    axis=1,
+                )
+                for g in range(kv_heads)
+            ],
+            axis=0,
+        ).astype(jnp.bfloat16)
+        mixed = jnp.dot(
+            wide,
+            values_ref[r].reshape(kv_heads * slots, head),
+            preferred_element_type=jnp.float32,
+        )
+        new_value = jnp.concatenate(
+            [
+                jnp.broadcast_to(
+                    value_ref[r * kv_heads + g : r * kv_heads + g + 1, :], (group, head)
+                )
+                for g in range(kv_heads)
+            ],
+            axis=0,
+        )
+        new_weight = new_weight_ref[rows, :].astype(jnp.bfloat16).astype(jnp.float32)
+        score_ref[rows, :] = mixed + new_weight * new_value
+    for h in range(heads):
+        out_ref[:, h * head : (h + 1) * head] = score_ref[
+            pl.ds(h, requests, stride=heads), :
+        ].astype(jnp.bfloat16)
+
+
+def in_smem():
+    return pl.BlockSpec(memory_space=pltpu.SMEM)
+
+
+def in_vmem():
+    return pl.BlockSpec(memory_space=pltpu.VMEM)
+
+
+def call(kernel, name, out_shape, scratch, scalars, arrays):
+    return pl.pallas_call(
+        kernel,
+        out_shape=out_shape,
+        in_specs=[in_smem()] * len(scalars) + [in_vmem()] * len(arrays),
+        out_specs=[in_vmem()] * len(out_shape),
+        scratch_shapes=scratch,
+        compiler_params=pltpu.CompilerParams(vmem_limit_bytes=VMEM_BYTES),
+        name=name,
+    )(*scalars, *arrays)
+
+
+def exchange(value, axis, size):
+    return [value] + [
+        lax.ppermute(value, axis, [(i, i ^ k) for i in range(size)]) for k in range(1, size)
+    ]
+
+
+def few_body(
+    hidden,
+    base_queries,
+    base_keys,
+    base_values,
+    adapter_down_weight,
+    adapter_up_query,
+    adapter_up_key_value,
+    cached_keys,
+    cached_values,
+    request_adapter,
+    lengths,
+):
+    planes, columns = lax.axis_size("adapter"), lax.axis_size("tensor")
+    place = lax.axis_index("adapter")
+    number = place * columns + lax.axis_index("tensor")
+    places = jnp.stack([place, number % planes]).astype(jnp.int32)
+    requests = hidden.shape[0]
+    every = requests * planes
+    rank3 = adapter_down_weight.shape[1]
+    head = cached_keys.shape[3]
+    kv_heads = cached_keys.shape[1]
+    heads = base_queries.shape[1] // head
+
+    everyone = exchange(hidden, "adapter", planes)
+    every_id = jnp.concatenate(exchange(request_adapter, "adapter", planes))[None, :]
+    f32, bf16 = jnp.float32, jnp.bfloat16
+    partial, every_id = call(
+        down_kernel,
+        "down",
+        [jax.ShapeDtypeStruct((rank3, every), f32), jax.ShapeDtypeStruct((1, every), jnp.int32)],
+        [pltpu.VMEM((every, hidden.shape[1]), bf16)],
+        [places],
+        [every_id, *everyone, adapter_down_weight],
+    )
+    summed = functools.reduce(jnp.add, exchange(partial, "tensor", columns)).astype(bf16)
+    shrink = exchange(summed, "adapter", planes)
+    width = adapter_up_query.shape[2] + 2 * adapter_up_key_value.shape[3]
+    terms = call(
+        up_kernel,
+        "up",
+        [jax.ShapeDtypeStruct((requests, width), f32)] * planes,
+        [pltpu.VMEM((every, width), f32)],
+        [places],
+        [every_id, *shrink, adapter_up_query, adapter_up_key_value],
+    )
+    arrived = [
+        lax.ppermute(
+            term,
+            ("adapter", "tensor"),
+            [(n, ((n % planes) ^ k) * columns + n // planes) for n in range(planes * columns)],
+        )
+        for k, term in enumerate(terms)
+    ]
+    cosine, sine = rotation_factors(lengths, head)
+    return tuple(
+        call(
+            attend_kernel,
+            "attend",
+            [
+                jax.ShapeDtypeStruct(base_queries.shape, bf16),
+                jax.ShapeDtypeStruct(base_keys.shape, bf16),
+                jax.ShapeDtypeStruct(base_values.shape, bf16),
+            ],
+            [
+                pltpu.VMEM((planes, requests, width), f32),
+                pltpu.VMEM((requests * heads, head), f32),
+                pltpu.VMEM((requests * kv_heads, head), f32),
+                pltpu.VMEM((requests * kv_heads, head), f32),
+                pltpu.VMEM((requests * heads, head), f32),
+                pltpu.VMEM((requests * heads, head), f32),
+                pltpu.VMEM((requests * heads, head), f32),
+            ],
+            [places, lengths],
+            [*arrived, base_queries, base_keys, base_values, cosine, sine, cached_keys, cached_values],
+        )
+    )
 
 
 def rotate_pairs(vectors, positions):
@@ -55,7 +395,7 @@
     return mixed.reshape(local_requests, query_heads * head_dim).astype(jnp.bfloat16)
 
 
-def body(
+def many_body(
     hidden,
     base_queries,
     base_keys,
@@ -165,8 +505,9 @@
 
 
 def solution(mesh):
+    few = mesh.shape["adapter"] == 4 and mesh.shape["tensor"] == 4
     return jax.shard_map(
-        body,
+        few_body if few else many_body,
         mesh=mesh,
         in_specs=(
             P(("groups", "adapter"), "tensor"),

time: 162 us -> 57.5 us (0.35)
  the two profiles are of different devices: /device:TPU:0 before, /device:TPU:17 now
where the time goes in v1:
time: 57.5 us; the launch traced here: 57.1 us
  waiting for transfers between devices  22.1 us (38%)
  starting transfers between devices  20.6 us (36%)
  local copies, waits for them, and re-layouts  7.41 us (13%)
  Pallas kernels  5.24 us (9%)
  other arithmetic  0.98 us (2%)
  between operations  0.72 us (1%)
    ppermute x12, waiting for transfers between devices, exchange(): lax.ppermute(value, axis, [(i, i ^ k) for i in range(size)])  14.5 us
    ppermute x12, starting transfers between devices, exchange(): lax.ppermute(value, axis, [(i, i ^ k) for i in range(size)])  11.9 us
    ppermute x4, starting transfers between devices, few_body(): lax.ppermute(term, ('adapter', 'tensor'), [(n, (n % planes ^ k) * columns...  8.78 us
    ppermute x4, waiting for transfers between devices, few_body(): lax.ppermute(term, ('adapter', 'tensor'), [(n, (n % planes ^ k) * columns...  7.68 us
    unnamed x20, local copies, waits for them, and re-layouts  7.41 us
    pallas_call x3, Pallas kernels, call(): pl.pallas_call(kernel, out_shape=out_shape, in_specs=[in_smem()] * len(sc...  5.24 us
  transfers between devices with their start and end apart: 16, of which 11 were waited for; matrix products, arithmetic and copies ran while one was open for 2% of the time, Pallas kernels for 0%

profile of v1, /device:TPU:17, one launch (start us, length us, event | category | flops | bytes accessed | tf_op | source)
XLA Modules:
  0.0 57.1 jit_solution(11812450739896731699)
XLA Ops:
  0.7 1.4 %collective-permute-start = (s32[32]{0:T(128)}, s32[32]{0:T(128)S(1)}, u32[]{:S(2)}, u32[]{:S(2)}) collective-permute-start(s32[32]{0:T(128)} %param.20), channel_id=1, source_target_pairs={{0,4},{4,0},{8,12},{12,8},{1,5},{5,1},{9,13},{13,9},{2,6},{6,2},{1... | collective-permute-start | bytes 392 | tf_op jit(solution)/shard_map/ppermute | solution.py:269
  2.1 1.3 %collective-permute-start.2 = (s32[32]{0:T(128)}, s32[32]{0:T(128)S(1)}, u32[]{:S(2)}, u32[]{:S(2)}) collective-permute-start(s32[32]{0:T(128)} %param.20), channel_id=1, source_target_pairs={{0,12},{4,8},{8,4},{12,0},{1,13},{5,9},{9,5},{13,1},{2,14},{6,10},... | collective-permute-start | bytes 392 | tf_op jit(solution)/shard_map/ppermute | solution.py:269
  3.4 1.0 %collective-permute-start.4 = (bf16[32,2048]{1,0:T(8,128)(2,1)}, bf16[32,2048]{1,0:T(8,128)(2,1)S(1)}, u32[]{:S(2)}, u32[]{:S(2)}) collective-permute-start(bf16[32,2048]{1,0:T(8,128)(2,1)} %refs_0_.1), channel_id=1, source_target_pairs={{0,8},{4,12},{8,0},{12,4},{1,9},{5,13},{9,1},{13,5},{2,10},{6,14},... | collective-permute-start | bytes 393224 | tf_op jit(solution)/shard_map/ppermute | solution.py:269
  4.4 1.2 %collective-permute-start.3 = (bf16[32,2048]{1,0:T(8,128)(2,1)}, bf16[32,2048]{1,0:T(8,128)(2,1)S(1)}, u32[]{:S(2)}, u32[]{:S(2)}) collective-permute-start(bf16[32,2048]{1,0:T(8,128)(2,1)} %refs_0_.1), channel_id=1, source_target_pairs={{0,4},{4,0},{8,12},{12,8},{1,5},{5,1},{9,13},{13,9},{2,6},{6,2},{1... | collective-permute-start | bytes 393224 | tf_op jit(solution)/shard_map/ppermute | solution.py:269
  5.6 1.2 %collective-permute-start.5 = (bf16[32,2048]{1,0:T(8,128)(2,1)}, bf16[32,2048]{1,0:T(8,128)(2,1)S(1)}, u32[]{:S(2)}, u32[]{:S(2)}) collective-permute-start(bf16[32,2048]{1,0:T(8,128)(2,1)} %refs_0_.1), channel_id=1, source_target_pairs={{0,12},{4,8},{8,4},{12,0},{1,13},{5,9},{9,5},{13,1},{2,14},{6,10},... | collective-permute-start | bytes 393224 | tf_op jit(solution)/shard_map/ppermute | solution.py:269
  8.4 2.6 %collective-permute-done.3.refs_1_ = bf16[32,2048]{1,0:T(8,128)(2,1)S(1)} collective-permute-done((bf16[32,2048]{1,0:T(8,128)(2,1)}, bf16[32,2048]{1,0:T(8,128)(2,1)S(1)}, u32[]{:S(2)}, u32[]{:S(2)}) %collective-permute-start.3) | collective-permute-done | bytes 131104 | tf_op jit(solution)/shard_map/ppermute | solution.py:269
  11.0 6.4 %collective-permute-done.5.refs_3_ = bf16[32,2048]{1,0:T(8,128)(2,1)S(1)} collective-permute-done((bf16[32,2048]{1,0:T(8,128)(2,1)}, bf16[32,2048]{1,0:T(8,128)(2,1)S(1)}, u32[]{:S(2)}, u32[]{:S(2)}) %collective-permute-start.5) | collective-permute-done | bytes 131104 | tf_op jit(solution)/shard_map/ppermute | solution.py:269
  17.4 1.9 %copy-done = bf16[8,96,2048]{2,1,0:T(8,128)(2,1)S(1)} copy-done((bf16[8,96,2048]{2,1,0:T(8,128)(2,1)S(1)}, bf16[8,96,2048]{2,1,0:T(8,128)(2,1)}, u32[]{:S(2)}) %copy-start) | copy-done | bytes 3145752
  20.2 1.6 %down.1 = (f32[96,128]{1,0:T(8,128)S(1)}, s32[1,128]{1,0:T(1,128)S(1)}) custom-call(s32[2]{0:T(128)S(1)} %pad_add_fusion.place_ref, s32[1,128]{1,0:T(1,128)S(1)} %add_bitcast_fusion.ids_ref, bf16[32,2048]{1,0:T(8,128)(2,1)S(1)} %copy-done.5, bf16[32,2048]{1,0:T(8,128)(2,1)S(1)} %collective-permute-done.3.refs_1_, ...), custom_call_target="tpu_custom_call" | custom-call | tf_op jit(solution)/shard_map/down/pallas_call | solution.py:256
  21.7 2.6 %collective-permute-start.8 = (f32[96,128]{1,0:T(8,128)S(1)}, f32[96,128]{1,0:T(8,128)S(1)}, u32[]{:S(2)}, u32[]{:S(2)}) collective-permute-start(f32[96,128]{1,0:T(8,128)S(1)} %get-tuple-element.10), channel_id=1, source_target_pairs={{0,3},{1,2},{2,1},{3,0},{4,7},{5,6},{6,5},{7,4},{8,11},{9,10},{10,... | collective-permute-start | bytes 147464 | tf_op jit(solution)/shard_map/ppermute | solution.py:269
  24.8 2.0 %collective-permute-done.8 = f32[96,128]{1,0:T(8,128)S(1)} collective-permute-done((f32[96,128]{1,0:T(8,128)S(1)}, f32[96,128]{1,0:T(8,128)S(1)}, u32[]{:S(2)}, u32[]{:S(2)}) %collective-permute-start.8) | collective-permute-done | bytes 49184 | tf_op jit(solution)/shard_map/ppermute | solution.py:269
  28.0 1.4 %collective-permute-start.10 = (bf16[96,128]{1,0:T(8,128)(2,1)S(1)}, bf16[96,128]{1,0:T(8,128)(2,1)S(1)}, u32[]{:S(2)}, u32[]{:S(2)}) collective-permute-start(bf16[96,128]{1,0:T(8,128)(2,1)S(1)} %add_convert_fusion.refs_0_), channel_id=1, source_target_pairs={{0,8},{4,12},{8,0},{12,4},{1,9},{5,13},{9,1},{13,5},{2,10},{6,14},... | collective-permute-start | bytes 73736 | tf_op jit(solution)/shard_map/ppermute | solution.py:269
  29.3 1.2 %collective-permute-start.9 = (bf16[96,128]{1,0:T(8,128)(2,1)S(1)}, bf16[96,128]{1,0:T(8,128)(2,1)S(1)}, u32[]{:S(2)}, u32[]{:S(2)}) collective-permute-start(bf16[96,128]{1,0:T(8,128)(2,1)S(1)} %add_convert_fusion.refs_0_), channel_id=1, source_target_pairs={{0,4},{4,0},{8,12},{12,8},{1,5},{5,1},{9,13},{13,9},{2,6},{6,2},{1... | collective-permute-start | bytes 73736 | tf_op jit(solution)/shard_map/ppermute | solution.py:269
  30.8 1.0 %collective-permute-done.10.refs_2_ = bf16[96,128]{1,0:T(8,128)(2,1)S(1)} collective-permute-done((bf16[96,128]{1,0:T(8,128)(2,1)S(1)}, bf16[96,128]{1,0:T(8,128)(2,1)S(1)}, u32[]{:S(2)}, u32[]{:S(2)}) %collective-permute-start.10) | collective-permute-done | bytes 24608 | tf_op jit(solution)/shard_map/ppermute | solution.py:269
  32.2 1.2 %copy-done.3 = bf16[32,32,512]{2,1,0:T(8,128)(2,1)S(1)} copy-done((bf16[32,32,512]{2,1,0:T(8,128)(2,1)S(1)}, bf16[32,32,512]{2,1,0:T(8,128)(2,1)}, u32[]{:S(2)}) %copy-start.3) | copy-done | bytes 1048600
  33.4 1.0 %copy-done.4 = bf16[32,2,32,64]{3,2,1,0:T(8,128)(2,1)S(1)} copy-done((bf16[32,2,32,64]{3,2,1,0:T(8,128)(2,1)S(1)}, bf16[32,2,32,64]{3,2,1,0:T(8,128)(2,1)}, u32[]{:S(2)}) %copy-start.4) | copy-done | bytes 262168
  34.5 1.4 %up.1 = (f32[32,640]{1,0:T(8,128)S(1)}, f32[32,640]{1,0:T(8,128)S(1)}, f32[32,640]{1,0:T(8,128)S(1)}, f32[32,640]{1,0:T(8,128)S(1)}) custom-call(s32[2]{0:T(128)S(1)} %pad_add_fusion.place_ref, s32[1,128]{1,0:T(1,128)S(1)} %get-tuple-element.9.ids_ref, bf16[96,128]{1,0:T(8,128)(2,1)S(1)} %add_convert_fusion.refs_0_, ...), custom_call_target="tpu_custom_call" | custom-call | tf_op jit(solution)/shard_map/up/pallas_call | solution.py:256
  35.8 4.9 %collective-permute-start.12 = (f32[32,640]{1,0:T(8,128)S(1)}, f32[32,640]{1,0:T(8,128)S(1)}, u32[]{:S(2)}, u32[]{:S(2)}) collective-permute-start(f32[32,640]{1,0:T(8,128)S(1)} %get-tuple-element.11), channel_id=1, source_target_pairs={{0,0},{1,4},{2,8},{3,12},{4,1},{5,5},{6,9},{7,13},{8,2},{9,6},{10,... | collective-permute-start | bytes 245768 | tf_op jit(solution)/shard_map/ppermute | solution.py:320
  40.7 2.4 %collective-permute-start.13 = (f32[32,640]{1,0:T(8,128)S(1)}, f32[32,640]{1,0:T(8,128)S(1)}, u32[]{:S(2)}, u32[]{:S(2)}) collective-permute-start(f32[32,640]{1,0:T(8,128)S(1)} %get-tuple-element.12), channel_id=1, source_target_pairs={{0,4},{1,0},{2,12},{3,8},{4,5},{5,1},{6,13},{7,9},{8,6},{9,2},{10,... | collective-permute-start | bytes 245768 | tf_op jit(solution)/shard_map/ppermute | solution.py:320
  43.2 1.5 %collective-permute-start.15 = (f32[32,640]{1,0:T(8,128)S(1)}, f32[32,640]{1,0:T(8,128)S(1)}, u32[]{:S(2)}, u32[]{:S(2)}) collective-permute-start(f32[32,640]{1,0:T(8,128)S(1)} %get-tuple-element.14), channel_id=1, source_target_pairs={{0,12},{1,8},{2,4},{3,0},{4,13},{5,9},{6,5},{7,1},{8,14},{9,10},{1... | collective-permute-start | bytes 245768 | tf_op jit(solution)/shard_map/ppermute | solution.py:320
  44.8 4.5 %collective-permute-done.13.refs_1_ = f32[32,640]{1,0:T(8,128)S(1)} collective-permute-done((f32[32,640]{1,0:T(8,128)S(1)}, f32[32,640]{1,0:T(8,128)S(1)}, u32[]{:S(2)}, u32[]{:S(2)}) %collective-permute-start.13) | collective-permute-done | bytes 81952 | tf_op jit(solution)/shard_map/ppermute | solution.py:320
  49.3 1.3 %collective-permute-done.14.refs_2_ = f32[32,640]{1,0:T(8,128)S(1)} collective-permute-done((f32[32,640]{1,0:T(8,128)S(1)}, f32[32,640]{1,0:T(8,128)S(1)}, u32[]{:S(2)}, u32[]{:S(2)}) %collective-permute-start.14) | collective-permute-done | bytes 81952 | tf_op jit(solution)/shard_map/ppermute | solution.py:320
  50.6 1.8 %collective-permute-done.15.refs_3_ = f32[32,640]{1,0:T(8,128)S(1)} collective-permute-done((f32[32,640]{1,0:T(8,128)S(1)}, f32[32,640]{1,0:T(8,128)S(1)}, u32[]{:S(2)}, u32[]{:S(2)}) %collective-permute-start.15) | collective-permute-done | bytes 81952 | tf_op jit(solution)/shard_map/ppermute | solution.py:320
  54.8 2.3 %attend.1 = (bf16[32,2048]{1,0:T(8,128)(2,1)}, bf16[32,256]{1,0:T(8,128)(2,1)}, bf16[32,256]{1,0:T(8,128)(2,1)}) custom-call(s32[2]{0:T(128)S(1)} %pad_add_fusion.place_ref, s32[32]{0:T(128)S(1)} %copy-done.9, f32[32,640]{1,0:T(8,128)S(1)} %collective-permute-done.12.refs_0_, f32[32,640]{1,0:T(8,128)S(1)} %collective-permute-done.13.refs_1_, ...), custom_call_target="tpu_custom_call" | custom-call | tf_op jit(solution)/shard_map/attend/pallas_call | solution.py:256
  (37 shorter events, 7.4 us)
Async XLA Ops:
  0.6 29.9 %copy-start.9 = (s32[32]{0:T(128)S(1)}, s32[32]{0:T(128)}, u32[]{:S(2)}) copy-start(s32[32]{0:T(128)} %lengths_ref.1) | copy-start | bytes 388
  0.6 4.9 %collective-permute-start.1 = (s32[32]{0:T(128)}, s32[32]{0:T(128)S(1)}, u32[]{:S(2)}, u32[]{:S(2)}) collective-permute-start(s32[32]{0:T(128)} %param.20), channel_id=1, source_target_pairs={{0,8},{4,12},{8,0},{12,4},{1,9},{5,13},{9,1},{13,5},{2,10},{6,14},... | collective-permute-start | bytes 392 | tf_op jit(solution)/shard_map/ppermute | solution.py:269
  0.7 6.1 %collective-permute-start = (s32[32]{0:T(128)}, s32[32]{0:T(128)S(1)}, u32[]{:S(2)}, u32[]{:S(2)}) collective-permute-start(s32[32]{0:T(128)} %param.20), channel_id=1, source_target_pairs={{0,4},{4,0},{8,12},{12,8},{1,5},{5,1},{9,13},{13,9},{2,6},{6,2},{1... | collective-permute-start | bytes 392 | tf_op jit(solution)/shard_map/ppermute | solution.py:269
  2.1 4.7 %collective-permute-start.2 = (s32[32]{0:T(128)}, s32[32]{0:T(128)S(1)}, u32[]{:S(2)}, u32[]{:S(2)}) collective-permute-start(s32[32]{0:T(128)} %param.20), channel_id=1, source_target_pairs={{0,12},{4,8},{8,4},{12,0},{1,13},{5,9},{9,5},{13,1},{2,14},{6,10},... | collective-permute-start | bytes 392 | tf_op jit(solution)/shard_map/ppermute | solution.py:269
  3.4 5.0 %collective-permute-start.4 = (bf16[32,2048]{1,0:T(8,128)(2,1)}, bf16[32,2048]{1,0:T(8,128)(2,1)S(1)}, u32[]{:S(2)}, u32[]{:S(2)}) collective-permute-start(bf16[32,2048]{1,0:T(8,128)(2,1)} %refs_0_.1), channel_id=1, source_target_pairs={{0,8},{4,12},{8,0},{12,4},{1,9},{5,13},{9,1},{13,5},{2,10},{6,14},... | collective-permute-start | bytes 393224 | tf_op jit(solution)/shard_map/ppermute | solution.py:269
  4.4 6.6 %collective-permute-start.3 = (bf16[32,2048]{1,0:T(8,128)(2,1)}, bf16[32,2048]{1,0:T(8,128)(2,1)S(1)}, u32[]{:S(2)}, u32[]{:S(2)}) collective-permute-start(bf16[32,2048]{1,0:T(8,128)(2,1)} %refs_0_.1), channel_id=1, source_target_pairs={{0,4},{4,0},{8,12},{12,8},{1,5},{5,1},{9,13},{13,9},{2,6},{6,2},{1... | collective-permute-start | bytes 393224 | tf_op jit(solution)/shard_map/ppermute | solution.py:269
  5.6 11.8 %collective-permute-start.5 = (bf16[32,2048]{1,0:T(8,128)(2,1)}, bf16[32,2048]{1,0:T(8,128)(2,1)S(1)}, u32[]{:S(2)}, u32[]{:S(2)}) collective-permute-start(bf16[32,2048]{1,0:T(8,128)(2,1)} %refs_0_.1), channel_id=1, source_target_pairs={{0,12},{4,8},{8,4},{12,0},{1,13},{5,9},{9,5},{13,1},{2,14},{6,10},... | collective-permute-start | bytes 393224 | tf_op jit(solution)/shard_map/ppermute | solution.py:269
  17.4 1.9 %copy-start = (bf16[8,96,2048]{2,1,0:T(8,128)(2,1)S(1)}, bf16[8,96,2048]{2,1,0:T(8,128)(2,1)}, u32[]{:S(2)}) copy-start(bf16[8,96,2048]{2,1,0:T(8,128)(2,1)} %refs_4_.3) | copy-start | bytes 9437188
  19.3 0.9 %copy-start.5 = (bf16[32,2048]{1,0:T(8,128)(2,1)S(1)}, bf16[32,2048]{1,0:T(8,128)(2,1)}, u32[]{:S(2)}) copy-start(bf16[32,2048]{1,0:T(8,128)(2,1)} %refs_0_.1) | copy-start | bytes 393220
  20.2 32.3 %copy-start.1 = (bf16[32,2,128,128]{3,2,1,0:T(8,128)(2,1)S(1)}, bf16[32,2,128,128]{3,2,1,0:T(8,128)(2,1)}, u32[]{:S(2)}) copy-start(bf16[32,2,128,128]{3,2,1,0:T(8,128)(2,1)} %refs_9_.1) | copy-start | bytes 6291460
  20.2 32.3 %copy-start.2 = (bf16[32,2,128,128]{3,2,1,0:T(8,128)(2,1)S(1)}, bf16[32,2,128,128]{3,2,1,0:T(8,128)(2,1)}, u32[]{:S(2)}) copy-start(bf16[32,2,128,128]{3,2,1,0:T(8,128)(2,1)} %refs_10_.1) | copy-start | bytes 6291460
  21.7 5.1 %collective-permute-start.8 = (f32[96,128]{1,0:T(8,128)S(1)}, f32[96,128]{1,0:T(8,128)S(1)}, u32[]{:S(2)}, u32[]{:S(2)}) collective-permute-start(f32[96,128]{1,0:T(8,128)S(1)} %get-tuple-element.10), channel_id=1, source_target_pairs={{0,3},{1,2},{2,1},{3,0},{4,7},{5,6},{6,5},{7,4},{8,11},{9,10},{10,... | collective-permute-start | bytes 147464 | tf_op jit(solution)/shard_map/ppermute | solution.py:269
  24.3 3.4 %collective-permute-start.7 = (f32[96,128]{1,0:T(8,128)S(1)}, f32[96,128]{1,0:T(8,128)S(1)}, u32[]{:S(2)}, u32[]{:S(2)}) collective-permute-start(f32[96,128]{1,0:T(8,128)S(1)} %get-tuple-element.10), channel_id=1, source_target_pairs={{0,2},{1,3},{2,0},{3,1},{4,6},{5,7},{6,4},{7,5},{8,10},{9,11},{10,... | collective-permute-start | bytes 147464 | tf_op jit(solution)/shard_map/ppermute | solution.py:269
  24.6 3.2 %collective-permute-start.6 = (f32[96,128]{1,0:T(8,128)S(1)}, f32[96,128]{1,0:T(8,128)S(1)}, u32[]{:S(2)}, u32[]{:S(2)}) collective-permute-start(f32[96,128]{1,0:T(8,128)S(1)} %get-tuple-element.10), channel_id=1, source_target_pairs={{0,1},{1,0},{2,3},{3,2},{4,5},{5,4},{6,7},{7,6},{8,9},{9,8},{10,11... | collective-permute-start | bytes 147464 | tf_op jit(solution)/shard_map/ppermute | solution.py:269
  27.8 3.0 %collective-permute-start.11 = (bf16[96,128]{1,0:T(8,128)(2,1)S(1)}, bf16[96,128]{1,0:T(8,128)(2,1)S(1)}, u32[]{:S(2)}, u32[]{:S(2)}) collective-permute-start(bf16[96,128]{1,0:T(8,128)(2,1)S(1)} %add_convert_fusion.refs_0_), channel_id=1, source_target_pairs={{0,12},{4,8},{8,4},{12,0},{1,13},{5,9},{9,5},{13,1},{2,14},{6,10},... | collective-permute-start | bytes 73736 | tf_op jit(solution)/shard_map/ppermute | solution.py:269
  28.0 3.8 %collective-permute-start.10 = (bf16[96,128]{1,0:T(8,128)(2,1)S(1)}, bf16[96,128]{1,0:T(8,128)(2,1)S(1)}, u32[]{:S(2)}, u32[]{:S(2)}) collective-permute-start(bf16[96,128]{1,0:T(8,128)(2,1)S(1)} %add_convert_fusion.refs_0_), channel_id=1, source_target_pairs={{0,8},{4,12},{8,0},{12,4},{1,9},{5,13},{9,1},{13,5},{2,10},{6,14},... | collective-permute-start | bytes 73736 | tf_op jit(solution)/shard_map/ppermute | solution.py:269
  29.3 2.9 %collective-permute-start.9 = (bf16[96,128]{1,0:T(8,128)(2,1)S(1)}, bf16[96,128]{1,0:T(8,128)(2,1)S(1)}, u32[]{:S(2)}, u32[]{:S(2)}) collective-permute-start(bf16[96,128]{1,0:T(8,128)(2,1)S(1)} %add_convert_fusion.refs_0_), channel_id=1, source_target_pairs={{0,4},{4,0},{8,12},{12,8},{1,5},{5,1},{9,13},{13,9},{2,6},{6,2},{1... | collective-permute-start | bytes 73736 | tf_op jit(solution)/shard_map/ppermute | solution.py:269
  32.2 1.2 %copy-start.3 = (bf16[32,32,512]{2,1,0:T(8,128)(2,1)S(1)}, bf16[32,32,512]{2,1,0:T(8,128)(2,1)}, u32[]{:S(2)}) copy-start(bf16[32,32,512]{2,1,0:T(8,128)(2,1)} %refs_4_.4) | copy-start | bytes 3145732
  33.4 1.0 %copy-start.4 = (bf16[32,2,32,64]{3,2,1,0:T(8,128)(2,1)S(1)}, bf16[32,2,32,64]{3,2,1,0:T(8,128)(2,1)}, u32[]{:S(2)}) copy-start(bf16[32,2,32,64]{3,2,1,0:T(8,128)(2,1)} %refs_5_.2) | copy-start | bytes 786436
  35.8 8.9 %collective-permute-start.12 = (f32[32,640]{1,0:T(8,128)S(1)}, f32[32,640]{1,0:T(8,128)S(1)}, u32[]{:S(2)}, u32[]{:S(2)}) collective-permute-start(f32[32,640]{1,0:T(8,128)S(1)} %get-tuple-element.11), channel_id=1, source_target_pairs={{0,0},{1,4},{2,8},{3,12},{4,1},{5,5},{6,9},{7,13},{8,2},{9,6},{10,... | collective-permute-start | bytes 245768 | tf_op jit(solution)/shard_map/ppermute | solution.py:320
  40.7 8.5 %collective-permute-start.13 = (f32[32,640]{1,0:T(8,128)S(1)}, f32[32,640]{1,0:T(8,128)S(1)}, u32[]{:S(2)}, u32[]{:S(2)}) collective-permute-start(f32[32,640]{1,0:T(8,128)S(1)} %get-tuple-element.12), channel_id=1, source_target_pairs={{0,4},{1,0},{2,12},{3,8},{4,5},{5,1},{6,13},{7,9},{8,6},{9,2},{10,... | collective-permute-start | bytes 245768 | tf_op jit(solution)/shard_map/ppermute | solution.py:320
  43.2 7.4 %collective-permute-start.14 = (f32[32,640]{1,0:T(8,128)S(1)}, f32[32,640]{1,0:T(8,128)S(1)}, u32[]{:S(2)}, u32[]{:S(2)}) collective-permute-start(f32[32,640]{1,0:T(8,128)S(1)} %get-tuple-element.13), channel_id=1, source_target_pairs={{0,8},{1,12},{2,0},{3,4},{4,9},{5,13},{6,1},{7,5},{8,10},{9,14},{1... | collective-permute-start | bytes 245768 | tf_op jit(solution)/shard_map/ppermute | solution.py:320
  43.2 9.3 %collective-permute-start.15 = (f32[32,640]{1,0:T(8,128)S(1)}, f32[32,640]{1,0:T(8,128)S(1)}, u32[]{:S(2)}, u32[]{:S(2)}) collective-permute-start(f32[32,640]{1,0:T(8,128)S(1)} %get-tuple-element.14), channel_id=1, source_target_pairs={{0,12},{1,8},{2,4},{3,0},{4,13},{5,9},{6,5},{7,1},{8,14},{9,10},{1... | collective-permute-start | bytes 245768 | tf_op jit(solution)/shard_map/ppermute | solution.py:320
  52.5 0.9 %copy-start.6 = (bf16[32,2048]{1,0:T(8,128)(2,1)S(1)}, bf16[32,2048]{1,0:T(8,128)(2,1)}, u32[]{:S(2)}) copy-start(bf16[32,2048]{1,0:T(8,128)(2,1)} %refs_4_.5) | copy-start | bytes 393220
  (2 other events, 1.4 us)

commit v2 on v1

--- a/solution.py
+++ b/solution.py
@@ -12,6 +12,8 @@
 ROPE_BASE = 500000.0
 LANES = 128
 VMEM_BYTES = 16 * 1024 * 1024
+LOAD_BYTES = 52 * 1024 * 1024
+PACK_BYTES = 60 * 1024 * 1024
 
 
 def rotation_factors(positions, head_dim):
@@ -23,33 +25,54 @@
     return jnp.cos(angles), jnp.sin(angles)
 
 
-def swap_blocks(row, place, block):
-    lane = lax.broadcasted_iota(jnp.int32, row.shape, 1)
-    far = pltpu.roll(row, 2 * block, 1)
-    row = jnp.where((place & 2) != 0, far, row)
-    up, down = pltpu.roll(row, block, 1), pltpu.roll(row, LANES - block, 1)
-    near = jnp.where((lane // block) % 2 == 0, down, up)
-    return jnp.where((place & 1) != 0, near, row)
-
-
-def down_kernel(place_ref, ids_ref, *refs):
-    *hidden_refs, down_ref, out_ref, ids_out_ref, rows_ref = refs
+def pack_kernel(ids_in, hidden_in, out_ref, ids_ref, sems):
+    requests, width = hidden_in.shape
+    ids_copy = pltpu.make_async_copy(ids_in, ids_ref, sems.at[0])
+    hidden_copy = pltpu.make_async_copy(hidden_in, out_ref.at[:, pl.ds(0, width)], sems.at[1])
+    hidden_copy.start()
+    ids_copy.start()
+    ids_copy.wait()
+    row = lax.broadcasted_iota(jnp.int32, (requests, LANES), 0)
+    ids = jnp.zeros((requests, LANES), jnp.int32)
+    for r in range(requests):
+        ids = jnp.where(row == r, ids_ref[r], ids)
+    out_ref[:, width:] = ids.astype(jnp.float32).astype(jnp.bfloat16)
+    hidden_copy.wait()
+
+
+def pack(request_adapter, hidden):
+    requests, width = hidden.shape
+    return pl.pallas_call(
+        pack_kernel,
+        out_shape=pltpu.VMEM((requests, width + LANES), jnp.bfloat16),
+        in_specs=[pl.BlockSpec(memory_space=pltpu.HBM)] * 2,
+        out_specs=in_vmem(),
+        scratch_shapes=[
+            pltpu.SMEM(request_adapter.shape, jnp.int32),
+            pltpu.SemaphoreType.DMA((2,)),
+        ],
+        compiler_params=pltpu.CompilerParams(vmem_limit_bytes=PACK_BYTES),
+        name="pack",
+    )(request_adapter, hidden)
+
+
+def down_kernel(place_ref, *refs):
+    *message_refs, down_ref, out_ref, ids_ref, rows_ref = refs
     place = place_ref[0]
-    block = hidden_refs[0].shape[0]
-    for k, hidden_ref in enumerate(hidden_refs):
+    held, rank, width = down_ref.shape
+    block = message_refs[0].shape[0]
+    for k, message_ref in zip((0, 3, 2, 1), message_refs):
         start = pl.multiple_of((place ^ k) * block, block)
-        rows_ref[pl.ds(start, block), :] = hidden_ref[...]
-    held = down_ref.shape[0]
-    ids = swap_blocks(jnp.broadcast_to(ids_ref[...], (8, LANES)), place, block)[0:1]
-    ids_out_ref[...] = ids
+        rows_ref[pl.ds(start, block), :] = message_ref[...]
+    ids = rows_ref[:, width:].astype(jnp.float32)
+    ids_ref[...] = ids
+    slot = jnp.transpose(ids)[0:1] - (place * held).astype(jnp.float32)
     product = lax.dot_general(
-        down_ref[...].reshape(held * down_ref.shape[1], down_ref.shape[2]),
-        rows_ref[...],
+        down_ref[...].reshape(held * rank, width),
+        rows_ref[:, :width],
         (((1,), (1,)), ((), ())),
         preferred_element_type=jnp.float32,
     )
-    slot = ids - place * held
-    rank = down_ref.shape[1]
     total = jnp.zeros(out_ref.shape, jnp.float32)
     for s in range(held):
         total += jnp.where(slot == s, product[s * rank : (s + 1) * rank], 0.0)
@@ -66,7 +89,7 @@
     rows = shrink.shape[1]
     shrink = jnp.concatenate([shrink, jnp.zeros((LANES - 3 * rank, rows), jnp.float32)], axis=0)
     shrink = jnp.transpose(shrink)
-    ids = jnp.transpose(jnp.broadcast_to(ids_ref[...].astype(jnp.float32), (LANES, rows)))
+    ids = ids_ref[...]
     lane = lax.broadcasted_iota(jnp.int32, (rows, LANES), 1)
     count = up_query_ref.shape[0]
     query = jnp.concatenate([shrink[:, :rank]] * (LANES // rank), axis=1)
@@ -244,6 +267,33 @@
         ].astype(jnp.bfloat16)
 
 
+def load_kernel(*refs):
+    count = (len(refs) - 1) // 2
+    sems = refs[-1]
+    copies = [
+        pltpu.make_async_copy(refs[i], refs[count + i], sems.at[i]) for i in range(count)
+    ]
+    for copy in copies:
+        copy.start()
+    for copy in copies:
+        copy.wait()
+
+
+def load(arrays):
+    return pl.pallas_call(
+        load_kernel,
+        out_shape=[pltpu.VMEM(a.shape, a.dtype) for a in arrays],
+        in_specs=[pl.BlockSpec(memory_space=pltpu.HBM)] * len(arrays),
+        out_specs=[in_vmem()] * len(arrays),
+        scratch_shapes=[pltpu.SemaphoreType.DMA((len(arrays),))],
+        compiler_params=pltpu.CompilerParams(vmem_limit_bytes=LOAD_BYTES),
+        cost_estimate=pl.CostEstimate(
+            flops=0, bytes_accessed=sum(a.size for a in arrays) * 4, transcendentals=0
+        ),
+        name="load",
+    )(*arrays)
+
+
 def in_smem():
     return pl.BlockSpec(memory_space=pltpu.SMEM)
 
@@ -264,10 +314,12 @@
     )(*scalars, *arrays)
 
 
+def step(value, axis, size, k):
+    return lax.ppermute(value, axis, [(i, i ^ k) for i in range(size)])
+
+
 def exchange(value, axis, size):
-    return [value] + [
-        lax.ppermute(value, axis, [(i, i ^ k) for i in range(size)]) for k in range(1, size)
-    ]
+    return [value] + [step(value, axis, size, k) for k in range(size - 1, 0, -1)]
 
 
 def few_body(
@@ -294,16 +346,39 @@
     kv_heads = cached_keys.shape[1]
     heads = base_queries.shape[1] // head
 
-    everyone = exchange(hidden, "adapter", planes)
-    every_id = jnp.concatenate(exchange(request_adapter, "adapter", planes))[None, :]
     f32, bf16 = jnp.float32, jnp.bfloat16
+    message = pack(request_adapter, hidden)
+    mirror = step(message, "adapter", planes, planes - 1)
+    near = step(message, "adapter", planes, 1)
+    everyone = [message, mirror, step(mirror, "adapter", planes, 1), near]
+    (
+        adapter_down_weight,
+        adapter_up_query,
+        adapter_up_key_value,
+        base_queries,
+        base_keys,
+        base_values,
+        cached_keys,
+        cached_values,
+    ) = load(
+        [
+            adapter_down_weight,
+            adapter_up_query,
+            adapter_up_key_value,
+            base_queries,
+            base_keys,
+            base_values,
+            cached_keys,
+            cached_values,
+        ]
+    )
     partial, every_id = call(
         down_kernel,
         "down",
-        [jax.ShapeDtypeStruct((rank3, every), f32), jax.ShapeDtypeStruct((1, every), jnp.int32)],
-        [pltpu.VMEM((every, hidden.shape[1]), bf16)],
+        [jax.ShapeDtypeStruct((rank3, every), f32), jax.ShapeDtypeStruct((every, LANES), f32)],
+        [pltpu.VMEM((every, hidden.shape[1] + LANES), bf16)],
         [places],
-        [every_id, *everyone, adapter_down_weight],
+        [*everyone, adapter_down_weight],
     )
     summed = functools.reduce(jnp.add, exchange(partial, "tensor", columns)).astype(bf16)
     shrink = exchange(summed, "adapter", planes)

time: 57.5 us -> 46.5 us (0.81)
  the two profiles are of different devices: /device:TPU:17 before, /device:TPU:20 now
where the time goes in v2:
time: 46.5 us; the launch traced here: 46.3 us
  waiting for transfers between devices  18.8 us (40%)
  starting transfers between devices  16.6 us (36%)
  Pallas kernels  9.9 us (21%)
  between operations  0.74 us (2%)
    ppermute x9, waiting for transfers between devices, step(): return lax.ppermute(value, axis, [(i, i ^ k) for i in range(size)])  13.4 us
    ppermute x9, starting transfers between devices, step(): return lax.ppermute(value, axis, [(i, i ^ k) for i in range(size)])  9.02 us
    ppermute x4, starting transfers between devices, few_body(): lax.ppermute(term, ('adapter', 'tensor'), [(n, (n % planes ^ k) * columns...  7.55 us
    ppermute x4, waiting for transfers between devices, few_body(): lax.ppermute(term, ('adapter', 'tensor'), [(n, (n % planes ^ k) * columns...  5.47 us
    pallas_call x3, Pallas kernels, call(): pl.pallas_call(kernel, out_shape=out_shape, in_specs=[in_smem()] * len(sc...  5.22 us
    pallas_call x1, Pallas kernels, load(): pl.pallas_call(load_kernel, out_shape=[pltpu.VMEM(a.shape, a.dtype) for a...  3.76 us
  transfers between devices with their start and end apart: 13, of which 7 were waited for; matrix products, arithmetic and copies ran while one was open for 0% of the time, Pallas kernels for 8%

profile of v2, /device:TPU:20, one launch (start us, length us, event | category | flops | bytes accessed | tf_op | source)
XLA Modules:
  0.0 46.3 jit_solution(18029060388399516658)
XLA Ops:
  0.6 0.9 %pack.1.refs_0_ = bf16[32,2176]{1,0:T(8,128)(2,1)S(1)} custom-call(s32[32]{0:T(128)} %ids_in.1, bf16[32,2048]{1,0:T(8,128)(2,1)} %hidden_in.1), custom_call_target="tpu_custom_call" | custom-call | tf_op jit(solution)/shard_map/pack/pallas_call | solution.py:45
  1.6 0.5 %collective-permute-start = (bf16[32,2176]{1,0:T(8,128)(2,1)S(1)}, bf16[32,2176]{1,0:T(8,128)(2,1)S(1)}, u32[]{:S(2)}, u32[]{:S(2)}) collective-permute-start(bf16[32,2176]{1,0:T(8,128)(2,1)S(1)} %pack.1.refs_0_), channel_id=1, source_target_pairs={{0,12},{4,8},{8,4},{12,0},{1,13},{5,9},{9,5},{13,1},{2,14},{6,10},... | collective-permute-start | bytes 417800 | tf_op jit(solution)/shard_map/ppermute | solution.py:318
  2.1 1.3 %collective-permute-start.2 = (bf16[32,2176]{1,0:T(8,128)(2,1)S(1)}, bf16[32,2176]{1,0:T(8,128)(2,1)S(1)}, u32[]{:S(2)}, u32[]{:S(2)}) collective-permute-start(bf16[32,2176]{1,0:T(8,128)(2,1)S(1)} %pack.1.refs_0_), channel_id=1, source_target_pairs={{0,4},{4,0},{8,12},{12,8},{1,5},{5,1},{9,13},{13,9},{2,6},{6,2},{1... | collective-permute-start | bytes 417800 | tf_op jit(solution)/shard_map/ppermute | solution.py:318
  3.4 6.5 %collective-permute-done.refs_1_ = bf16[32,2176]{1,0:T(8,128)(2,1)S(1)} collective-permute-done((bf16[32,2176]{1,0:T(8,128)(2,1)S(1)}, bf16[32,2176]{1,0:T(8,128)(2,1)S(1)}, u32[]{:S(2)}, u32[]{:S(2)}) %collective-permute-start) | collective-permute-done | bytes 139296 | tf_op jit(solution)/shard_map/ppermute | solution.py:318
  9.9 1.6 %collective-permute-start.1 = (bf16[32,2176]{1,0:T(8,128)(2,1)S(1)}, bf16[32,2176]{1,0:T(8,128)(2,1)S(1)}, u32[]{:S(2)}, u32[]{:S(2)}) collective-permute-start(bf16[32,2176]{1,0:T(8,128)(2,1)S(1)} %collective-permute-done.refs_1_), channel_id=1, source_target_pairs={{0,4},{4,0},{8,12},{12,8},{1,5},{5,1},{9,13},{13,9},{2,6},{6,2},{1... | collective-permute-start | bytes 417800 | tf_op jit(solution)/shard_map/ppermute | solution.py:318
  11.6 3.8 %load.1 = (bf16[8,96,2048]{2,1,0:T(8,128)(2,1)S(1)}, bf16[32,32,512]{2,1,0:T(8,128)(2,1)S(1)}, bf16[32,2,32,64]{3,2,1,0:T(8,128)(2,1)S(1)}, bf16[32,2048]{1,0:T(...) custom-call(bf16[8,96,2048]{2,1,0:T(8,128)(2,1)} %refs_0_.1, ...), custom_call_target="tpu_custom_call" | custom-call | bytes 17629184 | tf_op jit(solution)/shard_map/load/pallas_call | solution.py:283
  15.4 1.6 %down.1 = (f32[96,128]{1,0:T(8,128)S(1)}, f32[128,128]{1,0:T(8,128)S(1)}) custom-call(s32[2]{0:T(128)S(1)} %pad_add_fusion.place_ref, bf16[32,2176]{1,0:T(8,128)(2,1)S(1)} %pack.1.refs_0_, bf16[32,2176]{1,0:T(8,128)(2,1)S(1)} %collective-permute-done.refs_1_, bf16[32,2176]{1,0:T(8,128)(2,1)S(1)} %collective-permute-done.1.refs_2_, ...), custom_call_target="tpu_custom_call" | custom-call | tf_op jit(solution)/shard_map/down/pallas_call | solution.py:306
  17.1 1.6 %collective-permute-start.4 = (f32[96,128]{1,0:T(8,128)S(1)}, f32[96,128]{1,0:T(8,128)S(1)}, u32[]{:S(2)}, u32[]{:S(2)}) collective-permute-start(f32[96,128]{1,0:T(8,128)S(1)} %get-tuple-element.19), channel_id=1, source_target_pairs={{0,2},{1,3},{2,0},{3,1},{4,6},{5,7},{6,4},{7,5},{8,10},{9,11},{10,... | collective-permute-start | bytes 147464 | tf_op jit(solution)/shard_map/ppermute | solution.py:318
  18.6 0.3 collective-permute-start.5
  18.9 2.1 %collective-permute-done.3 = f32[96,128]{1,0:T(8,128)S(1)} collective-permute-done((f32[96,128]{1,0:T(8,128)S(1)}, f32[96,128]{1,0:T(8,128)S(1)}, u32[]{:S(2)}, u32[]{:S(2)}) %collective-permute-start.3) | collective-permute-done | bytes 49184 | tf_op jit(solution)/shard_map/ppermute | solution.py:318
  21.1 0.9 %collective-permute-done.4 = f32[96,128]{1,0:T(8,128)S(1)} collective-permute-done((f32[96,128]{1,0:T(8,128)S(1)}, f32[96,128]{1,0:T(8,128)S(1)}, u32[]{:S(2)}, u32[]{:S(2)}) %collective-permute-start.4) | collective-permute-done | bytes 49184 | tf_op jit(solution)/shard_map/ppermute | solution.py:318
  22.0 0.2 collective-permute-start.6
  22.2 3.4 %collective-permute-start.7 = (bf16[96,128]{1,0:T(8,128)(2,1)S(1)}, bf16[96,128]{1,0:T(8,128)(2,1)S(1)}, u32[]{:S(2)}, u32[]{:S(2)}) collective-permute-start(bf16[96,128]{1,0:T(8,128)(2,1)S(1)} %add_convert_fusion.refs_0_), channel_id=1, source_target_pairs={{0,8},{4,12},{8,0},{12,4},{1,9},{5,13},{9,1},{13,5},{2,10},{6,14},... | collective-permute-start | bytes 73736 | tf_op jit(solution)/shard_map/ppermute | solution.py:318
  25.6 0.4 collective-permute-done.6.refs_1_
  26.0 1.7 %collective-permute-done.7.refs_2_ = bf16[96,128]{1,0:T(8,128)(2,1)S(1)} collective-permute-done((bf16[96,128]{1,0:T(8,128)(2,1)S(1)}, bf16[96,128]{1,0:T(8,128)(2,1)S(1)}, u32[]{:S(2)}, u32[]{:S(2)}) %collective-permute-start.7) | collective-permute-done | bytes 24608 | tf_op jit(solution)/shard_map/ppermute | solution.py:318
  27.7 1.7 %collective-permute-done.8.refs_3_ = bf16[96,128]{1,0:T(8,128)(2,1)S(1)} collective-permute-done((bf16[96,128]{1,0:T(8,128)(2,1)S(1)}, bf16[96,128]{1,0:T(8,128)(2,1)S(1)}, u32[]{:S(2)}, u32[]{:S(2)}) %collective-permute-start.8) | collective-permute-done | bytes 24608 | tf_op jit(solution)/shard_map/ppermute | solution.py:318
  29.4 1.4 %up.1 = (f32[32,640]{1,0:T(8,128)S(1)}, f32[32,640]{1,0:T(8,128)S(1)}, f32[32,640]{1,0:T(8,128)S(1)}, f32[32,640]{1,0:T(8,128)S(1)}) custom-call(s32[2]{0:T(128)S(1)} %pad_add_fusion.place_ref, f32[128,128]{1,0:T(8,128)S(1)} %get-tuple-element.18.ids_ref, bf16[96,128]{1,0:T(8,128)(2,1)S(1)} %add_convert_fusion.refs_0_, ...), custom_call_target="tpu_custom_call" | custom-call | tf_op jit(solution)/shard_map/up/pallas_call | solution.py:306
  30.8 0.4 collective-permute-start.10
  31.2 0.9 %collective-permute-start.11 = (f32[32,640]{1,0:T(8,128)S(1)}, f32[32,640]{1,0:T(8,128)S(1)}, u32[]{:S(2)}, u32[]{:S(2)}) collective-permute-start(f32[32,640]{1,0:T(8,128)S(1)} %get-tuple-element.24), channel_id=1, source_target_pairs={{0,8},{1,12},{2,0},{3,4},{4,9},{5,13},{6,1},{7,5},{8,10},{9,14},{1... | collective-permute-start | bytes 245768 | tf_op jit(solution)/shard_map/ppermute | solution.py:395
  32.1 3.8 %collective-permute-start.12 = (f32[32,640]{1,0:T(8,128)S(1)}, f32[32,640]{1,0:T(8,128)S(1)}, u32[]{:S(2)}, u32[]{:S(2)}) collective-permute-start(f32[32,640]{1,0:T(8,128)S(1)} %get-tuple-element.25), channel_id=1, source_target_pairs={{0,12},{1,8},{2,4},{3,0},{4,13},{5,9},{6,5},{7,1},{8,14},{9,10},{1... | collective-permute-start | bytes 245768 | tf_op jit(solution)/shard_map/ppermute | solution.py:395
  35.9 2.5 %collective-permute-start.9 = (f32[32,640]{1,0:T(8,128)S(1)}, f32[32,640]{1,0:T(8,128)S(1)}, u32[]{:S(2)}, u32[]{:S(2)}) collective-permute-start(f32[32,640]{1,0:T(8,128)S(1)} %get-tuple-element.22), channel_id=1, source_target_pairs={{0,0},{1,4},{2,8},{3,12},{4,1},{5,5},{6,9},{7,13},{8,2},{9,6},{10,... | collective-permute-start | bytes 245768 | tf_op jit(solution)/shard_map/ppermute | solution.py:395
  38.4 0.1 multiply_sine_fusion
  38.6 5.5 %collective-permute-done.9.refs_0_ = f32[32,640]{1,0:T(8,128)S(1)} collective-permute-done((f32[32,640]{1,0:T(8,128)S(1)}, f32[32,640]{1,0:T(8,128)S(1)}, u32[]{:S(2)}, u32[]{:S(2)}) %collective-permute-start.9) | collective-permute-done | bytes 81952 | tf_op jit(solution)/shard_map/ppermute | solution.py:395
  44.0 2.3 %attend.1 = (bf16[32,2048]{1,0:T(8,128)(2,1)}, bf16[32,256]{1,0:T(8,128)(2,1)}, bf16[32,256]{1,0:T(8,128)(2,1)}) custom-call(s32[2]{0:T(128)S(1)} %pad_add_fusion.place_ref, s32[32]{0:T(128)S(1)} %copy-done, f32[32,640]{1,0:T(8,128)S(1)} %collective-permute-done.9.refs_0_, f32[32,640]{1,0:T(8,128)S(1)} %collective-permute-done.10.refs_1_, ...), custom_call_target="tpu_custom_call" | custom-call | tf_op jit(solution)/shard_map/attend/pallas_call | solution.py:306
  (14 shorter events, 0.2 us)
Async XLA Ops:
  1.6 8.4 %collective-permute-start = (bf16[32,2176]{1,0:T(8,128)(2,1)S(1)}, bf16[32,2176]{1,0:T(8,128)(2,1)S(1)}, u32[]{:S(2)}, u32[]{:S(2)}) collective-permute-start(bf16[32,2176]{1,0:T(8,128)(2,1)S(1)} %pack.1.refs_0_), channel_id=1, source_target_pairs={{0,12},{4,8},{8,4},{12,0},{1,13},{5,9},{9,5},{13,1},{2,14},{6,10},... | collective-permute-start | bytes 417800 | tf_op jit(solution)/shard_map/ppermute | solution.py:318
  2.1 13.3 %collective-permute-start.2 = (bf16[32,2176]{1,0:T(8,128)(2,1)S(1)}, bf16[32,2176]{1,0:T(8,128)(2,1)S(1)}, u32[]{:S(2)}, u32[]{:S(2)}) collective-permute-start(bf16[32,2176]{1,0:T(8,128)(2,1)S(1)} %pack.1.refs_0_), channel_id=1, source_target_pairs={{0,4},{4,0},{8,12},{12,8},{1,5},{5,1},{9,13},{13,9},{2,6},{6,2},{1... | collective-permute-start | bytes 417800 | tf_op jit(solution)/shard_map/ppermute | solution.py:318
  9.9 5.5 %collective-permute-start.1 = (bf16[32,2176]{1,0:T(8,128)(2,1)S(1)}, bf16[32,2176]{1,0:T(8,128)(2,1)S(1)}, u32[]{:S(2)}, u32[]{:S(2)}) collective-permute-start(bf16[32,2176]{1,0:T(8,128)(2,1)S(1)} %collective-permute-done.refs_1_), channel_id=1, source_target_pairs={{0,4},{4,0},{8,12},{12,8},{1,5},{5,1},{9,13},{13,9},{2,6},{6,2},{1... | collective-permute-start | bytes 417800 | tf_op jit(solution)/shard_map/ppermute | solution.py:318
  15.3 10.3 %copy-start = (s32[32]{0:T(128)S(1)}, s32[32]{0:T(128)}, u32[]{:S(2)}) copy-start(s32[32]{0:T(128)} %lengths_ref.1) | copy-start | bytes 388
  17.0 4.1 %collective-permute-start.3 = (f32[96,128]{1,0:T(8,128)S(1)}, f32[96,128]{1,0:T(8,128)S(1)}, u32[]{:S(2)}, u32[]{:S(2)}) collective-permute-start(f32[96,128]{1,0:T(8,128)S(1)} %get-tuple-element.19), channel_id=1, source_target_pairs={{0,3},{1,2},{2,1},{3,0},{4,7},{5,6},{6,5},{7,4},{8,11},{9,10},{10,... | collective-permute-start | bytes 147464 | tf_op jit(solution)/shard_map/ppermute | solution.py:318
  17.1 4.9 %collective-permute-start.4 = (f32[96,128]{1,0:T(8,128)S(1)}, f32[96,128]{1,0:T(8,128)S(1)}, u32[]{:S(2)}, u32[]{:S(2)}) collective-permute-start(f32[96,128]{1,0:T(8,128)S(1)} %get-tuple-element.19), channel_id=1, source_target_pairs={{0,2},{1,3},{2,0},{3,1},{4,6},{5,7},{6,4},{7,5},{8,10},{9,11},{10,... | collective-permute-start | bytes 147464 | tf_op jit(solution)/shard_map/ppermute | solution.py:318
  18.6 3.3 %collective-permute-start.5 = (f32[96,128]{1,0:T(8,128)S(1)}, f32[96,128]{1,0:T(8,128)S(1)}, u32[]{:S(2)}, u32[]{:S(2)}) collective-permute-start(f32[96,128]{1,0:T(8,128)S(1)} %get-tuple-element.19), channel_id=1, source_target_pairs={{0,1},{1,0},{2,3},{3,2},{4,5},{5,4},{6,7},{7,6},{8,9},{9,8},{10,11... | collective-permute-start | bytes 147464 | tf_op jit(solution)/shard_map/ppermute | solution.py:318
  22.0 4.0 %collective-permute-start.6 = (bf16[96,128]{1,0:T(8,128)(2,1)S(1)}, bf16[96,128]{1,0:T(8,128)(2,1)S(1)}, u32[]{:S(2)}, u32[]{:S(2)}) collective-permute-start(bf16[96,128]{1,0:T(8,128)(2,1)S(1)} %add_convert_fusion.refs_0_), channel_id=1, source_target_pairs={{0,12},{4,8},{8,4},{12,0},{1,13},{5,9},{9,5},{13,1},{2,14},{6,10},... | collective-permute-start | bytes 73736 | tf_op jit(solution)/shard_map/ppermute | solution.py:318
  22.2 5.6 %collective-permute-start.7 = (bf16[96,128]{1,0:T(8,128)(2,1)S(1)}, bf16[96,128]{1,0:T(8,128)(2,1)S(1)}, u32[]{:S(2)}, u32[]{:S(2)}) collective-permute-start(bf16[96,128]{1,0:T(8,128)(2,1)S(1)} %add_convert_fusion.refs_0_), channel_id=1, source_target_pairs={{0,8},{4,12},{8,0},{12,4},{1,9},{5,13},{9,1},{13,5},{2,10},{6,14},... | collective-permute-start | bytes 73736 | tf_op jit(solution)/shard_map/ppermute | solution.py:318
  25.6 3.8 %collective-permute-start.8 = (bf16[96,128]{1,0:T(8,128)(2,1)S(1)}, bf16[96,128]{1,0:T(8,128)(2,1)S(1)}, u32[]{:S(2)}, u32[]{:S(2)}) collective-permute-start(bf16[96,128]{1,0:T(8,128)(2,1)S(1)} %add_convert_fusion.refs_0_), channel_id=1, source_target_pairs={{0,4},{4,0},{8,12},{12,8},{1,5},{5,1},{9,13},{13,9},{2,6},{6,2},{1... | collective-permute-start | bytes 73736 | tf_op jit(solution)/shard_map/ppermute | solution.py:318
  30.8 7.7 %collective-permute-start.10 = (f32[32,640]{1,0:T(8,128)S(1)}, f32[32,640]{1,0:T(8,128)S(1)}, u32[]{:S(2)}, u32[]{:S(2)}) collective-permute-start(f32[32,640]{1,0:T(8,128)S(1)} %get-tuple-element.23), channel_id=1, source_target_pairs={{0,4},{1,0},{2,12},{3,8},{4,5},{5,1},{6,13},{7,9},{8,6},{9,2},{10,... | collective-permute-start | bytes 245768 | tf_op jit(solution)/shard_map/ppermute | solution.py:395
  31.2 7.3 %collective-permute-start.11 = (f32[32,640]{1,0:T(8,128)S(1)}, f32[32,640]{1,0:T(8,128)S(1)}, u32[]{:S(2)}, u32[]{:S(2)}) collective-permute-start(f32[32,640]{1,0:T(8,128)S(1)} %get-tuple-element.24), channel_id=1, source_target_pairs={{0,8},{1,12},{2,0},{3,4},{4,9},{5,13},{6,1},{7,5},{8,10},{9,14},{1... | collective-permute-start | bytes 245768 | tf_op jit(solution)/shard_map/ppermute | solution.py:395
  32.1 6.5 %collective-permute-start.12 = (f32[32,640]{1,0:T(8,128)S(1)}, f32[32,640]{1,0:T(8,128)S(1)}, u32[]{:S(2)}, u32[]{:S(2)}) collective-permute-start(f32[32,640]{1,0:T(8,128)S(1)} %get-tuple-element.25), channel_id=1, source_target_pairs={{0,12},{1,8},{2,4},{3,0},{4,13},{5,9},{6,5},{7,1},{8,14},{9,10},{1... | collective-permute-start | bytes 245768 | tf_op jit(solution)/shard_map/ppermute | solution.py:395
  35.9 8.1 %collective-permute-start.9 = (f32[32,640]{1,0:T(8,128)S(1)}, f32[32,640]{1,0:T(8,128)S(1)}, u32[]{:S(2)}, u32[]{:S(2)}) collective-permute-start(f32[32,640]{1,0:T(8,128)S(1)} %get-tuple-element.22), channel_id=1, source_target_pairs={{0,0},{1,4},{2,8},{3,12},{4,1},{5,5},{6,9},{7,13},{8,2},{9,6},{10,... | collective-permute-start | bytes 245768 | tf_op jit(solution)/shard_map/ppermute | solution.py:395

commit v3 on v2

--- a/solution.py
+++ b/solution.py
@@ -23,6 +23,30 @@
     )
     angles = positions.astype(jnp.float32)[:, None] * inv_freq[None, :]
     return jnp.cos(angles), jnp.sin(angles)
+
+
+FLIPS = 0b1111
+
+
+def position():
+    column = lax.axis_index("tensor")
+    return lax.axis_index("adapter"), column % 2, column // 2
+
+
+def plane_of(core, index):
+    return (3 * index) ^ core
+
+
+def core_of(plane):
+    return (plane ^ (plane >> 1)) & 1
+
+
+def index_of(plane):
+    return plane >> 1
+
+
+def flip_of(plane, core):
+    return (FLIPS >> (2 * plane + core)) & 1
 
 
 def pack_kernel(ids_in, hidden_in, out_ref, ids_ref, sems):
@@ -56,9 +80,9 @@
     )(request_adapter, hidden)
 
 
-def down_kernel(place_ref, *refs):
+def down_kernel(*refs):
     *message_refs, down_ref, out_ref, ids_ref, rows_ref = refs
-    place = place_ref[0]
+    place = position()[0]
     held, rank, width = down_ref.shape
     block = message_refs[0].shape[0]
     for k, message_ref in zip((0, 3, 2, 1), message_refs):
@@ -79,69 +103,89 @@
     out_ref[...] = total
 
 
-def up_kernel(place_ref, ids_ref, *refs):
-    shrink_refs = refs[:4]
-    up_query_ref, up_kv_ref, *out_refs, terms_ref = refs[4:]
+def up_kernel(ids_ref, *refs):
+    shrink_refs, query_refs, kv_refs = refs[:4], refs[4:6], refs[6:8]
+    *out_refs, rows_ref, terms_ref = refs[8:]
+    place, core, side = position()
+    side ^= flip_of(place, core)
     shrink = shrink_refs[0][...].astype(jnp.float32)
     for ref in shrink_refs[1:]:
         shrink += ref[...].astype(jnp.float32)
     rank = shrink.shape[0] // 3
-    rows = shrink.shape[1]
-    shrink = jnp.concatenate([shrink, jnp.zeros((LANES - 3 * rank, rows), jnp.float32)], axis=0)
-    shrink = jnp.transpose(shrink)
-    ids = ids_ref[...]
+    every = shrink.shape[1]
+    shrink = jnp.concatenate([shrink, jnp.zeros((LANES - 3 * rank, every), jnp.float32)], axis=0)
+    rows_ref[...] = jnp.transpose(shrink)
+    rows = every // 2
+    block = out_refs[0].shape[0]
+    starts = [pl.multiple_of(plane_of(core, i) * block, block) for i in range(2)]
+    shrink = jnp.concatenate([rows_ref[pl.ds(start, block), :] for start in starts], axis=0)
+    ids = jnp.concatenate([ids_ref[pl.ds(start, block), :] for start in starts], axis=0)
     lane = lax.broadcasted_iota(jnp.int32, (rows, LANES), 1)
-    count = up_query_ref.shape[0]
-    query = jnp.concatenate([shrink[:, :rank]] * (LANES // rank), axis=1)
-    lane_slot = (lane // rank).astype(jnp.float32)
-    step = LANES // rank
-    spread = jnp.concatenate(
+    count = query_refs[0].shape[0]
+
+    def spread(part, width):
+        slot = (lane // width).astype(jnp.float32)
+        each = LANES // width
+        return jnp.concatenate(
+            [
+                jnp.where(ids - c * each == slot, part, 0.0).astype(jnp.bfloat16)
+                for c in range(count // each)
+            ],
+            axis=1,
+        )
+
+    query = spread(jnp.concatenate([shrink[:, :rank]] * (LANES // rank), axis=1), rank)
+    pair = jnp.concatenate([shrink[:, rank : 3 * rank]] * (LANES // (2 * rank)), axis=1)
+    is_key = (lane // rank) % 2 == 0
+    pair = jnp.concatenate(
         [
-            jnp.where(ids - c * step == lane_slot, query, 0.0).astype(jnp.bfloat16)
-            for c in range(count // step)
+            spread(jnp.where(is_key, pair, 0.0), 2 * rank),
+            spread(jnp.where(is_key, 0.0, pair), 2 * rank),
         ],
-        axis=1,
-    )
-    terms_ref[:, : up_query_ref.shape[2]] = ADAPTER_SCALE * jnp.dot(
-        spread,
-        up_query_ref[...].reshape(count * rank, up_query_ref.shape[2]),
-        preferred_element_type=jnp.float32,
-    )
-    pair = jnp.concatenate([shrink[:, rank : 3 * rank]] * (LANES // (2 * rank)), axis=1)
-    lane_slot = (lane // (2 * rank)).astype(jnp.float32)
-    is_key = (lane // rank) % 2 == 0
-    key, value = jnp.where(is_key, pair, 0.0), jnp.where(is_key, 0.0, pair)
-    step = LANES // (2 * rank)
-    both = []
-    for part in (key, value):
-        both.append(
-            jnp.concatenate(
-                [
-                    jnp.where(ids - c * step == lane_slot, part, 0.0).astype(jnp.bfloat16)
-                    for c in range(count // step)
-                ],
-                axis=1,
+        axis=0,
+    )
+    width = query_refs[0].shape[2]
+    half = kv_refs[0].shape[3]
+    kv = []
+    for which in range(2):
+        column = pl.multiple_of((core ^ which) * width, width)
+        terms_ref[:, pl.ds(column, width)] = ADAPTER_SCALE * jnp.dot(
+            query,
+            query_refs[which][...].reshape(count * rank, width),
+            preferred_element_type=jnp.float32,
+        )
+        kv.append(
+            ADAPTER_SCALE
+            * jnp.dot(
+                pair,
+                kv_refs[which][...].reshape(count * 2 * rank, half),
+                preferred_element_type=jnp.float32,
             )
         )
-    kv_width = up_kv_ref.shape[3]
-    kv = ADAPTER_SCALE * jnp.dot(
-        jnp.concatenate(both, axis=0),
-        up_kv_ref[...].reshape(count * 2 * rank, kv_width),
-        preferred_element_type=jnp.float32,
-    )
-    terms_ref[:, up_query_ref.shape[2] :] = jnp.concatenate([kv[:rows], kv[rows:]], axis=1)
-    block = out_refs[0].shape[0]
+    both = jnp.concatenate(kv, axis=1)
+    both = jnp.where(core == 0, both, pltpu.roll(both, half, 1))
+    terms_ref[:, 2 * width : 2 * width + LANES] = both[:rows]
+    terms_ref[:, 2 * width + LANES :] = both[rows:]
+    terms = terms_ref[...]
+    largest = jnp.max(jnp.abs(terms), axis=1, keepdims=True)
+    power = jnp.clip(jnp.ceil(jnp.log2(jnp.maximum(largest, 1e-30))), -100.0, 100.0)
+    terms_ref[...] = terms * jnp.exp2(-power)
+    total = terms.shape[1]
     for k, out_ref in enumerate(out_refs):
-        start = pl.multiple_of((place_ref[1] ^ k) * block, block)
-        out_ref[...] = terms_ref[pl.ds(start, block), :]
-
-
-def attend_kernel(place_ref, lengths_ref, *refs):
-    term_refs = refs[:4]
+        at = pl.multiple_of((side ^ k) * block, block)
+        out_ref[:, :total] = terms_ref[pl.ds(at, block), :]
+        out_ref[:, total:] = jnp.broadcast_to(
+            jnp.where((side ^ k) == 0, power[:block], power[block:]), (block, LANES)
+        )
+
+
+def attend_kernel(*refs):
+    term_refs = refs[:2]
     (
         base_query_ref,
         base_key_ref,
         base_value_ref,
+        lengths_ref,
         cosine_ref,
         sine_ref,
         keys_ref,
@@ -156,19 +200,21 @@
         score_ref,
         weight_ref,
         new_weight_ref,
-    ) = refs[4:]
-    place = place_ref[0]
+    ) = refs[2:]
+    place, core, side = position()
+    odd = index_of(place) ^ flip_of(2 * side + core, core_of(place))
+    total = terms_ref.shape[2]
     for k, term_ref in enumerate(term_refs):
-        terms_ref[place ^ k] = term_ref[...]
+        scale = jnp.exp2(term_ref[:, total : total + 1])
+        terms_ref[odd ^ k] = term_ref[:, :total] * scale
     requests = base_query_ref.shape[0]
     kv_heads = keys_ref.shape[1]
     slots, head = keys_ref.shape[2], keys_ref.shape[3]
     half = head // 2
     heads = base_query_ref.shape[1] // head
     group = heads // kv_heads
-    each = terms_ref.shape[2] // head - 1
+    wide = group * head
     cosine, sine = cosine_ref[...], sine_ref[...]
-    lane = lax.broadcasted_iota(jnp.int32, (requests, head), 1)
     cosine = jnp.concatenate([cosine, cosine], axis=1)
     sine = jnp.concatenate([-sine, sine], axis=1)
 
@@ -176,21 +222,17 @@
         return (u * cosine + pltpu.roll(u, half, 1) * sine).astype(jnp.bfloat16)
 
     for h in range(heads):
-        c = (h % each) * head
+        c = (h % group) * head
         u = base_query_ref[:, h * head : (h + 1) * head].astype(jnp.float32)
-        u += terms_ref[h // each, :, c : c + head]
+        u += terms_ref[h // group, :, c : c + head]
         query_ref[pl.ds(h, requests, stride=heads), :] = rotate(u).astype(jnp.float32)
     for g in range(kv_heads):
-        low = terms_ref[2 * g, :, each * head :]
-        high = terms_ref[2 * g + 1, :, each * head :]
         u = base_key_ref[:, g * head : (g + 1) * head].astype(jnp.float32)
-        u += jnp.where(lane < half, low, pltpu.roll(high, half, 1))
-        key = rotate(u)
+        key = rotate(u + terms_ref[g, :, wide : wide + head])
         fresh_key_ref[:, g * head : (g + 1) * head] = key
         key_ref[pl.ds(g, requests, stride=kv_heads), :] = key.astype(jnp.float32)
         u = base_value_ref[:, g * head : (g + 1) * head].astype(jnp.float32)
-        u += jnp.where(lane < half, pltpu.roll(low, half, 1), high)
-        value = u.astype(jnp.bfloat16)
+        value = (u + terms_ref[g, :, wide + head :]).astype(jnp.bfloat16)
         fresh_value_ref[:, g * head : (g + 1) * head] = value
         value_ref[pl.ds(g, requests, stride=kv_heads), :] = value.astype(jnp.float32)
 
@@ -207,7 +249,11 @@
             score_ref[r * heads + g * group : r * heads + (g + 1) * group, :] = scores[
                 g * group : (g + 1) * group, g * slots : (g + 1) * slots
             ]
-    slot = lax.broadcasted_iota(jnp.int32, (heads, slots), 1)
+    row = lax.broadcasted_iota(jnp.int32, (requests, requests), 0)
+    lane = lax.broadcasted_iota(jnp.int32, (requests, requests), 1)
+    limits = jnp.where(row == lane, lengths_ref[...].astype(jnp.float32), 0.0)
+    limits = jnp.broadcast_to(jnp.sum(limits, axis=1, keepdims=True), (requests, slots))
+    slot = lax.broadcasted_iota(jnp.int32, (heads, slots), 1).astype(jnp.float32)
     for r in range(requests):
         rows = slice(r * heads, (r + 1) * heads)
         query = query_ref[rows, :]
@@ -219,7 +265,7 @@
             axis=0,
         )
         new_score = jnp.sum(query * new_key, axis=1, keepdims=True) * inv_sqrt
-        scores = jnp.where(slot < lengths_ref[r], score_ref[rows, :] * inv_sqrt, -jnp.inf)
+        scores = jnp.where(slot < limits[r : r + 1, :], score_ref[rows, :] * inv_sqrt, -jnp.inf)
         row_max = jnp.maximum(jnp.max(scores, axis=1, keepdims=True), new_score)
         weights = jnp.exp(scores - row_max)
         new_weight = jnp.exp(new_score - row_max)
@@ -228,9 +274,8 @@
         new_weight_ref[rows, :] = jnp.broadcast_to(new_weight / total, (heads, head))
     for r in range(requests):
         rows = slice(r * heads, (r + 1) * heads)
-        weights = weight_ref[rows, :].astype(jnp.bfloat16)
         zero = jnp.zeros((group, slots), jnp.float32)
-        wide = jnp.concatenate(
+        spread = jnp.concatenate(
             [
                 jnp.concatenate(
                     [
@@ -246,7 +291,7 @@
             axis=0,
         ).astype(jnp.bfloat16)
         mixed = jnp.dot(
-            wide,
+            spread,
             values_ref[r].reshape(kv_heads * slots, head),
             preferred_element_type=jnp.float32,
         )
@@ -294,24 +339,20 @@
     )(*arrays)
 
 
-def in_smem():
-    return pl.BlockSpec(memory_space=pltpu.SMEM)
-
-
 def in_vmem():
     return pl.BlockSpec(memory_space=pltpu.VMEM)
 
 
-def call(kernel, name, out_shape, scratch, scalars, arrays):
+def call(kernel, name, out_shape, scratch, arrays):
     return pl.pallas_call(
         kernel,
         out_shape=out_shape,
-        in_specs=[in_smem()] * len(scalars) + [in_vmem()] * len(arrays),
+        in_specs=[in_vmem()] * len(arrays),
         out_specs=[in_vmem()] * len(out_shape),
         scratch_shapes=scratch,
         compiler_params=pltpu.CompilerParams(vmem_limit_bytes=VMEM_BYTES),
         name=name,
-    )(*scalars, *arrays)
+    )(*arrays)
 
 
 def step(value, axis, size, k):
@@ -336,9 +377,6 @@
     lengths,
 ):
     planes, columns = lax.axis_size("adapter"), lax.axis_size("tensor")
-    place = lax.axis_index("adapter")
-    number = place * columns + lax.axis_index("tensor")
-    places = jnp.stack([place, number % planes]).astype(jnp.int32)
     requests = hidden.shape[0]
     every = requests * planes
     rank3 = adapter_down_weight.shape[1]
@@ -351,6 +389,19 @@
     mirror = step(message, "adapter", planes, planes - 1)
     near = step(message, "adapter", planes, 1)
     everyone = [message, mirror, step(mirror, "adapter", planes, 1), near]
+    sent = [
+        [
+            (
+                a * columns + t,
+                plane_of(t % 2, (t // 2) ^ k ^ flip_of(a, t % 2)) * columns + a,
+            )
+            for a in range(planes)
+            for t in range(columns)
+        ]
+        for k in range(2)
+    ]
+    other_query = step(adapter_up_query, "tensor", columns, 1)
+    other_key_value = step(adapter_up_key_value, "tensor", columns, 1)
     (
         adapter_down_weight,
         adapter_up_query,
@@ -377,26 +428,27 @@
         "down",
         [jax.ShapeDtypeStruct((rank3, every), f32), jax.ShapeDtypeStruct((every, LANES), f32)],
         [pltpu.VMEM((every, hidden.shape[1] + LANES), bf16)],
-        [places],
         [*everyone, adapter_down_weight],
     )
     summed = functools.reduce(jnp.add, exchange(partial, "tensor", columns)).astype(bf16)
     shrink = exchange(summed, "adapter", planes)
-    width = adapter_up_query.shape[2] + 2 * adapter_up_key_value.shape[3]
+    width = 2 * adapter_up_query.shape[2] + 4 * adapter_up_key_value.shape[3]
     terms = call(
         up_kernel,
         "up",
-        [jax.ShapeDtypeStruct((requests, width), f32)] * planes,
-        [pltpu.VMEM((every, width), f32)],
-        [places],
-        [every_id, *shrink, adapter_up_query, adapter_up_key_value],
+        [jax.ShapeDtypeStruct((requests, width + LANES), f32)] * 2,
+        [pltpu.VMEM((every, LANES), f32), pltpu.VMEM((every // 2, width), f32)],
+        [
+            every_id,
+            *shrink,
+            adapter_up_query,
+            other_query,
+            adapter_up_key_value,
+            other_key_value,
+        ],
     )
     arrived = [
-        lax.ppermute(
-            term,
-            ("adapter", "tensor"),
-            [(n, ((n % planes) ^ k) * columns + n // planes) for n in range(planes * columns)],
-        )
+        lax.ppermute(term.astype(jnp.float16), ("adapter", "tensor"), sent[k]).astype(f32)
         for k, term in enumerate(terms)
     ]
     cosine, sine = rotation_factors(lengths, head)
@@ -410,7 +462,7 @@
                 jax.ShapeDtypeStruct(base_values.shape, bf16),
             ],
             [
-                pltpu.VMEM((planes, requests, width), f32),
+                pltpu.VMEM((2, requests, width), f32),
                 pltpu.VMEM((requests * heads, head), f32),
                 pltpu.VMEM((requests * kv_heads, head), f32),
                 pltpu.VMEM((requests * kv_heads, head), f32),
@@ -418,8 +470,17 @@
                 pltpu.VMEM((requests * heads, head), f32),
                 pltpu.VMEM((requests * heads, head), f32),
             ],
-            [places, lengths],
-            [*arrived, base_queries, base_keys, base_values, cosine, sine, cached_keys, cached_values],
+            [
+                *arrived,
+                base_queries,
+                base_keys,
+                base_values,
+                lengths[None, :],
+                cosine,
+                sine,
+                cached_keys,
+                cached_values,
+            ],
         )
     )
 

time: 46.5 us -> 42.3 us (0.910)
  starting transfers between devices: 16.6 us -> 12.1 us
  waiting for transfers between devices: 18.8 us -> 20.3 us
  Pallas kernels: 9.9 us -> 8.71 us
    ppermute x4 -> x2, starting transfers between devices: 7.55 us -> 3.67 us  [few_body(): lax.ppermute(term.astype(jnp.float16), ('adapter', 'tensor'), sent[k])]
    pallas_call x3, Pallas kernels: 5.22 us -> 4.03 us  [call(): pl.pallas_call(kernel, out_shape=out_shape, in_specs=[in_vmem()] * len(ar...]
    ppermute x4 -> x2, waiting for transfers between devices: 5.47 us -> 6.27 us  [few_body(): lax.ppermute(term.astype(jnp.float16), ('adapter', 'tensor'), sent[k])]
    ppermute x9 -> x11, waiting for transfers between devices: 13.4 us -> 14 us  [step(): return lax.ppermute(value, axis, [(i, i ^ k) for i in range(size)])]
    ppermute x9 -> x11, starting transfers between devices: 9.02 us -> 8.46 us  [step(): return lax.ppermute(value, axis, [(i, i ^ k) for i in range(size)])]
  transfers between devices with their start and end apart: 13 -> 13, of which waited for: 7 -> 9; matrix products, arithmetic and copies ran while one was open for 0% -> 0% of each run, Pallas kernels for 8% -> 14%
where the time goes in v3:
time: 42.3 us; the launch traced here: 42.1 us
  waiting for transfers between devices  20.3 us (48%)
  starting transfers between devices  12.1 us (29%)
  Pallas kernels  8.71 us (21%)
  between operations  0.76 us (2%)
    ppermute x11, waiting for transfers between devices, step(): return lax.ppermute(value, axis, [(i, i ^ k) for i in range(size)])  14 us
    ppermute x11, starting transfers between devices, step(): return lax.ppermute(value, axis, [(i, i ^ k) for i in range(size)])  8.46 us
    ppermute x2, waiting for transfers between devices, few_body(): lax.ppermute(term.astype(jnp.float16), ('adapter', 'tensor'), sent[k])  6.27 us
    pallas_call x3, Pallas kernels, call(): pl.pallas_call(kernel, out_shape=out_shape, in_specs=[in_vmem()] * len(ar...  4.03 us
    pallas_call x1, Pallas kernels, load(): pl.pallas_call(load_kernel, out_shape=[pltpu.VMEM(a.shape, a.dtype) for a...  3.76 us
    ppermute x2, starting transfers between devices, few_body(): lax.ppermute(term.astype(jnp.float16), ('adapter', 'tensor'), sent[k])  3.67 us
    pallas_call x1, Pallas kernels, pack(): pl.pallas_call(pack_kernel, out_shape=pltpu.VMEM((requests, width + LANES...  0.92 us
  transfers between devices with their start and end apart: 13, of which 9 were waited for; matrix products, arithmetic and copies ran while one was open for 0% of the time, Pallas kernels for 14%

profile of v3, /device:TPU:20, one launch (start us, length us, event | category | flops | bytes accessed | tf_op | source)
XLA Modules:
  0.0 42.1 jit_solution(8171950518894426208)
XLA Ops:
  0.7 0.9 %pack.1.refs_0_ = bf16[32,2176]{1,0:T(8,128)(2,1)S(1)} custom-call(s32[32]{0:T(128)} %ids_in.1, bf16[32,2048]{1,0:T(8,128)(2,1)} %hidden_in.1), custom_call_target="tpu_custom_call" | custom-call | tf_op jit(solution)/shard_map/pack/pallas_call | solution.py:69
  1.6 0.5 %collective-permute-start = (bf16[32,2176]{1,0:T(8,128)(2,1)S(1)}, bf16[32,2176]{1,0:T(8,128)(2,1)S(1)}, u32[]{:S(2)}, u32[]{:S(2)}) collective-permute-start(bf16[32,2176]{1,0:T(8,128)(2,1)S(1)} %pack.1.refs_0_), channel_id=1, source_target_pairs={{0,12},{4,8},{8,4},{12,0},{1,13},{5,9},{9,5},{13,1},{2,14},{6,10},... | collective-permute-start | bytes 417800 | tf_op jit(solution)/shard_map/ppermute | solution.py:359
  2.2 1.3 %collective-permute-start.2 = (bf16[32,2176]{1,0:T(8,128)(2,1)S(1)}, bf16[32,2176]{1,0:T(8,128)(2,1)S(1)}, u32[]{:S(2)}, u32[]{:S(2)}) collective-permute-start(bf16[32,2176]{1,0:T(8,128)(2,1)S(1)} %pack.1.refs_0_), channel_id=1, source_target_pairs={{0,4},{4,0},{8,12},{12,8},{1,5},{5,1},{9,13},{13,9},{2,6},{6,2},{1... | collective-permute-start | bytes 417800 | tf_op jit(solution)/shard_map/ppermute | solution.py:359
  3.5 7.3 %collective-permute-done.refs_1_ = bf16[32,2176]{1,0:T(8,128)(2,1)S(1)} collective-permute-done((bf16[32,2176]{1,0:T(8,128)(2,1)S(1)}, bf16[32,2176]{1,0:T(8,128)(2,1)S(1)}, u32[]{:S(2)}, u32[]{:S(2)}) %collective-permute-start) | collective-permute-done | bytes 139296 | tf_op jit(solution)/shard_map/ppermute | solution.py:359
  10.8 0.8 %collective-permute-start.1 = (bf16[32,2176]{1,0:T(8,128)(2,1)S(1)}, bf16[32,2176]{1,0:T(8,128)(2,1)S(1)}, u32[]{:S(2)}, u32[]{:S(2)}) collective-permute-start(bf16[32,2176]{1,0:T(8,128)(2,1)S(1)} %collective-permute-done.refs_1_), channel_id=1, source_target_pairs={{0,4},{4,0},{8,12},{12,8},{1,5},{5,1},{9,13},{13,9},{2,6},{6,2},{1... | collective-permute-start | bytes 417800 | tf_op jit(solution)/shard_map/ppermute | solution.py:359
  11.6 3.8 %load.1 = (bf16[8,96,2048]{2,1,0:T(8,128)(2,1)S(1)}, bf16[32,32,512]{2,1,0:T(8,128)(2,1)S(1)}, bf16[32,2,32,64]{3,2,1,0:T(8,128)(2,1)S(1)}, bf16[32,2048]{1,0:T(...) custom-call(bf16[8,96,2048]{2,1,0:T(8,128)(2,1)} %refs_0_.1, ...), custom_call_target="tpu_custom_call" | custom-call | bytes 17629184 | tf_op jit(solution)/shard_map/load/pallas_call | solution.py:328
  15.4 0.6 %collective-permute-done.1.refs_2_ = bf16[32,2176]{1,0:T(8,128)(2,1)S(1)} collective-permute-done((bf16[32,2176]{1,0:T(8,128)(2,1)S(1)}, bf16[32,2176]{1,0:T(8,128)(2,1)S(1)}, u32[]{:S(2)}, u32[]{:S(2)}) %collective-permute-start.1) | collective-permute-done | bytes 139296 | tf_op jit(solution)/shard_map/ppermute | solution.py:359
  16.0 1.0 %down.1 = (f32[96,128]{1,0:T(8,128)S(1)}, f32[128,128]{1,0:T(8,128)S(1)}) custom-call(bf16[32,2176]{1,0:T(8,128)(2,1)S(1)} %pack.1.refs_0_, bf16[32,2176]{1,0:T(8,128)(2,1)S(1)} %collective-permute-done.refs_1_, bf16[32,2176]{1,0:T(8,128)(2,1)S(1)} %collective-permute-done.1.refs_2_, bf16[32,2176]{1,0:T(8,128)(2,1)S(1)} %collective-permute-done.2.refs_3_, ...), custom_call_target="tpu_custom_call" | custom-call | tf_op jit(solution)/shard_map/down/pallas_call | solution.py:347
  17.2 1.6 %collective-permute-start.4 = (f32[96,128]{1,0:T(8,128)S(1)}, f32[96,128]{1,0:T(8,128)S(1)}, u32[]{:S(2)}, u32[]{:S(2)}) collective-permute-start(f32[96,128]{1,0:T(8,128)S(1)} %get-tuple-element.17), channel_id=1, source_target_pairs={{0,2},{1,3},{2,0},{3,1},{4,6},{5,7},{6,4},{7,5},{8,10},{9,11},{10,... | collective-permute-start | bytes 147464 | tf_op jit(solution)/shard_map/ppermute | solution.py:359
  18.7 0.3 collective-permute-start.5
  19.2 1.9 %collective-permute-done.3 = f32[96,128]{1,0:T(8,128)S(1)} collective-permute-done((f32[96,128]{1,0:T(8,128)S(1)}, f32[96,128]{1,0:T(8,128)S(1)}, u32[]{:S(2)}, u32[]{:S(2)}) %collective-permute-start.3) | collective-permute-done | bytes 49184 | tf_op jit(solution)/shard_map/ppermute | solution.py:359
  21.1 0.9 %collective-permute-done.4 = f32[96,128]{1,0:T(8,128)S(1)} collective-permute-done((f32[96,128]{1,0:T(8,128)S(1)}, f32[96,128]{1,0:T(8,128)S(1)}, u32[]{:S(2)}, u32[]{:S(2)}) %collective-permute-start.4) | collective-permute-done | bytes 49184 | tf_op jit(solution)/shard_map/ppermute | solution.py:359
  22.1 0.5 %collective-permute-start.6 = (bf16[96,128]{1,0:T(8,128)(2,1)S(1)}, bf16[96,128]{1,0:T(8,128)(2,1)S(1)}, u32[]{:S(2)}, u32[]{:S(2)}) collective-permute-start(bf16[96,128]{1,0:T(8,128)(2,1)S(1)} %add_convert_fusion.refs_0_), channel_id=1, source_target_pairs={{0,12},{4,8},{8,4},{12,0},{1,13},{5,9},{9,5},{13,1},{2,14},{6,10},... | collective-permute-start | bytes 73736 | tf_op jit(solution)/shard_map/ppermute | solution.py:359
  22.6 2.5 %collective-permute-start.7 = (bf16[96,128]{1,0:T(8,128)(2,1)S(1)}, bf16[96,128]{1,0:T(8,128)(2,1)S(1)}, u32[]{:S(2)}, u32[]{:S(2)}) collective-permute-start(bf16[96,128]{1,0:T(8,128)(2,1)S(1)} %add_convert_fusion.refs_0_), channel_id=1, source_target_pairs={{0,8},{4,12},{8,0},{12,4},{1,9},{5,13},{9,1},{13,5},{2,10},{6,14},... | collective-permute-start | bytes 73736 | tf_op jit(solution)/shard_map/ppermute | solution.py:359
  25.1 0.5 %collective-permute-start.8 = (bf16[96,128]{1,0:T(8,128)(2,1)S(1)}, bf16[96,128]{1,0:T(8,128)(2,1)S(1)}, u32[]{:S(2)}, u32[]{:S(2)}) collective-permute-start(bf16[96,128]{1,0:T(8,128)(2,1)S(1)} %add_convert_fusion.refs_0_), channel_id=1, source_target_pairs={{0,4},{4,0},{8,12},{12,8},{1,5},{5,1},{9,13},{13,9},{2,6},{6,2},{1... | collective-permute-start | bytes 73736 | tf_op jit(solution)/shard_map/ppermute | solution.py:359
  25.7 0.9 %collective-permute-done.6.refs_1_ = bf16[96,128]{1,0:T(8,128)(2,1)S(1)} collective-permute-done((bf16[96,128]{1,0:T(8,128)(2,1)S(1)}, bf16[96,128]{1,0:T(8,128)(2,1)S(1)}, u32[]{:S(2)}, u32[]{:S(2)}) %collective-permute-start.6) | collective-permute-done | bytes 24608 | tf_op jit(solution)/shard_map/ppermute | solution.py:359
  26.6 0.9 %collective-permute-done.7.refs_2_ = bf16[96,128]{1,0:T(8,128)(2,1)S(1)} collective-permute-done((bf16[96,128]{1,0:T(8,128)(2,1)S(1)}, bf16[96,128]{1,0:T(8,128)(2,1)S(1)}, u32[]{:S(2)}, u32[]{:S(2)}) %collective-permute-start.7) | collective-permute-done | bytes 24608 | tf_op jit(solution)/shard_map/ppermute | solution.py:359
  27.4 1.5 %collective-permute-done.8.refs_3_ = bf16[96,128]{1,0:T(8,128)(2,1)S(1)} collective-permute-done((bf16[96,128]{1,0:T(8,128)(2,1)S(1)}, bf16[96,128]{1,0:T(8,128)(2,1)S(1)}, u32[]{:S(2)}, u32[]{:S(2)}) %collective-permute-start.8) | collective-permute-done | bytes 24608 | tf_op jit(solution)/shard_map/ppermute | solution.py:359
  29.0 1.2 %up.1 = (f32[32,1408]{1,0:T(8,128)S(1)}, f32[32,1408]{1,0:T(8,128)S(1)}) custom-call(f32[128,128]{1,0:T(8,128)S(1)} %get-tuple-element.16.ids_ref, bf16[96,128]{1,0:T(8,128)(2,1)S(1)} %add_convert_fusion.refs_0_, bf16[96,128]{1,0:T(8,128)(2,1)S(1)} %collective-permute-done.6.refs_1_, bf16[96,128]{1,0:T(8,128)(2,1)S(1)} %collective-permute-done.7.refs_2_, ...), custom_call_target="tpu_custom_call" | custom-call | tf_op jit(solution)/shard_map/up/pallas_call | solution.py:347
  30.1 1.7 %collective-permute-start.11 = (f16[32,1408]{1,0:T(8,128)(2,1)S(1)}, f16[32,1408]{1,0:T(8,128)(2,1)S(1)}, u32[]{:S(2)}, u32[]{:S(2)}) collective-permute-start(f16[32,1408]{1,0:T(8,128)(2,1)S(1)} %convert_element_type.19), channel_id=1, source_target_pairs={{0,12},{1,8},{2,0},{3,4},{4,13},{5,9},{6,1},{7,5},{8,2},{9,6},{10,... | collective-permute-start | bytes 270344 | tf_op jit(solution)/shard_map/ppermute | solution.py:451
  31.9 1.9 %collective-permute-start.12 = (f16[32,1408]{1,0:T(8,128)(2,1)S(1)}, f16[32,1408]{1,0:T(8,128)(2,1)S(1)}, u32[]{:S(2)}, u32[]{:S(2)}) collective-permute-start(f16[32,1408]{1,0:T(8,128)(2,1)S(1)} %convert_element_type.21), channel_id=1, source_target_pairs={{0,0},{1,4},{2,12},{3,8},{4,1},{5,5},{6,13},{7,9},{8,14},{9,10},{1... | collective-permute-start | bytes 270344 | tf_op jit(solution)/shard_map/ppermute | solution.py:451
  34.0 1.6 %collective-permute-done.11 = f16[32,1408]{1,0:T(8,128)(2,1)S(1)} collective-permute-done((f16[32,1408]{1,0:T(8,128)(2,1)S(1)}, f16[32,1408]{1,0:T(8,128)(2,1)S(1)}, u32[]{:S(2)}, u32[]{:S(2)}) %collective-permute-start.11) | collective-permute-done | bytes 90144 | tf_op jit(solution)/shard_map/ppermute | solution.py:451
  35.6 4.7 %collective-permute-done.12 = f16[32,1408]{1,0:T(8,128)(2,1)S(1)} collective-permute-done((f16[32,1408]{1,0:T(8,128)(2,1)S(1)}, f16[32,1408]{1,0:T(8,128)(2,1)S(1)}, u32[]{:S(2)}, u32[]{:S(2)}) %collective-permute-start.12) | collective-permute-done | bytes 90144 | tf_op jit(solution)/shard_map/ppermute | solution.py:451
  40.3 1.8 %attend.1 = (bf16[32,2048]{1,0:T(8,128)(2,1)}, bf16[32,256]{1,0:T(8,128)(2,1)}, bf16[32,256]{1,0:T(8,128)(2,1)}) custom-call(f32[32,1408]{1,0:T(8,128)S(1)} %convert_element_type.20.refs_0_, f32[32,1408]{1,0:T(8,128)S(1)} %convert_element_type.22.refs_1_, bf16[32,2048]{1,0:T(8,128)(2,1)S(1)} %get-tuple-element.22.refs_2_, ...), custom_call_target="tpu_custom_call" | custom-call | tf_op jit(solution)/shard_map/attend/pallas_call | solution.py:347
  (19 shorter events, 0.6 us)
Async XLA Ops:
  0.6 28.3 %collective-permute-start.9 = (bf16[32,32,512]{2,1,0:T(8,128)(2,1)}, bf16[32,32,512]{2,1,0:T(8,128)(2,1)S(1)}, u32[]{:S(2)}, u32[]{:S(2)}) collective-permute-start(bf16[32,32,512]{2,1,0:T(8,128)(2,1)} %refs_1_.1), channel_id=1, source_target_pairs={{0,1},{1,0},{2,3},{3,2},{4,5},{5,4},{6,7},{7,6},{8,9},{9,8},{10,11... | collective-permute-start | bytes 3145736 | tf_op jit(solution)/shard_map/ppermute | solution.py:359
  1.6 9.1 %collective-permute-start = (bf16[32,2176]{1,0:T(8,128)(2,1)S(1)}, bf16[32,2176]{1,0:T(8,128)(2,1)S(1)}, u32[]{:S(2)}, u32[]{:S(2)}) collective-permute-start(bf16[32,2176]{1,0:T(8,128)(2,1)S(1)} %pack.1.refs_0_), channel_id=1, source_target_pairs={{0,12},{4,8},{8,4},{12,0},{1,13},{5,9},{9,5},{13,1},{2,14},{6,10},... | collective-permute-start | bytes 417800 | tf_op jit(solution)/shard_map/ppermute | solution.py:359
  2.2 13.2 %collective-permute-start.2 = (bf16[32,2176]{1,0:T(8,128)(2,1)S(1)}, bf16[32,2176]{1,0:T(8,128)(2,1)S(1)}, u32[]{:S(2)}, u32[]{:S(2)}) collective-permute-start(bf16[32,2176]{1,0:T(8,128)(2,1)S(1)} %pack.1.refs_0_), channel_id=1, source_target_pairs={{0,4},{4,0},{8,12},{12,8},{1,5},{5,1},{9,13},{13,9},{2,6},{6,2},{1... | collective-permute-start | bytes 417800 | tf_op jit(solution)/shard_map/ppermute | solution.py:359
  10.8 5.3 %collective-permute-start.1 = (bf16[32,2176]{1,0:T(8,128)(2,1)S(1)}, bf16[32,2176]{1,0:T(8,128)(2,1)S(1)}, u32[]{:S(2)}, u32[]{:S(2)}) collective-permute-start(bf16[32,2176]{1,0:T(8,128)(2,1)S(1)} %collective-permute-done.refs_1_), channel_id=1, source_target_pairs={{0,4},{4,0},{8,12},{12,8},{1,5},{5,1},{9,13},{13,9},{2,6},{6,2},{1... | collective-permute-start | bytes 417800 | tf_op jit(solution)/shard_map/ppermute | solution.py:359
  15.4 3.6 %copy-start.1 = (bf16[32,2,32,64]{3,2,1,0:T(8,128)(2,1)S(1)}, bf16[32,2,32,64]{3,2,1,0:T(8,128)(2,1)}, u32[]{:S(2)}) copy-start(bf16[32,2,32,64]{3,2,1,0:T(8,128)(2,1)} %refs_2_.1) | copy-start | bytes 786436
  15.4 10.3 %copy-start = (s32[32]{0:T(128)S(1)}, s32[32]{0:T(128)}, u32[]{:S(2)}) copy-start(s32[32]{0:T(128)} %param.21) | copy-start | bytes 388
  17.1 4.1 %collective-permute-start.3 = (f32[96,128]{1,0:T(8,128)S(1)}, f32[96,128]{1,0:T(8,128)S(1)}, u32[]{:S(2)}, u32[]{:S(2)}) collective-permute-start(f32[96,128]{1,0:T(8,128)S(1)} %get-tuple-element.17), channel_id=1, source_target_pairs={{0,3},{1,2},{2,1},{3,0},{4,7},{5,6},{6,5},{7,4},{8,11},{9,10},{10,... | collective-permute-start | bytes 147464 | tf_op jit(solution)/shard_map/ppermute | solution.py:359
  17.2 4.9 %collective-permute-start.4 = (f32[96,128]{1,0:T(8,128)S(1)}, f32[96,128]{1,0:T(8,128)S(1)}, u32[]{:S(2)}, u32[]{:S(2)}) collective-permute-start(f32[96,128]{1,0:T(8,128)S(1)} %get-tuple-element.17), channel_id=1, source_target_pairs={{0,2},{1,3},{2,0},{3,1},{4,6},{5,7},{6,4},{7,5},{8,10},{9,11},{10,... | collective-permute-start | bytes 147464 | tf_op jit(solution)/shard_map/ppermute | solution.py:359
  18.7 3.3 %collective-permute-start.5 = (f32[96,128]{1,0:T(8,128)S(1)}, f32[96,128]{1,0:T(8,128)S(1)}, u32[]{:S(2)}, u32[]{:S(2)}) collective-permute-start(f32[96,128]{1,0:T(8,128)S(1)} %get-tuple-element.17), channel_id=1, source_target_pairs={{0,1},{1,0},{2,3},{3,2},{4,5},{5,4},{6,7},{7,6},{8,9},{9,8},{10,11... | collective-permute-start | bytes 147464 | tf_op jit(solution)/shard_map/ppermute | solution.py:359
  19.0 6.7 %collective-permute-start.10 = (bf16[32,2,32,64]{3,2,1,0:T(8,128)(2,1)S(1)}, bf16[32,2,32,64]{3,2,1,0:T(8,128)(2,1)S(1)}, u32[]{:S(2)}, u32[]{:S(2)}) collective-permute-start(bf16[32,2,32,64]{3,2,1,0:T(8,128)(2,1)S(1)} %copy-done.1), channel_id=1, source_target_pairs={{0,1},{1,0},{2,3},{3,2},{4,5},{5,4},{6,7},{7,6},{8,9},{9,8},{10,11... | collective-permute-start | bytes 786440 | tf_op jit(solution)/shard_map/ppermute | solution.py:359
  22.1 4.5 %collective-permute-start.6 = (bf16[96,128]{1,0:T(8,128)(2,1)S(1)}, bf16[96,128]{1,0:T(8,128)(2,1)S(1)}, u32[]{:S(2)}, u32[]{:S(2)}) collective-permute-start(bf16[96,128]{1,0:T(8,128)(2,1)S(1)} %add_convert_fusion.refs_0_), channel_id=1, source_target_pairs={{0,12},{4,8},{8,4},{12,0},{1,13},{5,9},{9,5},{13,1},{2,14},{6,10},... | collective-permute-start | bytes 73736 | tf_op jit(solution)/shard_map/ppermute | solution.py:359
  22.6 4.8 %collective-permute-start.7 = (bf16[96,128]{1,0:T(8,128)(2,1)S(1)}, bf16[96,128]{1,0:T(8,128)(2,1)S(1)}, u32[]{:S(2)}, u32[]{:S(2)}) collective-permute-start(bf16[96,128]{1,0:T(8,128)(2,1)S(1)} %add_convert_fusion.refs_0_), channel_id=1, source_target_pairs={{0,8},{4,12},{8,0},{12,4},{1,9},{5,13},{9,1},{13,5},{2,10},{6,14},... | collective-permute-start | bytes 73736 | tf_op jit(solution)/shard_map/ppermute | solution.py:359
  25.1 3.8 %collective-permute-start.8 = (bf16[96,128]{1,0:T(8,128)(2,1)S(1)}, bf16[96,128]{1,0:T(8,128)(2,1)S(1)}, u32[]{:S(2)}, u32[]{:S(2)}) collective-permute-start(bf16[96,128]{1,0:T(8,128)(2,1)S(1)} %add_convert_fusion.refs_0_), channel_id=1, source_target_pairs={{0,4},{4,0},{8,12},{12,8},{1,5},{5,1},{9,13},{13,9},{2,6},{6,2},{1... | collective-permute-start | bytes 73736 | tf_op jit(solution)/shard_map/ppermute | solution.py:359
  30.1 5.4 %collective-permute-start.11 = (f16[32,1408]{1,0:T(8,128)(2,1)S(1)}, f16[32,1408]{1,0:T(8,128)(2,1)S(1)}, u32[]{:S(2)}, u32[]{:S(2)}) collective-permute-start(f16[32,1408]{1,0:T(8,128)(2,1)S(1)} %convert_element_type.19), channel_id=1, source_target_pairs={{0,12},{1,8},{2,0},{3,4},{4,13},{5,9},{6,1},{7,5},{8,2},{9,6},{10,... | collective-permute-start | bytes 270344 | tf_op jit(solution)/shard_map/ppermute | solution.py:451
  31.9 8.4 %collective-permute-start.12 = (f16[32,1408]{1,0:T(8,128)(2,1)S(1)}, f16[32,1408]{1,0:T(8,128)(2,1)S(1)}, u32[]{:S(2)}, u32[]{:S(2)}) collective-permute-start(f16[32,1408]{1,0:T(8,128)(2,1)S(1)} %convert_element_type.21), channel_id=1, source_target_pairs={{0,0},{1,4},{2,12},{3,8},{4,1},{5,5},{6,13},{7,9},{8,14},{9,10},{1... | collective-permute-start | bytes 270344 | tf_op jit(solution)/shard_map/ppermute | solution.py:451

commit v4 on v3

--- a/solution.py
+++ b/solution.py
@@ -123,49 +123,36 @@
     lane = lax.broadcasted_iota(jnp.int32, (rows, LANES), 1)
     count = query_refs[0].shape[0]
 
-    def spread(part, width):
-        slot = (lane // width).astype(jnp.float32)
-        each = LANES // width
+    each = LANES // rank
+    here = [ids - c * each == (lane // rank).astype(jnp.float32) for c in range(count // each)]
+
+    def spread(part):
+        part = jnp.concatenate([part] * each, axis=1)
         return jnp.concatenate(
-            [
-                jnp.where(ids - c * each == slot, part, 0.0).astype(jnp.bfloat16)
-                for c in range(count // each)
-            ],
-            axis=1,
-        )
-
-    query = spread(jnp.concatenate([shrink[:, :rank]] * (LANES // rank), axis=1), rank)
-    pair = jnp.concatenate([shrink[:, rank : 3 * rank]] * (LANES // (2 * rank)), axis=1)
-    is_key = (lane // rank) % 2 == 0
-    pair = jnp.concatenate(
-        [
-            spread(jnp.where(is_key, pair, 0.0), 2 * rank),
-            spread(jnp.where(is_key, 0.0, pair), 2 * rank),
-        ],
-        axis=0,
-    )
+            [jnp.where(mask, part, 0.0).astype(jnp.bfloat16) for mask in here], axis=1
+        )
+
+    query, key, value = [spread(shrink[:, i * rank : (i + 1) * rank]) for i in range(3)]
     width = query_refs[0].shape[2]
     half = kv_refs[0].shape[3]
-    kv = []
+
+    def product(rows_spread, factors):
+        return ADAPTER_SCALE * jnp.dot(
+            rows_spread,
+            factors.reshape(count * rank, factors.shape[-1]),
+            preferred_element_type=jnp.float32,
+        )
+
+    keys, new_values = [], []
     for which in range(2):
         column = pl.multiple_of((core ^ which) * width, width)
-        terms_ref[:, pl.ds(column, width)] = ADAPTER_SCALE * jnp.dot(
-            query,
-            query_refs[which][...].reshape(count * rank, width),
-            preferred_element_type=jnp.float32,
-        )
-        kv.append(
-            ADAPTER_SCALE
-            * jnp.dot(
-                pair,
-                kv_refs[which][...].reshape(count * 2 * rank, half),
-                preferred_element_type=jnp.float32,
-            )
-        )
-    both = jnp.concatenate(kv, axis=1)
-    both = jnp.where(core == 0, both, pltpu.roll(both, half, 1))
-    terms_ref[:, 2 * width : 2 * width + LANES] = both[:rows]
-    terms_ref[:, 2 * width + LANES :] = both[rows:]
+        terms_ref[:, pl.ds(column, width)] = product(query, query_refs[which][...])
+        keys.append(product(key, kv_refs[which][:, 0]))
+        new_values.append(product(value, kv_refs[which][:, 1]))
+    for i, parts in enumerate((keys, new_values)):
+        both = jnp.concatenate(parts, axis=1)
+        both = jnp.where(core == 0, both, pltpu.roll(both, half, 1))
+        terms_ref[:, 2 * width + i * LANES : 2 * width + (i + 1) * LANES] = both
     terms = terms_ref[...]
     largest = jnp.max(jnp.abs(terms), axis=1, keepdims=True)
     power = jnp.clip(jnp.ceil(jnp.log2(jnp.maximum(largest, 1e-30))), -100.0, 100.0)
@@ -179,9 +166,9 @@
         )
 
 
-def attend_kernel(*refs):
-    term_refs = refs[:2]
+def attend_kernel(message, *refs):
     (
+        term_ref,
         base_query_ref,
         base_key_ref,
         base_value_ref,
@@ -190,30 +177,28 @@
         sine_ref,
         keys_ref,
         values_ref,
+    ) = refs[:9]
+    (
         out_ref,
         fresh_key_ref,
         fresh_value_ref,
-        terms_ref,
+        mixed_ref,
+        fresh_ref,
         query_ref,
-        key_ref,
-        value_ref,
         score_ref,
         weight_ref,
         new_weight_ref,
-    ) = refs[2:]
+        sems,
+    ) = refs[-10:]
     place, core, side = position()
-    odd = index_of(place) ^ flip_of(2 * side + core, core_of(place))
-    total = terms_ref.shape[2]
-    for k, term_ref in enumerate(term_refs):
-        scale = jnp.exp2(term_ref[:, total : total + 1])
-        terms_ref[odd ^ k] = term_ref[:, :total] * scale
+    g = index_of(place) ^ flip_of(2 * side + core, core_of(place)) ^ message
     requests = base_query_ref.shape[0]
-    kv_heads = keys_ref.shape[1]
     slots, head = keys_ref.shape[2], keys_ref.shape[3]
+    wide = base_query_ref.shape[1] // keys_ref.shape[1]
+    group = wide // head
     half = head // 2
-    heads = base_query_ref.shape[1] // head
-    group = heads // kv_heads
-    wide = group * head
+    total = term_ref.shape[1] - LANES
+    scale = jnp.exp2(term_ref[:, total : total + 1])
     cosine, sine = cosine_ref[...], sine_ref[...]
     cosine = jnp.concatenate([cosine, cosine], axis=1)
     sine = jnp.concatenate([-sine, sine], axis=1)
@@ -221,95 +206,122 @@
     def rotate(u):
         return (u * cosine + pltpu.roll(u, half, 1) * sine).astype(jnp.bfloat16)
 
-    for h in range(heads):
-        c = (h % group) * head
-        u = base_query_ref[:, h * head : (h + 1) * head].astype(jnp.float32)
-        u += terms_ref[h // group, :, c : c + head]
-        query_ref[pl.ds(h, requests, stride=heads), :] = rotate(u).astype(jnp.float32)
-    for g in range(kv_heads):
-        u = base_key_ref[:, g * head : (g + 1) * head].astype(jnp.float32)
-        key = rotate(u + terms_ref[g, :, wide : wide + head])
-        fresh_key_ref[:, g * head : (g + 1) * head] = key
-        key_ref[pl.ds(g, requests, stride=kv_heads), :] = key.astype(jnp.float32)
-        u = base_value_ref[:, g * head : (g + 1) * head].astype(jnp.float32)
-        value = (u + terms_ref[g, :, wide + head :]).astype(jnp.bfloat16)
-        fresh_value_ref[:, g * head : (g + 1) * head] = value
-        value_ref[pl.ds(g, requests, stride=kv_heads), :] = value.astype(jnp.float32)
+    def columns(width):
+        return pl.ds(pl.multiple_of(g * width, width), width)
+
+    base = base_query_ref[:, columns(wide)].astype(jnp.float32)
+    for h in range(group):
+        c = h * head
+        u = base[:, c : c + head] + term_ref[:, c : c + head] * scale
+        query_ref[pl.ds(h, requests, stride=group), :] = rotate(u).astype(jnp.float32)
+    u = base_key_ref[:, columns(head)].astype(jnp.float32)
+    new_key = rotate(u + term_ref[:, wide : wide + head] * scale)
+    u = base_value_ref[:, columns(head)].astype(jnp.float32)
+    new_value = (u + term_ref[:, wide + head : wide + 2 * head] * scale).astype(jnp.bfloat16)
+    fresh_ref[0] = new_key
+    fresh_ref[1] = new_value
+    fresh_copies = [
+        pltpu.make_async_copy(fresh_ref.at[i], ref.at[:, columns(head)], sems.at[i])
+        for i, ref in enumerate((fresh_key_ref, fresh_value_ref))
+    ]
+    for copy in fresh_copies:
+        copy.start()
+    new_key, new_value = new_key.astype(jnp.float32), new_value.astype(jnp.float32)
 
     inv_sqrt = 1.0 / math.sqrt(head)
-    for r in range(requests):
-        query = query_ref[r * heads : (r + 1) * heads, :].astype(jnp.bfloat16)
+    zero = jnp.zeros((group, head), jnp.float32)
+
+    def four(ref, r):
+        parts = [ref[(r + i) * group : (r + i + 1) * group, :] for i in range(4)]
+        return jnp.concatenate(
+            [
+                jnp.concatenate([parts[i], zero] if i % 2 == 0 else [zero, parts[i]], axis=1)
+                for i in range(4)
+            ],
+            axis=0,
+        ).astype(jnp.bfloat16)
+
+    for r in range(0, requests, 4):
+        keys = [keys_ref[r + i, g] for i in range(4)]
+        keys = jnp.concatenate(
+            [jnp.concatenate(keys[:2], axis=1), jnp.concatenate(keys[2:], axis=1)], axis=0
+        )
         scores = lax.dot_general(
-            query,
-            keys_ref[r].reshape(kv_heads * slots, head),
-            (((1,), (1,)), ((), ())),
-            preferred_element_type=jnp.float32,
-        )
-        for g in range(kv_heads):
-            score_ref[r * heads + g * group : r * heads + (g + 1) * group, :] = scores[
-                g * group : (g + 1) * group, g * slots : (g + 1) * slots
+            four(query_ref, r), keys, (((1,), (1,)), ((), ())), preferred_element_type=jnp.float32
+        )
+        for i in range(4):
+            score_ref[(r + i) * group : (r + i + 1) * group, :] = scores[
+                i * group : (i + 1) * group, (i // 2) * slots : (i // 2 + 1) * slots
             ]
     row = lax.broadcasted_iota(jnp.int32, (requests, requests), 0)
     lane = lax.broadcasted_iota(jnp.int32, (requests, requests), 1)
     limits = jnp.where(row == lane, lengths_ref[...].astype(jnp.float32), 0.0)
     limits = jnp.broadcast_to(jnp.sum(limits, axis=1, keepdims=True), (requests, slots))
-    slot = lax.broadcasted_iota(jnp.int32, (heads, slots), 1).astype(jnp.float32)
+    slot = lax.broadcasted_iota(jnp.int32, (group, slots), 1).astype(jnp.float32)
     for r in range(requests):
-        rows = slice(r * heads, (r + 1) * heads)
-        query = query_ref[rows, :]
-        new_key = jnp.concatenate(
-            [
-                jnp.broadcast_to(key_ref[r * kv_heads + g : r * kv_heads + g + 1, :], (group, head))
-                for g in range(kv_heads)
-            ],
-            axis=0,
-        )
-        new_score = jnp.sum(query * new_key, axis=1, keepdims=True) * inv_sqrt
-        scores = jnp.where(slot < limits[r : r + 1, :], score_ref[rows, :] * inv_sqrt, -jnp.inf)
+        rows = slice(r * group, (r + 1) * group)
+        new_score = (
+            jnp.sum(query_ref[rows, :] * new_key[r : r + 1], axis=1, keepdims=True) * inv_sqrt
+        )
+        scores = jnp.where(slot < limits[r : r + 1], score_ref[rows, :] * inv_sqrt, -jnp.inf)
         row_max = jnp.maximum(jnp.max(scores, axis=1, keepdims=True), new_score)
         weights = jnp.exp(scores - row_max)
         new_weight = jnp.exp(new_score - row_max)
         total = jnp.sum(weights, axis=1, keepdims=True) + new_weight
         weight_ref[rows, :] = weights / total
-        new_weight_ref[rows, :] = jnp.broadcast_to(new_weight / total, (heads, head))
-    for r in range(requests):
-        rows = slice(r * heads, (r + 1) * heads)
-        zero = jnp.zeros((group, slots), jnp.float32)
-        spread = jnp.concatenate(
-            [
-                jnp.concatenate(
-                    [
-                        weight_ref[r * heads + g * group : r * heads + (g + 1) * group, :]
-                        if o == g
-                        else zero
-                        for o in range(kv_heads)
-                    ],
-                    axis=1,
-                )
-                for g in range(kv_heads)
-            ],
-            axis=0,
-        ).astype(jnp.bfloat16)
-        mixed = jnp.dot(
-            spread,
-            values_ref[r].reshape(kv_heads * slots, head),
-            preferred_element_type=jnp.float32,
-        )
-        new_value = jnp.concatenate(
-            [
-                jnp.broadcast_to(
-                    value_ref[r * kv_heads + g : r * kv_heads + g + 1, :], (group, head)
-                )
-                for g in range(kv_heads)
-            ],
-            axis=0,
-        )
-        new_weight = new_weight_ref[rows, :].astype(jnp.bfloat16).astype(jnp.float32)
-        score_ref[rows, :] = mixed + new_weight * new_value
-    for h in range(heads):
-        out_ref[:, h * head : (h + 1) * head] = score_ref[
-            pl.ds(h, requests, stride=heads), :
+        new_weight_ref[rows, :] = jnp.broadcast_to(new_weight / total, (group, head))
+    for r in range(0, requests, 4):
+        values = [values_ref[r + i, g] for i in range(4)]
+        values = jnp.concatenate(
+            [jnp.concatenate([values[i], values[i + 2]], axis=1) for i in range(2)], axis=0
+        )
+        mixed = jnp.dot(four(weight_ref, r), values, preferred_element_type=jnp.float32)
+        for i in range(4):
+            rows = slice((r + i) * group, (r + i + 1) * group)
+            new_weight = new_weight_ref[rows, :].astype(jnp.bfloat16).astype(jnp.float32)
+            score_ref[rows, :] = (
+                mixed[i * group : (i + 1) * group, (i // 2) * head : (i // 2 + 1) * head]
+                + new_weight * new_value[r + i : r + i + 1]
+            )
+    for h in range(group):
+        mixed_ref[:, h * head : (h + 1) * head] = score_ref[
+            pl.ds(h, requests, stride=group), :
         ].astype(jnp.bfloat16)
+    copy = pltpu.make_async_copy(mixed_ref, out_ref.at[:, columns(wide)], sems.at[2])
+    copy.start()
+    for fresh_copy in fresh_copies:
+        fresh_copy.wait()
+    copy.wait()
+
+
+def attend(message, arrays, before):
+    base_queries, base_keys, base_values = arrays[1:4]
+    requests, head = base_queries.shape[0], arrays[-1].shape[3]
+    kv_heads = arrays[-1].shape[1]
+    wide = base_queries.shape[1] // kv_heads
+    rows = requests * wide // head
+    shapes = [
+        jax.ShapeDtypeStruct(a.shape, a.dtype) for a in (base_queries, base_keys, base_values)
+    ]
+    in_hbm = pl.BlockSpec(memory_space=pltpu.HBM)
+    return pl.pallas_call(
+        functools.partial(attend_kernel, message),
+        out_shape=shapes,
+        in_specs=[in_vmem()] * len(arrays) + [in_hbm] * len(before),
+        out_specs=[in_hbm] * 3,
+        input_output_aliases={len(arrays) + i: i for i in range(len(before))},
+        scratch_shapes=[
+            pltpu.VMEM((requests, wide), jnp.bfloat16),
+            pltpu.VMEM((2, requests, head), jnp.bfloat16),
+            pltpu.VMEM((rows, head), jnp.float32),
+            pltpu.VMEM((rows, head), jnp.float32),
+            pltpu.VMEM((rows, head), jnp.float32),
+            pltpu.VMEM((rows, head), jnp.float32),
+            pltpu.SemaphoreType.DMA((3,)),
+        ],
+        compiler_params=pltpu.CompilerParams(vmem_limit_bytes=VMEM_BYTES),
+        name="attend",
+    )(*arrays, *before)
 
 
 def load_kernel(*refs):
@@ -452,37 +464,21 @@
         for k, term in enumerate(terms)
     ]
     cosine, sine = rotation_factors(lengths, head)
-    return tuple(
-        call(
-            attend_kernel,
-            "attend",
-            [
-                jax.ShapeDtypeStruct(base_queries.shape, bf16),
-                jax.ShapeDtypeStruct(base_keys.shape, bf16),
-                jax.ShapeDtypeStruct(base_values.shape, bf16),
-            ],
-            [
-                pltpu.VMEM((2, requests, width), f32),
-                pltpu.VMEM((requests * heads, head), f32),
-                pltpu.VMEM((requests * kv_heads, head), f32),
-                pltpu.VMEM((requests * kv_heads, head), f32),
-                pltpu.VMEM((requests * heads, head), f32),
-                pltpu.VMEM((requests * heads, head), f32),
-                pltpu.VMEM((requests * heads, head), f32),
-            ],
-            [
-                *arrived,
-                base_queries,
-                base_keys,
-                base_values,
-                lengths[None, :],
-                cosine,
-                sine,
-                cached_keys,
-                cached_values,
-            ],
-        )
-    )
+    outs = []
+    for k, term in enumerate(arrived):
+        arrays = [
+            term,
+            base_queries,
+            base_keys,
+            base_values,
+            lengths[None, :],
+            cosine,
+            sine,
+            cached_keys,
+            cached_values,
+        ]
+        outs = attend(k, arrays, outs)
+    return tuple(outs)
 
 
 def rotate_pairs(vectors, positions):

time: 42.3 us -> 41.9 us (level)
  waiting for transfers between devices: 20.3 us -> 18.8 us
  Pallas kernels: 8.71 us -> 9.79 us
    pallas_call x0 -> x2, Pallas kernels: none -> 3 us  [attend(): pl.pallas_call(functools.partial(attend_kernel, message), out_shape=shape...]
    pallas_call x3 -> x2, Pallas kernels: 4.03 us -> 2.1 us  [call(): pl.pallas_call(kernel, out_shape=out_shape, in_specs=[in_vmem()] * len(ar...]
    ppermute x2, waiting for transfers between devices: 6.27 us -> 4.76 us  [few_body(): lax.ppermute(term.astype(jnp.float16), ('adapter', 'tensor'), sent[k])]
  transfers between devices with their start and end apart: 13 -> 13, of which waited for: 9 -> 9; matrix products, arithmetic and copies ran while one was open for 0% -> 0% of each run, Pallas kernels for 14% -> 17%
where the time goes in v4:
time: 41.9 us; the launch traced here: 41.7 us
  waiting for transfers between devices  18.8 us (45%)
  starting transfers between devices  12.1 us (29%)
  Pallas kernels  9.79 us (23%)
  between operations  0.77 us (2%)
    ppermute x11, waiting for transfers between devices, step(): return lax.ppermute(value, axis, [(i, i ^ k) for i in range(size)])  14 us
    ppermute x11, starting transfers between devices, step(): return lax.ppermute(value, axis, [(i, i ^ k) for i in range(size)])  8.46 us
    ppermute x2, waiting for transfers between devices, few_body(): lax.ppermute(term.astype(jnp.float16), ('adapter', 'tensor'), sent[k])  4.76 us
    pallas_call x1, Pallas kernels, load(): pl.pallas_call(load_kernel, out_shape=[pltpu.VMEM(a.shape, a.dtype) for a...  3.76 us
    ppermute x2, starting transfers between devices, few_body(): lax.ppermute(term.astype(jnp.float16), ('adapter', 'tensor'), sent[k])  3.67 us
    pallas_call x2, Pallas kernels, attend(): pl.pallas_call(functools.partial(attend_kernel, message), out_shape=shape...  3 us
    pallas_call x2, Pallas kernels, call(): pl.pallas_call(kernel, out_shape=out_shape, in_specs=[in_vmem()] * len(ar...  2.1 us
    pallas_call x1, Pallas kernels, pack(): pl.pallas_call(pack_kernel, out_shape=pltpu.VMEM((requests, width + LANES...  0.92 us
  transfers between devices with their start and end apart: 13, of which 9 were waited for; matrix products, arithmetic and copies ran while one was open for 0% of the time, Pallas kernels for 17%

profile of v4, /device:TPU:20, one launch (start us, length us, event | category | flops | bytes accessed | tf_op | source)
XLA Modules:
  0.0 41.7 jit_solution(13691992769926711467)
XLA Ops:
  0.7 0.9 %pack.1.refs_0_ = bf16[32,2176]{1,0:T(8,128)(2,1)S(1)} custom-call(s32[32]{0:T(128)} %ids_in.1, bf16[32,2048]{1,0:T(8,128)(2,1)} %hidden_in.1), custom_call_target="tpu_custom_call" | custom-call | tf_op jit(solution)/shard_map/pack/pallas_call | solution.py:69
  1.6 0.5 %collective-permute-start = (bf16[32,2176]{1,0:T(8,128)(2,1)S(1)}, bf16[32,2176]{1,0:T(8,128)(2,1)S(1)}, u32[]{:S(2)}, u32[]{:S(2)}) collective-permute-start(bf16[32,2176]{1,0:T(8,128)(2,1)S(1)} %pack.1.refs_0_), channel_id=1, source_target_pairs={{0,12},{4,8},{8,4},{12,0},{1,13},{5,9},{9,5},{13,1},{2,14},{6,10},... | collective-permute-start | bytes 417800 | tf_op jit(solution)/shard_map/ppermute | solution.py:371
  2.2 1.3 %collective-permute-start.2 = (bf16[32,2176]{1,0:T(8,128)(2,1)S(1)}, bf16[32,2176]{1,0:T(8,128)(2,1)S(1)}, u32[]{:S(2)}, u32[]{:S(2)}) collective-permute-start(bf16[32,2176]{1,0:T(8,128)(2,1)S(1)} %pack.1.refs_0_), channel_id=1, source_target_pairs={{0,4},{4,0},{8,12},{12,8},{1,5},{5,1},{9,13},{13,9},{2,6},{6,2},{1... | collective-permute-start | bytes 417800 | tf_op jit(solution)/shard_map/ppermute | solution.py:371
  3.5 7.3 %collective-permute-done.refs_1_ = bf16[32,2176]{1,0:T(8,128)(2,1)S(1)} collective-permute-done((bf16[32,2176]{1,0:T(8,128)(2,1)S(1)}, bf16[32,2176]{1,0:T(8,128)(2,1)S(1)}, u32[]{:S(2)}, u32[]{:S(2)}) %collective-permute-start) | collective-permute-done | bytes 139296 | tf_op jit(solution)/shard_map/ppermute | solution.py:371
  10.8 0.8 %collective-permute-start.1 = (bf16[32,2176]{1,0:T(8,128)(2,1)S(1)}, bf16[32,2176]{1,0:T(8,128)(2,1)S(1)}, u32[]{:S(2)}, u32[]{:S(2)}) collective-permute-start(bf16[32,2176]{1,0:T(8,128)(2,1)S(1)} %collective-permute-done.refs_1_), channel_id=1, source_target_pairs={{0,4},{4,0},{8,12},{12,8},{1,5},{5,1},{9,13},{13,9},{2,6},{6,2},{1... | collective-permute-start | bytes 417800 | tf_op jit(solution)/shard_map/ppermute | solution.py:371
  11.6 3.8 %load.1 = (bf16[8,96,2048]{2,1,0:T(8,128)(2,1)S(1)}, bf16[32,32,512]{2,1,0:T(8,128)(2,1)S(1)}, bf16[32,2,32,64]{3,2,1,0:T(8,128)(2,1)S(1)}, bf16[32,2048]{1,0:T(...) custom-call(bf16[8,96,2048]{2,1,0:T(8,128)(2,1)} %refs_0_.1, ...), custom_call_target="tpu_custom_call" | custom-call | bytes 17629184 | tf_op jit(solution)/shard_map/load/pallas_call | solution.py:340
  15.4 0.6 %collective-permute-done.1.refs_2_ = bf16[32,2176]{1,0:T(8,128)(2,1)S(1)} collective-permute-done((bf16[32,2176]{1,0:T(8,128)(2,1)S(1)}, bf16[32,2176]{1,0:T(8,128)(2,1)S(1)}, u32[]{:S(2)}, u32[]{:S(2)}) %collective-permute-start.1) | collective-permute-done | bytes 139296 | tf_op jit(solution)/shard_map/ppermute | solution.py:371
  16.0 1.0 %down.1 = (f32[96,128]{1,0:T(8,128)S(1)}, f32[128,128]{1,0:T(8,128)S(1)}) custom-call(bf16[32,2176]{1,0:T(8,128)(2,1)S(1)} %pack.1.refs_0_, bf16[32,2176]{1,0:T(8,128)(2,1)S(1)} %collective-permute-done.refs_1_, bf16[32,2176]{1,0:T(8,128)(2,1)S(1)} %collective-permute-done.1.refs_2_, bf16[32,2176]{1,0:T(8,128)(2,1)S(1)} %collective-permute-done.2.refs_3_, ...), custom_call_target="tpu_custom_call" | custom-call | tf_op jit(solution)/shard_map/down/pallas_call | solution.py:359
  17.2 1.6 %collective-permute-start.4 = (f32[96,128]{1,0:T(8,128)S(1)}, f32[96,128]{1,0:T(8,128)S(1)}, u32[]{:S(2)}, u32[]{:S(2)}) collective-permute-start(f32[96,128]{1,0:T(8,128)S(1)} %get-tuple-element.20), channel_id=1, source_target_pairs={{0,2},{1,3},{2,0},{3,1},{4,6},{5,7},{6,4},{7,5},{8,10},{9,11},{10,... | collective-permute-start | bytes 147464 | tf_op jit(solution)/shard_map/ppermute | solution.py:371
  19.2 1.9 %collective-permute-done.3 = f32[96,128]{1,0:T(8,128)S(1)} collective-permute-done((f32[96,128]{1,0:T(8,128)S(1)}, f32[96,128]{1,0:T(8,128)S(1)}, u32[]{:S(2)}, u32[]{:S(2)}) %collective-permute-start.3) | collective-permute-done | bytes 49184 | tf_op jit(solution)/shard_map/ppermute | solution.py:371
  21.1 0.9 %collective-permute-done.4 = f32[96,128]{1,0:T(8,128)S(1)} collective-permute-done((f32[96,128]{1,0:T(8,128)S(1)}, f32[96,128]{1,0:T(8,128)S(1)}, u32[]{:S(2)}, u32[]{:S(2)}) %collective-permute-start.4) | collective-permute-done | bytes 49184 | tf_op jit(solution)/shard_map/ppermute | solution.py:371
  22.1 0.5 %collective-permute-start.6 = (bf16[96,128]{1,0:T(8,128)(2,1)S(1)}, bf16[96,128]{1,0:T(8,128)(2,1)S(1)}, u32[]{:S(2)}, u32[]{:S(2)}) collective-permute-start(bf16[96,128]{1,0:T(8,128)(2,1)S(1)} %add_convert_fusion.refs_0_), channel_id=1, source_target_pairs={{0,12},{4,8},{8,4},{12,0},{1,13},{5,9},{9,5},{13,1},{2,14},{6,10},... | collective-permute-start | bytes 73736 | tf_op jit(solution)/shard_map/ppermute | solution.py:371
  22.6 2.5 %collective-permute-start.7 = (bf16[96,128]{1,0:T(8,128)(2,1)S(1)}, bf16[96,128]{1,0:T(8,128)(2,1)S(1)}, u32[]{:S(2)}, u32[]{:S(2)}) collective-permute-start(bf16[96,128]{1,0:T(8,128)(2,1)S(1)} %add_convert_fusion.refs_0_), channel_id=1, source_target_pairs={{0,8},{4,12},{8,0},{12,4},{1,9},{5,13},{9,1},{13,5},{2,10},{6,14},... | collective-permute-start | bytes 73736 | tf_op jit(solution)/shard_map/ppermute | solution.py:371
  25.1 0.5 %collective-permute-start.8 = (bf16[96,128]{1,0:T(8,128)(2,1)S(1)}, bf16[96,128]{1,0:T(8,128)(2,1)S(1)}, u32[]{:S(2)}, u32[]{:S(2)}) collective-permute-start(bf16[96,128]{1,0:T(8,128)(2,1)S(1)} %add_convert_fusion.refs_0_), channel_id=1, source_target_pairs={{0,4},{4,0},{8,12},{12,8},{1,5},{5,1},{9,13},{13,9},{2,6},{6,2},{1... | collective-permute-start | bytes 73736 | tf_op jit(solution)/shard_map/ppermute | solution.py:371
  25.7 0.9 %collective-permute-done.6.refs_1_ = bf16[96,128]{1,0:T(8,128)(2,1)S(1)} collective-permute-done((bf16[96,128]{1,0:T(8,128)(2,1)S(1)}, bf16[96,128]{1,0:T(8,128)(2,1)S(1)}, u32[]{:S(2)}, u32[]{:S(2)}) %collective-permute-start.6) | collective-permute-done | bytes 24608 | tf_op jit(solution)/shard_map/ppermute | solution.py:371
  26.6 0.9 %collective-permute-done.7.refs_2_ = bf16[96,128]{1,0:T(8,128)(2,1)S(1)} collective-permute-done((bf16[96,128]{1,0:T(8,128)(2,1)S(1)}, bf16[96,128]{1,0:T(8,128)(2,1)S(1)}, u32[]{:S(2)}, u32[]{:S(2)}) %collective-permute-start.7) | collective-permute-done | bytes 24608 | tf_op jit(solution)/shard_map/ppermute | solution.py:371
  27.4 1.5 %collective-permute-done.8.refs_3_ = bf16[96,128]{1,0:T(8,128)(2,1)S(1)} collective-permute-done((bf16[96,128]{1,0:T(8,128)(2,1)S(1)}, bf16[96,128]{1,0:T(8,128)(2,1)S(1)}, u32[]{:S(2)}, u32[]{:S(2)}) %collective-permute-start.8) | collective-permute-done | bytes 24608 | tf_op jit(solution)/shard_map/ppermute | solution.py:371
  29.0 1.1 %up.1 = (f32[32,1408]{1,0:T(8,128)S(1)}, f32[32,1408]{1,0:T(8,128)S(1)}) custom-call(f32[128,128]{1,0:T(8,128)S(1)} %get-tuple-element.19.ids_ref, bf16[96,128]{1,0:T(8,128)(2,1)S(1)} %add_convert_fusion.refs_0_, bf16[96,128]{1,0:T(8,128)(2,1)S(1)} %collective-permute-done.6.refs_1_, bf16[96,128]{1,0:T(8,128)(2,1)S(1)} %collective-permute-done.7.refs_2_, ...), custom_call_target="tpu_custom_call" | custom-call | tf_op jit(solution)/shard_map/up/pallas_call | solution.py:359
  30.1 1.7 %collective-permute-start.12 = (f16[32,1408]{1,0:T(8,128)(2,1)S(1)}, f16[32,1408]{1,0:T(8,128)(2,1)S(1)}, u32[]{:S(2)}, u32[]{:S(2)}) collective-permute-start(f16[32,1408]{1,0:T(8,128)(2,1)S(1)} %convert_element_type.22), channel_id=1, source_target_pairs={{0,12},{1,8},{2,0},{3,4},{4,13},{5,9},{6,1},{7,5},{8,2},{9,6},{10,... | collective-permute-start | bytes 270344 | tf_op jit(solution)/shard_map/ppermute | solution.py:463
  31.8 1.9 %collective-permute-start.11 = (f16[32,1408]{1,0:T(8,128)(2,1)S(1)}, f16[32,1408]{1,0:T(8,128)(2,1)S(1)}, u32[]{:S(2)}, u32[]{:S(2)}) collective-permute-start(f16[32,1408]{1,0:T(8,128)(2,1)S(1)} %convert_element_type.19), channel_id=1, source_target_pairs={{0,0},{1,4},{2,12},{3,8},{4,1},{5,5},{6,13},{7,9},{8,14},{9,10},{1... | collective-permute-start | bytes 270344 | tf_op jit(solution)/shard_map/ppermute | solution.py:463
  33.9 1.6 %collective-permute-done.12 = f16[32,1408]{1,0:T(8,128)(2,1)S(1)} collective-permute-done((f16[32,1408]{1,0:T(8,128)(2,1)S(1)}, f16[32,1408]{1,0:T(8,128)(2,1)S(1)}, u32[]{:S(2)}, u32[]{:S(2)}) %collective-permute-start.12) | collective-permute-done | bytes 90144 | tf_op jit(solution)/shard_map/ppermute | solution.py:463
  35.5 1.5 %attend.2 = (bf16[32,2048]{1,0:T(8,128)(2,1)}, bf16[32,256]{1,0:T(8,128)(2,1)}, bf16[32,256]{1,0:T(8,128)(2,1)}) custom-call(f32[32,1408]{1,0:T(8,128)S(1)} %convert_element_type.23.refs_0_, bf16[32,2048]{1,0:T(8,128)(2,1)S(1)} %get-tuple-element.24.refs_1_, bf16[32,256]{1,0:T(8,128)(2,1)S(1)} %get-tuple-element.25.refs_2_, ...), custom_call_target="tpu_custom_call" | custom-call | tf_op jit(solution)/shard_map/attend/pallas_call | solution.py:307
  37.0 3.2 %collective-permute-done.11 = f16[32,1408]{1,0:T(8,128)(2,1)S(1)} collective-permute-done((f16[32,1408]{1,0:T(8,128)(2,1)S(1)}, f16[32,1408]{1,0:T(8,128)(2,1)S(1)}, u32[]{:S(2)}, u32[]{:S(2)}) %collective-permute-start.11) | collective-permute-done | bytes 90144 | tf_op jit(solution)/shard_map/ppermute | solution.py:463
  40.2 1.5 %attend.3 = (bf16[32,2048]{1,0:T(8,128)(2,1)}, bf16[32,256]{1,0:T(8,128)(2,1)}, bf16[32,256]{1,0:T(8,128)(2,1)}) custom-call(f32[32,1408]{1,0:T(8,128)S(1)} %convert_element_type.20.refs_0_, bf16[32,2048]{1,0:T(8,128)(2,1)S(1)} %get-tuple-element.24.refs_1_, ...), custom_call_target="tpu_custom_call", output_to_operand_aliasing={{0}: (9, {}), {1}: (10, {}), {2}: (11, {})} | custom-call | tf_op jit(solution)/shard_map/attend/pallas_call | solution.py:307
  (20 shorter events, 0.9 us)
Async XLA Ops:
  0.6 28.3 %collective-permute-start.9 = (bf16[32,32,512]{2,1,0:T(8,128)(2,1)}, bf16[32,32,512]{2,1,0:T(8,128)(2,1)S(1)}, u32[]{:S(2)}, u32[]{:S(2)}) collective-permute-start(bf16[32,32,512]{2,1,0:T(8,128)(2,1)} %refs_1_.1), channel_id=1, source_target_pairs={{0,1},{1,0},{2,3},{3,2},{4,5},{5,4},{6,7},{7,6},{8,9},{9,8},{10,11... | collective-permute-start | bytes 3145736 | tf_op jit(solution)/shard_map/ppermute | solution.py:371
  1.6 9.1 %collective-permute-start = (bf16[32,2176]{1,0:T(8,128)(2,1)S(1)}, bf16[32,2176]{1,0:T(8,128)(2,1)S(1)}, u32[]{:S(2)}, u32[]{:S(2)}) collective-permute-start(bf16[32,2176]{1,0:T(8,128)(2,1)S(1)} %pack.1.refs_0_), channel_id=1, source_target_pairs={{0,12},{4,8},{8,4},{12,0},{1,13},{5,9},{9,5},{13,1},{2,14},{6,10},... | collective-permute-start | bytes 417800 | tf_op jit(solution)/shard_map/ppermute | solution.py:371
  2.2 13.2 %collective-permute-start.2 = (bf16[32,2176]{1,0:T(8,128)(2,1)S(1)}, bf16[32,2176]{1,0:T(8,128)(2,1)S(1)}, u32[]{:S(2)}, u32[]{:S(2)}) collective-permute-start(bf16[32,2176]{1,0:T(8,128)(2,1)S(1)} %pack.1.refs_0_), channel_id=1, source_target_pairs={{0,4},{4,0},{8,12},{12,8},{1,5},{5,1},{9,13},{13,9},{2,6},{6,2},{1... | collective-permute-start | bytes 417800 | tf_op jit(solution)/shard_map/ppermute | solution.py:371
  10.8 5.3 %collective-permute-start.1 = (bf16[32,2176]{1,0:T(8,128)(2,1)S(1)}, bf16[32,2176]{1,0:T(8,128)(2,1)S(1)}, u32[]{:S(2)}, u32[]{:S(2)}) collective-permute-start(bf16[32,2176]{1,0:T(8,128)(2,1)S(1)} %collective-permute-done.refs_1_), channel_id=1, source_target_pairs={{0,4},{4,0},{8,12},{12,8},{1,5},{5,1},{9,13},{13,9},{2,6},{6,2},{1... | collective-permute-start | bytes 417800 | tf_op jit(solution)/shard_map/ppermute | solution.py:371
  15.4 3.6 %copy-start.1 = (bf16[32,2,32,64]{3,2,1,0:T(8,128)(2,1)S(1)}, bf16[32,2,32,64]{3,2,1,0:T(8,128)(2,1)}, u32[]{:S(2)}) copy-start(bf16[32,2,32,64]{3,2,1,0:T(8,128)(2,1)} %refs_2_.1) | copy-start | bytes 786436
  15.4 10.3 %copy-start = (s32[32]{0:T(128)S(1)}, s32[32]{0:T(128)}, u32[]{:S(2)}) copy-start(s32[32]{0:T(128)} %param.21) | copy-start | bytes 388
  17.1 4.1 %collective-permute-start.3 = (f32[96,128]{1,0:T(8,128)S(1)}, f32[96,128]{1,0:T(8,128)S(1)}, u32[]{:S(2)}, u32[]{:S(2)}) collective-permute-start(f32[96,128]{1,0:T(8,128)S(1)} %get-tuple-element.20), channel_id=1, source_target_pairs={{0,3},{1,2},{2,1},{3,0},{4,7},{5,6},{6,5},{7,4},{8,11},{9,10},{10,... | collective-permute-start | bytes 147464 | tf_op jit(solution)/shard_map/ppermute | solution.py:371
  17.2 4.9 %collective-permute-start.4 = (f32[96,128]{1,0:T(8,128)S(1)}, f32[96,128]{1,0:T(8,128)S(1)}, u32[]{:S(2)}, u32[]{:S(2)}) collective-permute-start(f32[96,128]{1,0:T(8,128)S(1)} %get-tuple-element.20), channel_id=1, source_target_pairs={{0,2},{1,3},{2,0},{3,1},{4,6},{5,7},{6,4},{7,5},{8,10},{9,11},{10,... | collective-permute-start | bytes 147464 | tf_op jit(solution)/shard_map/ppermute | solution.py:371
  18.7 3.3 %collective-permute-start.5 = (f32[96,128]{1,0:T(8,128)S(1)}, f32[96,128]{1,0:T(8,128)S(1)}, u32[]{:S(2)}, u32[]{:S(2)}) collective-permute-start(f32[96,128]{1,0:T(8,128)S(1)} %get-tuple-element.20), channel_id=1, source_target_pairs={{0,1},{1,0},{2,3},{3,2},{4,5},{5,4},{6,7},{7,6},{8,9},{9,8},{10,11... | collective-permute-start | bytes 147464 | tf_op jit(solution)/shard_map/ppermute | solution.py:371
  19.0 6.7 %collective-permute-start.10 = (bf16[32,2,32,64]{3,2,1,0:T(8,128)(2,1)S(1)}, bf16[32,2,32,64]{3,2,1,0:T(8,128)(2,1)S(1)}, u32[]{:S(2)}, u32[]{:S(2)}) collective-permute-start(bf16[32,2,32,64]{3,2,1,0:T(8,128)(2,1)S(1)} %copy-done.1), channel_id=1, source_target_pairs={{0,1},{1,0},{2,3},{3,2},{4,5},{5,4},{6,7},{7,6},{8,9},{9,8},{10,11... | collective-permute-start | bytes 786440 | tf_op jit(solution)/shard_map/ppermute | solution.py:371
  22.1 4.5 %collective-permute-start.6 = (bf16[96,128]{1,0:T(8,128)(2,1)S(1)}, bf16[96,128]{1,0:T(8,128)(2,1)S(1)}, u32[]{:S(2)}, u32[]{:S(2)}) collective-permute-start(bf16[96,128]{1,0:T(8,128)(2,1)S(1)} %add_convert_fusion.refs_0_), channel_id=1, source_target_pairs={{0,12},{4,8},{8,4},{12,0},{1,13},{5,9},{9,5},{13,1},{2,14},{6,10},... | collective-permute-start | bytes 73736 | tf_op jit(solution)/shard_map/ppermute | solution.py:371
  22.6 4.8 %collective-permute-start.7 = (bf16[96,128]{1,0:T(8,128)(2,1)S(1)}, bf16[96,128]{1,0:T(8,128)(2,1)S(1)}, u32[]{:S(2)}, u32[]{:S(2)}) collective-permute-start(bf16[96,128]{1,0:T(8,128)(2,1)S(1)} %add_convert_fusion.refs_0_), channel_id=1, source_target_pairs={{0,8},{4,12},{8,0},{12,4},{1,9},{5,13},{9,1},{13,5},{2,10},{6,14},... | collective-permute-start | bytes 73736 | tf_op jit(solution)/shard_map/ppermute | solution.py:371
  25.1 3.8 %collective-permute-start.8 = (bf16[96,128]{1,0:T(8,128)(2,1)S(1)}, bf16[96,128]{1,0:T(8,128)(2,1)S(1)}, u32[]{:S(2)}, u32[]{:S(2)}) collective-permute-start(bf16[96,128]{1,0:T(8,128)(2,1)S(1)} %add_convert_fusion.refs_0_), channel_id=1, source_target_pairs={{0,4},{4,0},{8,12},{12,8},{1,5},{5,1},{9,13},{13,9},{2,6},{6,2},{1... | collective-permute-start | bytes 73736 | tf_op jit(solution)/shard_map/ppermute | solution.py:371
  30.1 5.4 %collective-permute-start.12 = (f16[32,1408]{1,0:T(8,128)(2,1)S(1)}, f16[32,1408]{1,0:T(8,128)(2,1)S(1)}, u32[]{:S(2)}, u32[]{:S(2)}) collective-permute-start(f16[32,1408]{1,0:T(8,128)(2,1)S(1)} %convert_element_type.22), channel_id=1, source_target_pairs={{0,12},{1,8},{2,0},{3,4},{4,13},{5,9},{6,1},{7,5},{8,2},{9,6},{10,... | collective-permute-start | bytes 270344 | tf_op jit(solution)/shard_map/ppermute | solution.py:463
  31.8 8.4 %collective-permute-start.11 = (f16[32,1408]{1,0:T(8,128)(2,1)S(1)}, f16[32,1408]{1,0:T(8,128)(2,1)S(1)}, u32[]{:S(2)}, u32[]{:S(2)}) collective-permute-start(f16[32,1408]{1,0:T(8,128)(2,1)S(1)} %convert_element_type.19), channel_id=1, source_target_pairs={{0,0},{1,4},{2,12},{3,8},{4,1},{5,5},{6,13},{7,9},{8,14},{9,10},{1... | collective-permute-start | bytes 270344 | tf_op jit(solution)/shard_map/ppermute | solution.py:463

commit v5 on v4

--- a/solution.py
+++ b/solution.py
@@ -25,7 +25,11 @@
     return jnp.cos(angles), jnp.sin(angles)
 
 
-FLIPS = 0b1111
+ORDER = (((2, 3), (1, 0)), ((1, 2), (3, 0)), ((0, 1), (2, 3)), ((1, 3), (2, 0)))
+PLANES = [
+    sum(ORDER[a][c][i] << (4 * a + 2 * i) for a in range(4) for i in range(2)) for c in range(2)
+]
+INDEX = sum(i << (4 * a + ORDER[a][c][i]) for a in range(4) for c in range(2) for i in range(2))
 
 
 def position():
@@ -33,20 +37,13 @@
     return lax.axis_index("adapter"), column % 2, column // 2
 
 
-def plane_of(core, index):
-    return (3 * index) ^ core
-
-
-def core_of(plane):
-    return (plane ^ (plane >> 1)) & 1
-
-
-def index_of(plane):
-    return plane >> 1
-
-
-def flip_of(plane, core):
-    return (FLIPS >> (2 * plane + core)) & 1
+def plane_of(place, core, index):
+    both = jnp.where(core == 0, PLANES[0], PLANES[1])
+    return (both >> (4 * place + 2 * index)) & 3
+
+
+def index_of(plane, place):
+    return (INDEX >> (4 * plane + place)) & 1
 
 
 def pack_kernel(ids_in, hidden_in, out_ref, ids_ref, sems):
@@ -107,7 +104,6 @@
     shrink_refs, query_refs, kv_refs = refs[:4], refs[4:6], refs[6:8]
     *out_refs, rows_ref, terms_ref = refs[8:]
     place, core, side = position()
-    side ^= flip_of(place, core)
     shrink = shrink_refs[0][...].astype(jnp.float32)
     for ref in shrink_refs[1:]:
         shrink += ref[...].astype(jnp.float32)
@@ -117,7 +113,7 @@
     rows_ref[...] = jnp.transpose(shrink)
     rows = every // 2
     block = out_refs[0].shape[0]
-    starts = [pl.multiple_of(plane_of(core, i) * block, block) for i in range(2)]
+    starts = [pl.multiple_of(plane_of(place, core, i) * block, block) for i in range(2)]
     shrink = jnp.concatenate([rows_ref[pl.ds(start, block), :] for start in starts], axis=0)
     ids = jnp.concatenate([ids_ref[pl.ds(start, block), :] for start in starts], axis=0)
     lane = lax.broadcasted_iota(jnp.int32, (rows, LANES), 1)
@@ -191,7 +187,7 @@
         sems,
     ) = refs[-10:]
     place, core, side = position()
-    g = index_of(place) ^ flip_of(2 * side + core, core_of(place)) ^ message
+    g = index_of(2 * side + core, place) ^ message
     requests = base_query_ref.shape[0]
     slots, head = keys_ref.shape[2], keys_ref.shape[3]
     wide = base_query_ref.shape[1] // keys_ref.shape[1]
@@ -403,10 +399,7 @@
     everyone = [message, mirror, step(mirror, "adapter", planes, 1), near]
     sent = [
         [
-            (
-                a * columns + t,
-                plane_of(t % 2, (t // 2) ^ k ^ flip_of(a, t % 2)) * columns + a,
-            )
+            (a * columns + t, ORDER[a][t % 2][(t // 2) ^ k] * columns + a)
             for a in range(planes)
             for t in range(columns)
         ]

time: 41.9 us -> 40.1 us (0.957)
  starting transfers between devices: 12.1 us -> 10.3 us
    ppermute x2, starting transfers between devices: 3.67 us -> 1.83 us  [few_body(): lax.ppermute(term.astype(jnp.float16), ('adapter', 'tensor'), sent[k])]
  transfers between devices with their start and end apart: 13 -> 13, of which waited for: 9 -> 9; matrix products, arithmetic and copies ran while one was open for 0% -> 0% of each run, Pallas kernels for 17% -> 18%
where the time goes in v5:
time: 40.1 us; the launch traced here: 39.7 us
  waiting for transfers between devices  18.7 us (47%)
  starting transfers between devices  10.3 us (26%)
  Pallas kernels  9.77 us (24%)
  between operations  0.77 us (2%)
    ppermute x11, waiting for transfers between devices, step(): return lax.ppermute(value, axis, [(i, i ^ k) for i in range(size)])  14 us
    ppermute x11, starting transfers between devices, step(): return lax.ppermute(value, axis, [(i, i ^ k) for i in range(size)])  8.46 us
    ppermute x2, waiting for transfers between devices, few_body(): lax.ppermute(term.astype(jnp.float16), ('adapter', 'tensor'), sent[k])  4.64 us
    pallas_call x1, Pallas kernels, load(): pl.pallas_call(load_kernel, out_shape=[pltpu.VMEM(a.shape, a.dtype) for a...  3.76 us
    pallas_call x2, Pallas kernels, attend(): pl.pallas_call(functools.partial(attend_kernel, message), out_shape=shape...  3 us
    pallas_call x2, Pallas kernels, call(): pl.pallas_call(kernel, out_shape=out_shape, in_specs=[in_vmem()] * len(ar...  2.09 us
    ppermute x2, starting transfers between devices, few_body(): lax.ppermute(term.astype(jnp.float16), ('adapter', 'tensor'), sent[k])  1.83 us
    pallas_call x1, Pallas kernels, pack(): pl.pallas_call(pack_kernel, out_shape=pltpu.VMEM((requests, width + LANES...  0.92 us
  transfers between devices with their start and end apart: 13, of which 9 were waited for; matrix products, arithmetic and copies ran while one was open for 0% of the time, Pallas kernels for 18%

profile of v5, /device:TPU:20, one launch (start us, length us, event | category | flops | bytes accessed | tf_op | source)
XLA Modules:
  0.0 39.7 jit_solution(4328692154223249070)
XLA Ops:
  0.7 0.9 %pack.1.refs_0_ = bf16[32,2176]{1,0:T(8,128)(2,1)S(1)} custom-call(s32[32]{0:T(128)} %ids_in.1, bf16[32,2048]{1,0:T(8,128)(2,1)} %hidden_in.1), custom_call_target="tpu_custom_call" | custom-call | tf_op jit(solution)/shard_map/pack/pallas_call | solution.py:66
  1.6 0.5 %collective-permute-start = (bf16[32,2176]{1,0:T(8,128)(2,1)S(1)}, bf16[32,2176]{1,0:T(8,128)(2,1)S(1)}, u32[]{:S(2)}, u32[]{:S(2)}) collective-permute-start(bf16[32,2176]{1,0:T(8,128)(2,1)S(1)} %pack.1.refs_0_), channel_id=1, source_target_pairs={{0,12},{4,8},{8,4},{12,0},{1,13},{5,9},{9,5},{13,1},{2,14},{6,10},... | collective-permute-start | bytes 417800 | tf_op jit(solution)/shard_map/ppermute | solution.py:367
  2.2 1.3 %collective-permute-start.2 = (bf16[32,2176]{1,0:T(8,128)(2,1)S(1)}, bf16[32,2176]{1,0:T(8,128)(2,1)S(1)}, u32[]{:S(2)}, u32[]{:S(2)}) collective-permute-start(bf16[32,2176]{1,0:T(8,128)(2,1)S(1)} %pack.1.refs_0_), channel_id=1, source_target_pairs={{0,4},{4,0},{8,12},{12,8},{1,5},{5,1},{9,13},{13,9},{2,6},{6,2},{1... | collective-permute-start | bytes 417800 | tf_op jit(solution)/shard_map/ppermute | solution.py:367
  3.5 7.3 %collective-permute-done.refs_1_ = bf16[32,2176]{1,0:T(8,128)(2,1)S(1)} collective-permute-done((bf16[32,2176]{1,0:T(8,128)(2,1)S(1)}, bf16[32,2176]{1,0:T(8,128)(2,1)S(1)}, u32[]{:S(2)}, u32[]{:S(2)}) %collective-permute-start) | collective-permute-done | bytes 139296 | tf_op jit(solution)/shard_map/ppermute | solution.py:367
  10.8 0.8 %collective-permute-start.1 = (bf16[32,2176]{1,0:T(8,128)(2,1)S(1)}, bf16[32,2176]{1,0:T(8,128)(2,1)S(1)}, u32[]{:S(2)}, u32[]{:S(2)}) collective-permute-start(bf16[32,2176]{1,0:T(8,128)(2,1)S(1)} %collective-permute-done.refs_1_), channel_id=1, source_target_pairs={{0,4},{4,0},{8,12},{12,8},{1,5},{5,1},{9,13},{13,9},{2,6},{6,2},{1... | collective-permute-start | bytes 417800 | tf_op jit(solution)/shard_map/ppermute | solution.py:367
  11.6 3.8 %load.1 = (bf16[8,96,2048]{2,1,0:T(8,128)(2,1)S(1)}, bf16[32,32,512]{2,1,0:T(8,128)(2,1)S(1)}, bf16[32,2,32,64]{3,2,1,0:T(8,128)(2,1)S(1)}, bf16[32,2048]{1,0:T(...) custom-call(bf16[8,96,2048]{2,1,0:T(8,128)(2,1)} %refs_0_.1, ...), custom_call_target="tpu_custom_call" | custom-call | bytes 17629184 | tf_op jit(solution)/shard_map/load/pallas_call | solution.py:336
  15.4 0.6 %collective-permute-done.1.refs_2_ = bf16[32,2176]{1,0:T(8,128)(2,1)S(1)} collective-permute-done((bf16[32,2176]{1,0:T(8,128)(2,1)S(1)}, bf16[32,2176]{1,0:T(8,128)(2,1)S(1)}, u32[]{:S(2)}, u32[]{:S(2)}) %collective-permute-start.1) | collective-permute-done | bytes 139296 | tf_op jit(solution)/shard_map/ppermute | solution.py:367
  16.0 1.0 %down.1 = (f32[96,128]{1,0:T(8,128)S(1)}, f32[128,128]{1,0:T(8,128)S(1)}) custom-call(bf16[32,2176]{1,0:T(8,128)(2,1)S(1)} %pack.1.refs_0_, bf16[32,2176]{1,0:T(8,128)(2,1)S(1)} %collective-permute-done.refs_1_, bf16[32,2176]{1,0:T(8,128)(2,1)S(1)} %collective-permute-done.1.refs_2_, bf16[32,2176]{1,0:T(8,128)(2,1)S(1)} %collective-permute-done.2.refs_3_, ...), custom_call_target="tpu_custom_call" | custom-call | tf_op jit(solution)/shard_map/down/pallas_call | solution.py:355
  17.2 1.6 %collective-permute-start.4 = (f32[96,128]{1,0:T(8,128)S(1)}, f32[96,128]{1,0:T(8,128)S(1)}, u32[]{:S(2)}, u32[]{:S(2)}) collective-permute-start(f32[96,128]{1,0:T(8,128)S(1)} %get-tuple-element.20), channel_id=1, source_target_pairs={{0,2},{1,3},{2,0},{3,1},{4,6},{5,7},{6,4},{7,5},{8,10},{9,11},{10,... | collective-permute-start | bytes 147464 | tf_op jit(solution)/shard_map/ppermute | solution.py:367
  18.7 0.3 collective-permute-start.5
  19.2 1.9 %collective-permute-done.3 = f32[96,128]{1,0:T(8,128)S(1)} collective-permute-done((f32[96,128]{1,0:T(8,128)S(1)}, f32[96,128]{1,0:T(8,128)S(1)}, u32[]{:S(2)}, u32[]{:S(2)}) %collective-permute-start.3) | collective-permute-done | bytes 49184 | tf_op jit(solution)/shard_map/ppermute | solution.py:367
  21.1 0.9 %collective-permute-done.4 = f32[96,128]{1,0:T(8,128)S(1)} collective-permute-done((f32[96,128]{1,0:T(8,128)S(1)}, f32[96,128]{1,0:T(8,128)S(1)}, u32[]{:S(2)}, u32[]{:S(2)}) %collective-permute-start.4) | collective-permute-done | bytes 49184 | tf_op jit(solution)/shard_map/ppermute | solution.py:367
  22.1 0.5 %collective-permute-start.6 = (bf16[96,128]{1,0:T(8,128)(2,1)S(1)}, bf16[96,128]{1,0:T(8,128)(2,1)S(1)}, u32[]{:S(2)}, u32[]{:S(2)}) collective-permute-start(bf16[96,128]{1,0:T(8,128)(2,1)S(1)} %add_convert_fusion.refs_0_), channel_id=1, source_target_pairs={{0,12},{4,8},{8,4},{12,0},{1,13},{5,9},{9,5},{13,1},{2,14},{6,10},... | collective-permute-start | bytes 73736 | tf_op jit(solution)/shard_map/ppermute | solution.py:367
  22.6 2.5 %collective-permute-start.7 = (bf16[96,128]{1,0:T(8,128)(2,1)S(1)}, bf16[96,128]{1,0:T(8,128)(2,1)S(1)}, u32[]{:S(2)}, u32[]{:S(2)}) collective-permute-start(bf16[96,128]{1,0:T(8,128)(2,1)S(1)} %add_convert_fusion.refs_0_), channel_id=1, source_target_pairs={{0,8},{4,12},{8,0},{12,4},{1,9},{5,13},{9,1},{13,5},{2,10},{6,14},... | collective-permute-start | bytes 73736 | tf_op jit(solution)/shard_map/ppermute | solution.py:367
  25.1 0.5 %collective-permute-start.8 = (bf16[96,128]{1,0:T(8,128)(2,1)S(1)}, bf16[96,128]{1,0:T(8,128)(2,1)S(1)}, u32[]{:S(2)}, u32[]{:S(2)}) collective-permute-start(bf16[96,128]{1,0:T(8,128)(2,1)S(1)} %add_convert_fusion.refs_0_), channel_id=1, source_target_pairs={{0,4},{4,0},{8,12},{12,8},{1,5},{5,1},{9,13},{13,9},{2,6},{6,2},{1... | collective-permute-start | bytes 73736 | tf_op jit(solution)/shard_map/ppermute | solution.py:367
  25.7 0.9 %collective-permute-done.6.refs_1_ = bf16[96,128]{1,0:T(8,128)(2,1)S(1)} collective-permute-done((bf16[96,128]{1,0:T(8,128)(2,1)S(1)}, bf16[96,128]{1,0:T(8,128)(2,1)S(1)}, u32[]{:S(2)}, u32[]{:S(2)}) %collective-permute-start.6) | collective-permute-done | bytes 24608 | tf_op jit(solution)/shard_map/ppermute | solution.py:367
  26.6 0.9 %collective-permute-done.7.refs_2_ = bf16[96,128]{1,0:T(8,128)(2,1)S(1)} collective-permute-done((bf16[96,128]{1,0:T(8,128)(2,1)S(1)}, bf16[96,128]{1,0:T(8,128)(2,1)S(1)}, u32[]{:S(2)}, u32[]{:S(2)}) %collective-permute-start.7) | collective-permute-done | bytes 24608 | tf_op jit(solution)/shard_map/ppermute | solution.py:367
  27.4 1.5 %collective-permute-done.8.refs_3_ = bf16[96,128]{1,0:T(8,128)(2,1)S(1)} collective-permute-done((bf16[96,128]{1,0:T(8,128)(2,1)S(1)}, bf16[96,128]{1,0:T(8,128)(2,1)S(1)}, u32[]{:S(2)}, u32[]{:S(2)}) %collective-permute-start.8) | collective-permute-done | bytes 24608 | tf_op jit(solution)/shard_map/ppermute | solution.py:367
  29.0 1.1 %up.1 = (f32[32,1408]{1,0:T(8,128)S(1)}, f32[32,1408]{1,0:T(8,128)S(1)}) custom-call(f32[128,128]{1,0:T(8,128)S(1)} %get-tuple-element.19.ids_ref, bf16[96,128]{1,0:T(8,128)(2,1)S(1)} %add_convert_fusion.refs_0_, bf16[96,128]{1,0:T(8,128)(2,1)S(1)} %collective-permute-done.6.refs_1_, bf16[96,128]{1,0:T(8,128)(2,1)S(1)} %collective-permute-done.7.refs_2_, ...), custom_call_target="tpu_custom_call" | custom-call | tf_op jit(solution)/shard_map/up/pallas_call | solution.py:355
  30.0 1.8 %collective-permute-start.12 = (f16[32,1408]{1,0:T(8,128)(2,1)S(1)}, f16[32,1408]{1,0:T(8,128)(2,1)S(1)}, u32[]{:S(2)}, u32[]{:S(2)}) collective-permute-start(f16[32,1408]{1,0:T(8,128)(2,1)S(1)} %convert_element_type.22), channel_id=1, source_target_pairs={{0,8},{1,4},{2,12},{3,0},{4,5},{5,13},{6,9},{7,1},{8,2},{9,10},{10... | collective-permute-start | bytes 270344 | tf_op jit(solution)/shard_map/ppermute | solution.py:456
  32.0 3.6 %collective-permute-done.12 = f16[32,1408]{1,0:T(8,128)(2,1)S(1)} collective-permute-done((f16[32,1408]{1,0:T(8,128)(2,1)S(1)}, f16[32,1408]{1,0:T(8,128)(2,1)S(1)}, u32[]{:S(2)}, u32[]{:S(2)}) %collective-permute-start.12) | collective-permute-done | bytes 90144 | tf_op jit(solution)/shard_map/ppermute | solution.py:456
  35.6 1.5 %attend.2 = (bf16[32,2048]{1,0:T(8,128)(2,1)}, bf16[32,256]{1,0:T(8,128)(2,1)}, bf16[32,256]{1,0:T(8,128)(2,1)}) custom-call(f32[32,1408]{1,0:T(8,128)S(1)} %convert_element_type.23.refs_0_, bf16[32,2048]{1,0:T(8,128)(2,1)S(1)} %get-tuple-element.24.refs_1_, bf16[32,256]{1,0:T(8,128)(2,1)S(1)} %get-tuple-element.25.refs_2_, ...), custom_call_target="tpu_custom_call" | custom-call | tf_op jit(solution)/shard_map/attend/pallas_call | solution.py:303
  37.1 1.1 %collective-permute-done.11 = f16[32,1408]{1,0:T(8,128)(2,1)S(1)} collective-permute-done((f16[32,1408]{1,0:T(8,128)(2,1)S(1)}, f16[32,1408]{1,0:T(8,128)(2,1)S(1)}, u32[]{:S(2)}, u32[]{:S(2)}) %collective-permute-start.11) | collective-permute-done | bytes 90144 | tf_op jit(solution)/shard_map/ppermute | solution.py:456
  38.2 1.5 %attend.3 = (bf16[32,2048]{1,0:T(8,128)(2,1)}, bf16[32,256]{1,0:T(8,128)(2,1)}, bf16[32,256]{1,0:T(8,128)(2,1)}) custom-call(f32[32,1408]{1,0:T(8,128)S(1)} %convert_element_type.20.refs_0_, bf16[32,2048]{1,0:T(8,128)(2,1)S(1)} %get-tuple-element.24.refs_1_, ...), custom_call_target="tpu_custom_call", output_to_operand_aliasing={{0}: (9, {}), {1}: (10, {}), {2}: (11, {})} | custom-call | tf_op jit(solution)/shard_map/attend/pallas_call | solution.py:303
  (20 shorter events, 0.7 us)
Async XLA Ops:
  0.6 28.3 %collective-permute-start.9 = (bf16[32,32,512]{2,1,0:T(8,128)(2,1)}, bf16[32,32,512]{2,1,0:T(8,128)(2,1)S(1)}, u32[]{:S(2)}, u32[]{:S(2)}) collective-permute-start(bf16[32,32,512]{2,1,0:T(8,128)(2,1)} %refs_1_.1), channel_id=1, source_target_pairs={{0,1},{1,0},{2,3},{3,2},{4,5},{5,4},{6,7},{7,6},{8,9},{9,8},{10,11... | collective-permute-start | bytes 3145736 | tf_op jit(solution)/shard_map/ppermute | solution.py:367
  1.6 9.1 %collective-permute-start = (bf16[32,2176]{1,0:T(8,128)(2,1)S(1)}, bf16[32,2176]{1,0:T(8,128)(2,1)S(1)}, u32[]{:S(2)}, u32[]{:S(2)}) collective-permute-start(bf16[32,2176]{1,0:T(8,128)(2,1)S(1)} %pack.1.refs_0_), channel_id=1, source_target_pairs={{0,12},{4,8},{8,4},{12,0},{1,13},{5,9},{9,5},{13,1},{2,14},{6,10},... | collective-permute-start | bytes 417800 | tf_op jit(solution)/shard_map/ppermute | solution.py:367
  2.2 13.2 %collective-permute-start.2 = (bf16[32,2176]{1,0:T(8,128)(2,1)S(1)}, bf16[32,2176]{1,0:T(8,128)(2,1)S(1)}, u32[]{:S(2)}, u32[]{:S(2)}) collective-permute-start(bf16[32,2176]{1,0:T(8,128)(2,1)S(1)} %pack.1.refs_0_), channel_id=1, source_target_pairs={{0,4},{4,0},{8,12},{12,8},{1,5},{5,1},{9,13},{13,9},{2,6},{6,2},{1... | collective-permute-start | bytes 417800 | tf_op jit(solution)/shard_map/ppermute | solution.py:367
  10.8 5.3 %collective-permute-start.1 = (bf16[32,2176]{1,0:T(8,128)(2,1)S(1)}, bf16[32,2176]{1,0:T(8,128)(2,1)S(1)}, u32[]{:S(2)}, u32[]{:S(2)}) collective-permute-start(bf16[32,2176]{1,0:T(8,128)(2,1)S(1)} %collective-permute-done.refs_1_), channel_id=1, source_target_pairs={{0,4},{4,0},{8,12},{12,8},{1,5},{5,1},{9,13},{13,9},{2,6},{6,2},{1... | collective-permute-start | bytes 417800 | tf_op jit(solution)/shard_map/ppermute | solution.py:367
  15.4 3.6 %copy-start.1 = (bf16[32,2,32,64]{3,2,1,0:T(8,128)(2,1)S(1)}, bf16[32,2,32,64]{3,2,1,0:T(8,128)(2,1)}, u32[]{:S(2)}) copy-start(bf16[32,2,32,64]{3,2,1,0:T(8,128)(2,1)} %refs_2_.1) | copy-start | bytes 786436
  15.4 10.3 %copy-start = (s32[32]{0:T(128)S(1)}, s32[32]{0:T(128)}, u32[]{:S(2)}) copy-start(s32[32]{0:T(128)} %param.21) | copy-start | bytes 388
  17.1 4.1 %collective-permute-start.3 = (f32[96,128]{1,0:T(8,128)S(1)}, f32[96,128]{1,0:T(8,128)S(1)}, u32[]{:S(2)}, u32[]{:S(2)}) collective-permute-start(f32[96,128]{1,0:T(8,128)S(1)} %get-tuple-element.20), channel_id=1, source_target_pairs={{0,3},{1,2},{2,1},{3,0},{4,7},{5,6},{6,5},{7,4},{8,11},{9,10},{10,... | collective-permute-start | bytes 147464 | tf_op jit(solution)/shard_map/ppermute | solution.py:367
  17.2 4.9 %collective-permute-start.4 = (f32[96,128]{1,0:T(8,128)S(1)}, f32[96,128]{1,0:T(8,128)S(1)}, u32[]{:S(2)}, u32[]{:S(2)}) collective-permute-start(f32[96,128]{1,0:T(8,128)S(1)} %get-tuple-element.20), channel_id=1, source_target_pairs={{0,2},{1,3},{2,0},{3,1},{4,6},{5,7},{6,4},{7,5},{8,10},{9,11},{10,... | collective-permute-start | bytes 147464 | tf_op jit(solution)/shard_map/ppermute | solution.py:367
  18.7 3.3 %collective-permute-start.5 = (f32[96,128]{1,0:T(8,128)S(1)}, f32[96,128]{1,0:T(8,128)S(1)}, u32[]{:S(2)}, u32[]{:S(2)}) collective-permute-start(f32[96,128]{1,0:T(8,128)S(1)} %get-tuple-element.20), channel_id=1, source_target_pairs={{0,1},{1,0},{2,3},{3,2},{4,5},{5,4},{6,7},{7,6},{8,9},{9,8},{10,11... | collective-permute-start | bytes 147464 | tf_op jit(solution)/shard_map/ppermute | solution.py:367
  19.0 6.7 %collective-permute-start.10 = (bf16[32,2,32,64]{3,2,1,0:T(8,128)(2,1)S(1)}, bf16[32,2,32,64]{3,2,1,0:T(8,128)(2,1)S(1)}, u32[]{:S(2)}, u32[]{:S(2)}) collective-permute-start(bf16[32,2,32,64]{3,2,1,0:T(8,128)(2,1)S(1)} %copy-done.1), channel_id=1, source_target_pairs={{0,1},{1,0},{2,3},{3,2},{4,5},{5,4},{6,7},{7,6},{8,9},{9,8},{10,11... | collective-permute-start | bytes 786440 | tf_op jit(solution)/shard_map/ppermute | solution.py:367
  22.1 4.5 %collective-permute-start.6 = (bf16[96,128]{1,0:T(8,128)(2,1)S(1)}, bf16[96,128]{1,0:T(8,128)(2,1)S(1)}, u32[]{:S(2)}, u32[]{:S(2)}) collective-permute-start(bf16[96,128]{1,0:T(8,128)(2,1)S(1)} %add_convert_fusion.refs_0_), channel_id=1, source_target_pairs={{0,12},{4,8},{8,4},{12,0},{1,13},{5,9},{9,5},{13,1},{2,14},{6,10},... | collective-permute-start | bytes 73736 | tf_op jit(solution)/shard_map/ppermute | solution.py:367
  22.6 4.8 %collective-permute-start.7 = (bf16[96,128]{1,0:T(8,128)(2,1)S(1)}, bf16[96,128]{1,0:T(8,128)(2,1)S(1)}, u32[]{:S(2)}, u32[]{:S(2)}) collective-permute-start(bf16[96,128]{1,0:T(8,128)(2,1)S(1)} %add_convert_fusion.refs_0_), channel_id=1, source_target_pairs={{0,8},{4,12},{8,0},{12,4},{1,9},{5,13},{9,1},{13,5},{2,10},{6,14},... | collective-permute-start | bytes 73736 | tf_op jit(solution)/shard_map/ppermute | solution.py:367
  25.1 3.8 %collective-permute-start.8 = (bf16[96,128]{1,0:T(8,128)(2,1)S(1)}, bf16[96,128]{1,0:T(8,128)(2,1)S(1)}, u32[]{:S(2)}, u32[]{:S(2)}) collective-permute-start(bf16[96,128]{1,0:T(8,128)(2,1)S(1)} %add_convert_fusion.refs_0_), channel_id=1, source_target_pairs={{0,4},{4,0},{8,12},{12,8},{1,5},{5,1},{9,13},{13,9},{2,6},{6,2},{1... | collective-permute-start | bytes 73736 | tf_op jit(solution)/shard_map/ppermute | solution.py:367
  30.0 5.6 %collective-permute-start.12 = (f16[32,1408]{1,0:T(8,128)(2,1)S(1)}, f16[32,1408]{1,0:T(8,128)(2,1)S(1)}, u32[]{:S(2)}, u32[]{:S(2)}) collective-permute-start(f16[32,1408]{1,0:T(8,128)(2,1)S(1)} %convert_element_type.22), channel_id=1, source_target_pairs={{0,8},{1,4},{2,12},{3,0},{4,5},{5,13},{6,9},{7,1},{8,2},{9,10},{10... | collective-permute-start | bytes 270344 | tf_op jit(solution)/shard_map/ppermute | solution.py:456
  31.8 6.4 %collective-permute-start.11 = (f16[32,1408]{1,0:T(8,128)(2,1)S(1)}, f16[32,1408]{1,0:T(8,128)(2,1)S(1)}, u32[]{:S(2)}, u32[]{:S(2)}) collective-permute-start(f16[32,1408]{1,0:T(8,128)(2,1)S(1)} %convert_element_type.19), channel_id=1, source_target_pairs={{0,12},{1,0},{2,8},{3,4},{4,9},{5,1},{6,5},{7,13},{8,6},{9,14},{10... | collective-permute-start | bytes 270344 | tf_op jit(solution)/shard_map/ppermute | solution.py:456

commit v6 on v5

--- a/solution.py
+++ b/solution.py
@@ -25,7 +25,7 @@
     return jnp.cos(angles), jnp.sin(angles)
 
 
-ORDER = (((2, 3), (1, 0)), ((1, 2), (3, 0)), ((0, 1), (2, 3)), ((1, 3), (2, 0)))
+ORDER = (((2, 1), (3, 0)), ((1, 2), (3, 0)), ((1, 0), (2, 3)), ((0, 3), (1, 2)))
 PLANES = [
     sum(ORDER[a][c][i] << (4 * a + 2 * i) for a in range(4) for i in range(2)) for c in range(2)
 ]
@@ -405,7 +405,9 @@
         ]
         for k in range(2)
     ]
-    other_query = step(adapter_up_query, "tensor", columns, 1)
+    message, early_query = lax.optimization_barrier((message, adapter_up_query))
+    everyone[0] = message
+    other_query = step(early_query, "tensor", columns, 1)
     other_key_value = step(adapter_up_key_value, "tensor", columns, 1)
     (
         adapter_down_weight,

time: 40.1 us -> 39.7 us (0.990)
  waiting for transfers between devices: 18.7 us -> 17 us
  starting transfers between devices: 10.3 us -> 11.3 us
    ppermute x2, waiting for transfers between devices: 4.64 us -> 3.07 us  [few_body(): lax.ppermute(term.astype(jnp.float16), ('adapter', 'tensor'), sent[k])]
    ppermute x2, starting transfers between devices: 1.83 us -> 2.83 us  [few_body(): lax.ppermute(term.astype(jnp.float16), ('adapter', 'tensor'), sent[k])]
  transfers between devices with their start and end apart: 13 -> 13, of which waited for: 9 -> 9; matrix products, arithmetic and copies ran while one was open for 0% -> 0% of each run, Pallas kernels for 18% -> 16%
where the time goes in v6:
time: 39.7 us; the launch traced here: 39.1 us
  waiting for transfers between devices  17 us (43%)
  starting transfers between devices  11.3 us (28%)
  Pallas kernels  9.77 us (25%)
  between operations  0.76 us (2%)
    ppermute x11, waiting for transfers between devices, step(): return lax.ppermute(value, axis, [(i, i ^ k) for i in range(size)])  14 us
    ppermute x11, starting transfers between devices, step(): return lax.ppermute(value, axis, [(i, i ^ k) for i in range(size)])  8.52 us
    pallas_call x1, Pallas kernels, load(): pl.pallas_call(load_kernel, out_shape=[pltpu.VMEM(a.shape, a.dtype) for a...  3.76 us
    ppermute x2, waiting for transfers between devices, few_body(): lax.ppermute(term.astype(jnp.float16), ('adapter', 'tensor'), sent[k])  3.07 us
    pallas_call x2, Pallas kernels, attend(): pl.pallas_call(functools.partial(attend_kernel, message), out_shape=shape...  3 us
    ppermute x2, starting transfers between devices, few_body(): lax.ppermute(term.astype(jnp.float16), ('adapter', 'tensor'), sent[k])  2.83 us
    pallas_call x2, Pallas kernels, call(): pl.pallas_call(kernel, out_shape=out_shape, in_specs=[in_vmem()] * len(ar...  2.08 us
    pallas_call x1, Pallas kernels, pack(): pl.pallas_call(pack_kernel, out_shape=pltpu.VMEM((requests, width + LANES...  0.92 us
  transfers between devices with their start and end apart: 13, of which 9 were waited for; matrix products, arithmetic and copies ran while one was open for 0% of the time, Pallas kernels for 16%

profile of v6, /device:TPU:20, one launch (start us, length us, event | category | flops | bytes accessed | tf_op | source)
XLA Modules:
  0.0 39.1 jit_solution(13800334851920487056)
XLA Ops:
  0.6 0.9 %pack.1.refs_0_ = bf16[32,2176]{1,0:T(8,128)(2,1)S(1)} custom-call(s32[32]{0:T(128)} %ids_in.1, bf16[32,2048]{1,0:T(8,128)(2,1)} %hidden_in.1), custom_call_target="tpu_custom_call" | custom-call | tf_op jit(solution)/shard_map/pack/pallas_call | solution.py:66
  1.6 0.5 %collective-permute-start = (bf16[32,2176]{1,0:T(8,128)(2,1)S(1)}, bf16[32,2176]{1,0:T(8,128)(2,1)S(1)}, u32[]{:S(2)}, u32[]{:S(2)}) collective-permute-start(bf16[32,2176]{1,0:T(8,128)(2,1)S(1)} %pack.1.refs_0_), channel_id=1, source_target_pairs={{0,12},{4,8},{8,4},{12,0},{1,13},{5,9},{9,5},{13,1},{2,14},{6,10},... | collective-permute-start | bytes 417800 | tf_op jit(solution)/shard_map/ppermute | solution.py:367
  2.2 1.3 %collective-permute-start.2 = (bf16[32,2176]{1,0:T(8,128)(2,1)S(1)}, bf16[32,2176]{1,0:T(8,128)(2,1)S(1)}, u32[]{:S(2)}, u32[]{:S(2)}) collective-permute-start(bf16[32,2176]{1,0:T(8,128)(2,1)S(1)} %pack.1.refs_0_), channel_id=1, source_target_pairs={{0,4},{4,0},{8,12},{12,8},{1,5},{5,1},{9,13},{13,9},{2,6},{6,2},{1... | collective-permute-start | bytes 417800 | tf_op jit(solution)/shard_map/ppermute | solution.py:367
  3.5 7.2 %collective-permute-done.refs_1_ = bf16[32,2176]{1,0:T(8,128)(2,1)S(1)} collective-permute-done((bf16[32,2176]{1,0:T(8,128)(2,1)S(1)}, bf16[32,2176]{1,0:T(8,128)(2,1)S(1)}, u32[]{:S(2)}, u32[]{:S(2)}) %collective-permute-start) | collective-permute-done | bytes 139296 | tf_op jit(solution)/shard_map/ppermute | solution.py:367
  10.7 0.9 %collective-permute-start.1 = (bf16[32,2176]{1,0:T(8,128)(2,1)S(1)}, bf16[32,2176]{1,0:T(8,128)(2,1)S(1)}, u32[]{:S(2)}, u32[]{:S(2)}) collective-permute-start(bf16[32,2176]{1,0:T(8,128)(2,1)S(1)} %collective-permute-done.refs_1_), channel_id=1, source_target_pairs={{0,4},{4,0},{8,12},{12,8},{1,5},{5,1},{9,13},{13,9},{2,6},{6,2},{1... | collective-permute-start | bytes 417800 | tf_op jit(solution)/shard_map/ppermute | solution.py:367
  11.6 3.8 %load.1 = (bf16[8,96,2048]{2,1,0:T(8,128)(2,1)S(1)}, bf16[32,32,512]{2,1,0:T(8,128)(2,1)S(1)}, bf16[32,2,32,64]{3,2,1,0:T(8,128)(2,1)S(1)}, bf16[32,2048]{1,0:T(...) custom-call(bf16[8,96,2048]{2,1,0:T(8,128)(2,1)} %refs_0_.1, ...), custom_call_target="tpu_custom_call" | custom-call | bytes 17629184 | tf_op jit(solution)/shard_map/load/pallas_call | solution.py:336
  15.4 0.5 %collective-permute-done.1.refs_2_ = bf16[32,2176]{1,0:T(8,128)(2,1)S(1)} collective-permute-done((bf16[32,2176]{1,0:T(8,128)(2,1)S(1)}, bf16[32,2176]{1,0:T(8,128)(2,1)S(1)}, u32[]{:S(2)}, u32[]{:S(2)}) %collective-permute-start.1) | collective-permute-done | bytes 139296 | tf_op jit(solution)/shard_map/ppermute | solution.py:367
  16.0 1.0 %down.1 = (f32[96,128]{1,0:T(8,128)S(1)}, f32[128,128]{1,0:T(8,128)S(1)}) custom-call(bf16[32,2176]{1,0:T(8,128)(2,1)S(1)} %pack.1.refs_0_, bf16[32,2176]{1,0:T(8,128)(2,1)S(1)} %collective-permute-done.refs_1_, bf16[32,2176]{1,0:T(8,128)(2,1)S(1)} %collective-permute-done.1.refs_2_, bf16[32,2176]{1,0:T(8,128)(2,1)S(1)} %collective-permute-done.2.refs_3_, ...), custom_call_target="tpu_custom_call" | custom-call | tf_op jit(solution)/shard_map/down/pallas_call | solution.py:355
  17.1 1.6 %collective-permute-start.4 = (f32[96,128]{1,0:T(8,128)S(1)}, f32[96,128]{1,0:T(8,128)S(1)}, u32[]{:S(2)}, u32[]{:S(2)}) collective-permute-start(f32[96,128]{1,0:T(8,128)S(1)} %get-tuple-element.23), channel_id=1, source_target_pairs={{0,2},{1,3},{2,0},{3,1},{4,6},{5,7},{6,4},{7,5},{8,10},{9,11},{10,... | collective-permute-start | bytes 147464 | tf_op jit(solution)/shard_map/ppermute | solution.py:367
  18.6 0.3 collective-permute-start.5
  19.1 1.9 %collective-permute-done.3 = f32[96,128]{1,0:T(8,128)S(1)} collective-permute-done((f32[96,128]{1,0:T(8,128)S(1)}, f32[96,128]{1,0:T(8,128)S(1)}, u32[]{:S(2)}, u32[]{:S(2)}) %collective-permute-start.3) | collective-permute-done | bytes 49184 | tf_op jit(solution)/shard_map/ppermute | solution.py:367
  21.0 0.9 %collective-permute-done.4 = f32[96,128]{1,0:T(8,128)S(1)} collective-permute-done((f32[96,128]{1,0:T(8,128)S(1)}, f32[96,128]{1,0:T(8,128)S(1)}, u32[]{:S(2)}, u32[]{:S(2)}) %collective-permute-start.4) | collective-permute-done | bytes 49184 | tf_op jit(solution)/shard_map/ppermute | solution.py:367
  22.0 0.5 %collective-permute-start.6 = (bf16[96,128]{1,0:T(8,128)(2,1)S(1)}, bf16[96,128]{1,0:T(8,128)(2,1)S(1)}, u32[]{:S(2)}, u32[]{:S(2)}) collective-permute-start(bf16[96,128]{1,0:T(8,128)(2,1)S(1)} %add_convert_fusion.refs_0_), channel_id=1, source_target_pairs={{0,12},{4,8},{8,4},{12,0},{1,13},{5,9},{9,5},{13,1},{2,14},{6,10},... | collective-permute-start | bytes 73736 | tf_op jit(solution)/shard_map/ppermute | solution.py:367
  22.5 2.6 %collective-permute-start.7 = (bf16[96,128]{1,0:T(8,128)(2,1)S(1)}, bf16[96,128]{1,0:T(8,128)(2,1)S(1)}, u32[]{:S(2)}, u32[]{:S(2)}) collective-permute-start(bf16[96,128]{1,0:T(8,128)(2,1)S(1)} %add_convert_fusion.refs_0_), channel_id=1, source_target_pairs={{0,8},{4,12},{8,0},{12,4},{1,9},{5,13},{9,1},{13,5},{2,10},{6,14},... | collective-permute-start | bytes 73736 | tf_op jit(solution)/shard_map/ppermute | solution.py:367
  25.1 0.4 %collective-permute-start.8 = (bf16[96,128]{1,0:T(8,128)(2,1)S(1)}, bf16[96,128]{1,0:T(8,128)(2,1)S(1)}, u32[]{:S(2)}, u32[]{:S(2)}) collective-permute-start(bf16[96,128]{1,0:T(8,128)(2,1)S(1)} %add_convert_fusion.refs_0_), channel_id=1, source_target_pairs={{0,4},{4,0},{8,12},{12,8},{1,5},{5,1},{9,13},{13,9},{2,6},{6,2},{1... | collective-permute-start | bytes 73736 | tf_op jit(solution)/shard_map/ppermute | solution.py:367
  25.6 0.3 collective-permute-done.6.refs_1_
  25.9 1.5 %collective-permute-done.7.refs_2_ = bf16[96,128]{1,0:T(8,128)(2,1)S(1)} collective-permute-done((bf16[96,128]{1,0:T(8,128)(2,1)S(1)}, bf16[96,128]{1,0:T(8,128)(2,1)S(1)}, u32[]{:S(2)}, u32[]{:S(2)}) %collective-permute-start.7) | collective-permute-done | bytes 24608 | tf_op jit(solution)/shard_map/ppermute | solution.py:367
  27.4 1.5 %collective-permute-done.8.refs_3_ = bf16[96,128]{1,0:T(8,128)(2,1)S(1)} collective-permute-done((bf16[96,128]{1,0:T(8,128)(2,1)S(1)}, bf16[96,128]{1,0:T(8,128)(2,1)S(1)}, u32[]{:S(2)}, u32[]{:S(2)}) %collective-permute-start.8) | collective-permute-done | bytes 24608 | tf_op jit(solution)/shard_map/ppermute | solution.py:367
  29.0 1.1 %up.1 = (f32[32,1408]{1,0:T(8,128)S(1)}, f32[32,1408]{1,0:T(8,128)S(1)}) custom-call(f32[128,128]{1,0:T(8,128)S(1)} %get-tuple-element.22.ids_ref, bf16[96,128]{1,0:T(8,128)(2,1)S(1)} %add_convert_fusion.refs_0_, bf16[96,128]{1,0:T(8,128)(2,1)S(1)} %collective-permute-done.6.refs_1_, bf16[96,128]{1,0:T(8,128)(2,1)S(1)} %collective-permute-done.7.refs_2_, ...), custom_call_target="tpu_custom_call" | custom-call | tf_op jit(solution)/shard_map/up/pallas_call | solution.py:355
  30.0 1.1 %collective-permute-start.12 = (f16[32,1408]{1,0:T(8,128)(2,1)S(1)}, f16[32,1408]{1,0:T(8,128)(2,1)S(1)}, u32[]{:S(2)}, u32[]{:S(2)}) collective-permute-start(f16[32,1408]{1,0:T(8,128)(2,1)S(1)} %convert_element_type.22), channel_id=1, source_target_pairs={{0,8},{1,12},{2,4},{3,0},{4,5},{5,13},{6,9},{7,1},{8,6},{9,10},{10... | collective-permute-start | bytes 270344 | tf_op jit(solution)/shard_map/ppermute | solution.py:458
  31.1 1.8 %collective-permute-start.11 = (f16[32,1408]{1,0:T(8,128)(2,1)S(1)}, f16[32,1408]{1,0:T(8,128)(2,1)S(1)}, u32[]{:S(2)}, u32[]{:S(2)}) collective-permute-start(f16[32,1408]{1,0:T(8,128)(2,1)S(1)} %convert_element_type.19), channel_id=1, source_target_pairs={{0,4},{1,0},{2,8},{3,12},{4,9},{5,1},{6,5},{7,13},{8,2},{9,14},{10... | collective-permute-start | bytes 270344 | tf_op jit(solution)/shard_map/ppermute | solution.py:458
  33.0 2.9 %collective-permute-done.12 = f16[32,1408]{1,0:T(8,128)(2,1)S(1)} collective-permute-done((f16[32,1408]{1,0:T(8,128)(2,1)S(1)}, f16[32,1408]{1,0:T(8,128)(2,1)S(1)}, u32[]{:S(2)}, u32[]{:S(2)}) %collective-permute-start.12) | collective-permute-done | bytes 90144 | tf_op jit(solution)/shard_map/ppermute | solution.py:458
  35.9 1.5 %attend.2 = (bf16[32,2048]{1,0:T(8,128)(2,1)}, bf16[32,256]{1,0:T(8,128)(2,1)}, bf16[32,256]{1,0:T(8,128)(2,1)}) custom-call(f32[32,1408]{1,0:T(8,128)S(1)} %convert_element_type.23.refs_0_, bf16[32,2048]{1,0:T(8,128)(2,1)S(1)} %get-tuple-element.28.refs_1_, bf16[32,256]{1,0:T(8,128)(2,1)S(1)} %get-tuple-element.29.refs_2_, ...), custom_call_target="tpu_custom_call" | custom-call | tf_op jit(solution)/shard_map/attend/pallas_call | solution.py:303
  37.6 1.5 %attend.3 = (bf16[32,2048]{1,0:T(8,128)(2,1)}, bf16[32,256]{1,0:T(8,128)(2,1)}, bf16[32,256]{1,0:T(8,128)(2,1)}) custom-call(f32[32,1408]{1,0:T(8,128)S(1)} %convert_element_type.20.refs_0_, bf16[32,2048]{1,0:T(8,128)(2,1)S(1)} %get-tuple-element.28.refs_1_, ...), custom_call_target="tpu_custom_call", output_to_operand_aliasing={{0}: (9, {}), {1}: (10, {}), {2}: (11, {})} | custom-call | tf_op jit(solution)/shard_map/attend/pallas_call | solution.py:303
  (20 shorter events, 0.8 us)
Async XLA Ops:
  1.6 27.4 %collective-permute-start.9 = (bf16[32,32,512]{2,1,0:T(8,128)(2,1)}, bf16[32,32,512]{2,1,0:T(8,128)(2,1)S(1)}, u32[]{:S(2)}, u32[]{:S(2)}) collective-permute-start(bf16[32,32,512]{2,1,0:T(8,128)(2,1)} %refs_1_.1), channel_id=1, source_target_pairs={{0,1},{1,0},{2,3},{3,2},{4,5},{5,4},{6,7},{7,6},{8,9},{9,8},{10,11... | collective-permute-start | bytes 3145736 | tf_op jit(solution)/shard_map/ppermute | solution.py:367
  1.6 9.1 %collective-permute-start = (bf16[32,2176]{1,0:T(8,128)(2,1)S(1)}, bf16[32,2176]{1,0:T(8,128)(2,1)S(1)}, u32[]{:S(2)}, u32[]{:S(2)}) collective-permute-start(bf16[32,2176]{1,0:T(8,128)(2,1)S(1)} %pack.1.refs_0_), channel_id=1, source_target_pairs={{0,12},{4,8},{8,4},{12,0},{1,13},{5,9},{9,5},{13,1},{2,14},{6,10},... | collective-permute-start | bytes 417800 | tf_op jit(solution)/shard_map/ppermute | solution.py:367
  2.2 13.2 %collective-permute-start.2 = (bf16[32,2176]{1,0:T(8,128)(2,1)S(1)}, bf16[32,2176]{1,0:T(8,128)(2,1)S(1)}, u32[]{:S(2)}, u32[]{:S(2)}) collective-permute-start(bf16[32,2176]{1,0:T(8,128)(2,1)S(1)} %pack.1.refs_0_), channel_id=1, source_target_pairs={{0,4},{4,0},{8,12},{12,8},{1,5},{5,1},{9,13},{13,9},{2,6},{6,2},{1... | collective-permute-start | bytes 417800 | tf_op jit(solution)/shard_map/ppermute | solution.py:367
  10.7 5.2 %collective-permute-start.1 = (bf16[32,2176]{1,0:T(8,128)(2,1)S(1)}, bf16[32,2176]{1,0:T(8,128)(2,1)S(1)}, u32[]{:S(2)}, u32[]{:S(2)}) collective-permute-start(bf16[32,2176]{1,0:T(8,128)(2,1)S(1)} %collective-permute-done.refs_1_), channel_id=1, source_target_pairs={{0,4},{4,0},{8,12},{12,8},{1,5},{5,1},{9,13},{13,9},{2,6},{6,2},{1... | collective-permute-start | bytes 417800 | tf_op jit(solution)/shard_map/ppermute | solution.py:367
  15.4 3.5 %copy-start.1 = (bf16[32,2,32,64]{3,2,1,0:T(8,128)(2,1)S(1)}, bf16[32,2,32,64]{3,2,1,0:T(8,128)(2,1)}, u32[]{:S(2)}) copy-start(bf16[32,2,32,64]{3,2,1,0:T(8,128)(2,1)} %refs_2_.1) | copy-start | bytes 786436
  15.4 10.2 %copy-start = (s32[32]{0:T(128)S(1)}, s32[32]{0:T(128)}, u32[]{:S(2)}) copy-start(s32[32]{0:T(128)} %param.21) | copy-start | bytes 388
  17.0 4.1 %collective-permute-start.3 = (f32[96,128]{1,0:T(8,128)S(1)}, f32[96,128]{1,0:T(8,128)S(1)}, u32[]{:S(2)}, u32[]{:S(2)}) collective-permute-start(f32[96,128]{1,0:T(8,128)S(1)} %get-tuple-element.23), channel_id=1, source_target_pairs={{0,3},{1,2},{2,1},{3,0},{4,7},{5,6},{6,5},{7,4},{8,11},{9,10},{10,... | collective-permute-start | bytes 147464 | tf_op jit(solution)/shard_map/ppermute | solution.py:367
  17.1 4.9 %collective-permute-start.4 = (f32[96,128]{1,0:T(8,128)S(1)}, f32[96,128]{1,0:T(8,128)S(1)}, u32[]{:S(2)}, u32[]{:S(2)}) collective-permute-start(f32[96,128]{1,0:T(8,128)S(1)} %get-tuple-element.23), channel_id=1, source_target_pairs={{0,2},{1,3},{2,0},{3,1},{4,6},{5,7},{6,4},{7,5},{8,10},{9,11},{10,... | collective-permute-start | bytes 147464 | tf_op jit(solution)/shard_map/ppermute | solution.py:367
  18.6 3.3 %collective-permute-start.5 = (f32[96,128]{1,0:T(8,128)S(1)}, f32[96,128]{1,0:T(8,128)S(1)}, u32[]{:S(2)}, u32[]{:S(2)}) collective-permute-start(f32[96,128]{1,0:T(8,128)S(1)} %get-tuple-element.23), channel_id=1, source_target_pairs={{0,1},{1,0},{2,3},{3,2},{4,5},{5,4},{6,7},{7,6},{8,9},{9,8},{10,11... | collective-permute-start | bytes 147464 | tf_op jit(solution)/shard_map/ppermute | solution.py:367
  18.9 6.7 %collective-permute-start.10 = (bf16[32,2,32,64]{3,2,1,0:T(8,128)(2,1)S(1)}, bf16[32,2,32,64]{3,2,1,0:T(8,128)(2,1)S(1)}, u32[]{:S(2)}, u32[]{:S(2)}) collective-permute-start(bf16[32,2,32,64]{3,2,1,0:T(8,128)(2,1)S(1)} %copy-done.1), channel_id=1, source_target_pairs={{0,1},{1,0},{2,3},{3,2},{4,5},{5,4},{6,7},{7,6},{8,9},{9,8},{10,11... | collective-permute-start | bytes 786440 | tf_op jit(solution)/shard_map/ppermute | solution.py:367
  22.0 3.9 %collective-permute-start.6 = (bf16[96,128]{1,0:T(8,128)(2,1)S(1)}, bf16[96,128]{1,0:T(8,128)(2,1)S(1)}, u32[]{:S(2)}, u32[]{:S(2)}) collective-permute-start(bf16[96,128]{1,0:T(8,128)(2,1)S(1)} %add_convert_fusion.refs_0_), channel_id=1, source_target_pairs={{0,12},{4,8},{8,4},{12,0},{1,13},{5,9},{9,5},{13,1},{2,14},{6,10},... | collective-permute-start | bytes 73736 | tf_op jit(solution)/shard_map/ppermute | solution.py:367
  22.5 4.9 %collective-permute-start.7 = (bf16[96,128]{1,0:T(8,128)(2,1)S(1)}, bf16[96,128]{1,0:T(8,128)(2,1)S(1)}, u32[]{:S(2)}, u32[]{:S(2)}) collective-permute-start(bf16[96,128]{1,0:T(8,128)(2,1)S(1)} %add_convert_fusion.refs_0_), channel_id=1, source_target_pairs={{0,8},{4,12},{8,0},{12,4},{1,9},{5,13},{9,1},{13,5},{2,10},{6,14},... | collective-permute-start | bytes 73736 | tf_op jit(solution)/shard_map/ppermute | solution.py:367
  25.1 3.8 %collective-permute-start.8 = (bf16[96,128]{1,0:T(8,128)(2,1)S(1)}, bf16[96,128]{1,0:T(8,128)(2,1)S(1)}, u32[]{:S(2)}, u32[]{:S(2)}) collective-permute-start(bf16[96,128]{1,0:T(8,128)(2,1)S(1)} %add_convert_fusion.refs_0_), channel_id=1, source_target_pairs={{0,4},{4,0},{8,12},{12,8},{1,5},{5,1},{9,13},{13,9},{2,6},{6,2},{1... | collective-permute-start | bytes 73736 | tf_op jit(solution)/shard_map/ppermute | solution.py:367
  30.0 5.8 %collective-permute-start.12 = (f16[32,1408]{1,0:T(8,128)(2,1)S(1)}, f16[32,1408]{1,0:T(8,128)(2,1)S(1)}, u32[]{:S(2)}, u32[]{:S(2)}) collective-permute-start(f16[32,1408]{1,0:T(8,128)(2,1)S(1)} %convert_element_type.22), channel_id=1, source_target_pairs={{0,8},{1,12},{2,4},{3,0},{4,5},{5,13},{6,9},{7,1},{8,6},{9,10},{10... | collective-permute-start | bytes 270344 | tf_op jit(solution)/shard_map/ppermute | solution.py:458
  31.1 6.5 %collective-permute-start.11 = (f16[32,1408]{1,0:T(8,128)(2,1)S(1)}, f16[32,1408]{1,0:T(8,128)(2,1)S(1)}, u32[]{:S(2)}, u32[]{:S(2)}) collective-permute-start(f16[32,1408]{1,0:T(8,128)(2,1)S(1)} %convert_element_type.19), channel_id=1, source_target_pairs={{0,4},{1,0},{2,8},{3,12},{4,9},{5,1},{6,5},{7,13},{8,2},{9,14},{10... | collective-permute-start | bytes 270344 | tf_op jit(solution)/shard_map/ppermute | solution.py:458

commit v7 on v6

--- a/solution.py
+++ b/solution.py
@@ -48,29 +48,41 @@
 
 def pack_kernel(ids_in, hidden_in, out_ref, ids_ref, sems):
     requests, width = hidden_in.shape
+    half = requests // 2
     ids_copy = pltpu.make_async_copy(ids_in, ids_ref, sems.at[0])
-    hidden_copy = pltpu.make_async_copy(hidden_in, out_ref.at[:, pl.ds(0, width)], sems.at[1])
-    hidden_copy.start()
+    copies = [
+        pltpu.make_async_copy(
+            hidden_in.at[pl.ds(i * half, half)],
+            out_ref.at[:, pl.ds(i * width, width)],
+            sems.at[1 + i],
+        )
+        for i in range(2)
+    ]
+    for copy in copies:
+        copy.start()
     ids_copy.start()
     ids_copy.wait()
-    row = lax.broadcasted_iota(jnp.int32, (requests, LANES), 0)
-    ids = jnp.zeros((requests, LANES), jnp.int32)
+    row = lax.broadcasted_iota(jnp.int32, (half, LANES), 0)
+    lane = lax.broadcasted_iota(jnp.int32, (half, LANES), 1)
+    row += jnp.where(lane < LANES // 2, 0, half)
+    ids = jnp.zeros((half, LANES), jnp.int32)
     for r in range(requests):
         ids = jnp.where(row == r, ids_ref[r], ids)
-    out_ref[:, width:] = ids.astype(jnp.float32).astype(jnp.bfloat16)
-    hidden_copy.wait()
+    out_ref[:, 2 * width :] = ids.astype(jnp.float32).astype(jnp.bfloat16)
+    for copy in copies:
+        copy.wait()
 
 
 def pack(request_adapter, hidden):
     requests, width = hidden.shape
     return pl.pallas_call(
         pack_kernel,
-        out_shape=pltpu.VMEM((requests, width + LANES), jnp.bfloat16),
+        out_shape=pltpu.VMEM((requests // 2, 2 * width + LANES), jnp.bfloat16),
         in_specs=[pl.BlockSpec(memory_space=pltpu.HBM)] * 2,
         out_specs=in_vmem(),
         scratch_shapes=[
             pltpu.SMEM(request_adapter.shape, jnp.int32),
-            pltpu.SemaphoreType.DMA((2,)),
+            pltpu.SemaphoreType.DMA((3,)),
         ],
         compiler_params=pltpu.CompilerParams(vmem_limit_bytes=PACK_BYTES),
         name="pack",
@@ -81,16 +93,20 @@
     *message_refs, down_ref, out_ref, ids_ref, rows_ref = refs
     place = position()[0]
     held, rank, width = down_ref.shape
-    block = message_refs[0].shape[0]
+    half = message_refs[0].shape[0]
+    lane = lax.broadcasted_iota(jnp.int32, (half, LANES), 1)
     for k, message_ref in zip((0, 3, 2, 1), message_refs):
-        start = pl.multiple_of((place ^ k) * block, block)
-        rows_ref[pl.ds(start, block), :] = message_ref[...]
-    ids = rows_ref[:, width:].astype(jnp.float32)
-    ids_ref[...] = ids
+        pair = message_ref[:, 2 * width :].astype(jnp.float32)
+        swapped = pltpu.roll(pair, LANES // 2, 1)
+        for i in range(2):
+            start = pl.multiple_of((place ^ k) * 2 * half + i * half, half)
+            rows_ref[pl.ds(start, half), :] = message_ref[:, i * width : (i + 1) * width]
+            ids_ref[pl.ds(start, half), :] = jnp.where((lane < LANES // 2) == (i == 0), pair, swapped)
+    ids = ids_ref[...]
     slot = jnp.transpose(ids)[0:1] - (place * held).astype(jnp.float32)
     product = lax.dot_general(
         down_ref[...].reshape(held * rank, width),
-        rows_ref[:, :width],
+        rows_ref[...],
         (((1,), (1,)), ((), ())),
         preferred_element_type=jnp.float32,
     )
@@ -434,7 +450,7 @@
         down_kernel,
         "down",
         [jax.ShapeDtypeStruct((rank3, every), f32), jax.ShapeDtypeStruct((every, LANES), f32)],
-        [pltpu.VMEM((every, hidden.shape[1] + LANES), bf16)],
+        [pltpu.VMEM((every, hidden.shape[1]), bf16)],
         [*everyone, adapter_down_weight],
     )
     summed = functools.reduce(jnp.add, exchange(partial, "tensor", columns)).astype(bf16)

time: 39.7 us -> 39.4 us (level)
  no operation moved by 1% of the time
where the time goes in v7:
time: 39.4 us; the launch traced here: 39 us
  waiting for transfers between devices  16.8 us (43%)
  starting transfers between devices  11.4 us (29%)
  Pallas kernels  9.75 us (25%)
  between operations  0.76 us (2%)
    ppermute x11, waiting for transfers between devices, step(): return lax.ppermute(value, axis, [(i, i ^ k) for i in range(size)])  13.7 us
    ppermute x11, starting transfers between devices, step(): return lax.ppermute(value, axis, [(i, i ^ k) for i in range(size)])  8.61 us
    pallas_call x1, Pallas kernels, load(): pl.pallas_call(load_kernel, out_shape=[pltpu.VMEM(a.shape, a.dtype) for a...  3.76 us
    ppermute x2, waiting for transfers between devices, few_body(): lax.ppermute(term.astype(jnp.float16), ('adapter', 'tensor'), sent[k])  3.09 us
    pallas_call x2, Pallas kernels, attend(): pl.pallas_call(functools.partial(attend_kernel, message), out_shape=shape...  3 us
    ppermute x2, starting transfers between devices, few_body(): lax.ppermute(term.astype(jnp.float16), ('adapter', 'tensor'), sent[k])  2.77 us
    pallas_call x2, Pallas kernels, call(): pl.pallas_call(kernel, out_shape=out_shape, in_specs=[in_vmem()] * len(ar...  2.09 us
    pallas_call x1, Pallas kernels, pack(): pl.pallas_call(pack_kernel, out_shape=pltpu.VMEM((requests // 2, 2 * widt...  0.9 us
  transfers between devices with their start and end apart: 13, of which 9 were waited for; matrix products, arithmetic and copies ran while one was open for 0% of the time, Pallas kernels for 16%

profile of v7, /device:TPU:20, one launch (start us, length us, event | category | flops | bytes accessed | tf_op | source)
XLA Modules:
  0.0 39.0 jit_solution(2143655902204771752)
XLA Ops:
  0.6 0.9 %pack.1.refs_0_ = bf16[16,4224]{1,0:T(8,128)(2,1)S(1)} custom-call(s32[32]{0:T(128)} %ids_in.1, bf16[32,2048]{1,0:T(8,128)(2,1)} %hidden_in.1), custom_call_target="tpu_custom_call" | custom-call | tf_op jit(solution)/shard_map/pack/pallas_call | solution.py:78
  1.6 0.5 %collective-permute-start = (bf16[16,4224]{1,0:T(8,128)(2,1)S(1)}, bf16[16,4224]{1,0:T(8,128)(2,1)S(1)}, u32[]{:S(2)}, u32[]{:S(2)}) collective-permute-start(bf16[16,4224]{1,0:T(8,128)(2,1)S(1)} %pack.1.refs_0_), channel_id=1, source_target_pairs={{0,12},{4,8},{8,4},{12,0},{1,13},{5,9},{9,5},{13,1},{2,14},{6,10},... | collective-permute-start | bytes 405512 | tf_op jit(solution)/shard_map/ppermute | solution.py:383
  2.1 1.3 %collective-permute-start.2 = (bf16[16,4224]{1,0:T(8,128)(2,1)S(1)}, bf16[16,4224]{1,0:T(8,128)(2,1)S(1)}, u32[]{:S(2)}, u32[]{:S(2)}) collective-permute-start(bf16[16,4224]{1,0:T(8,128)(2,1)S(1)} %pack.1.refs_0_), channel_id=1, source_target_pairs={{0,4},{4,0},{8,12},{12,8},{1,5},{5,1},{9,13},{13,9},{2,6},{6,2},{1... | collective-permute-start | bytes 405512 | tf_op jit(solution)/shard_map/ppermute | solution.py:383
  3.5 7.0 %collective-permute-done.refs_1_ = bf16[16,4224]{1,0:T(8,128)(2,1)S(1)} collective-permute-done((bf16[16,4224]{1,0:T(8,128)(2,1)S(1)}, bf16[16,4224]{1,0:T(8,128)(2,1)S(1)}, u32[]{:S(2)}, u32[]{:S(2)}) %collective-permute-start) | collective-permute-done | bytes 135200 | tf_op jit(solution)/shard_map/ppermute | solution.py:383
  10.5 1.0 %collective-permute-start.1 = (bf16[16,4224]{1,0:T(8,128)(2,1)S(1)}, bf16[16,4224]{1,0:T(8,128)(2,1)S(1)}, u32[]{:S(2)}, u32[]{:S(2)}) collective-permute-start(bf16[16,4224]{1,0:T(8,128)(2,1)S(1)} %collective-permute-done.refs_1_), channel_id=1, source_target_pairs={{0,4},{4,0},{8,12},{12,8},{1,5},{5,1},{9,13},{13,9},{2,6},{6,2},{1... | collective-permute-start | bytes 405512 | tf_op jit(solution)/shard_map/ppermute | solution.py:383
  11.5 3.8 %load.1 = (bf16[8,96,2048]{2,1,0:T(8,128)(2,1)S(1)}, bf16[32,32,512]{2,1,0:T(8,128)(2,1)S(1)}, bf16[32,2,32,64]{3,2,1,0:T(8,128)(2,1)S(1)}, bf16[32,2048]{1,0:T(...) custom-call(bf16[8,96,2048]{2,1,0:T(8,128)(2,1)} %refs_0_.1, ...), custom_call_target="tpu_custom_call" | custom-call | bytes 17629184 | tf_op jit(solution)/shard_map/load/pallas_call | solution.py:352
  15.3 0.4 collective-permute-done.1.refs_2_
  15.7 1.0 %down.1 = (f32[96,128]{1,0:T(8,128)S(1)}, f32[128,128]{1,0:T(8,128)S(1)}) custom-call(bf16[16,4224]{1,0:T(8,128)(2,1)S(1)} %pack.1.refs_0_, bf16[16,4224]{1,0:T(8,128)(2,1)S(1)} %collective-permute-done.refs_1_, bf16[16,4224]{1,0:T(8,128)(2,1)S(1)} %collective-permute-done.1.refs_2_, bf16[16,4224]{1,0:T(8,128)(2,1)S(1)} %collective-permute-done.2.refs_3_, ...), custom_call_target="tpu_custom_call" | custom-call | tf_op jit(solution)/shard_map/down/pallas_call | solution.py:371
  16.8 1.6 %collective-permute-start.4 = (f32[96,128]{1,0:T(8,128)S(1)}, f32[96,128]{1,0:T(8,128)S(1)}, u32[]{:S(2)}, u32[]{:S(2)}) collective-permute-start(f32[96,128]{1,0:T(8,128)S(1)} %get-tuple-element.23), channel_id=1, source_target_pairs={{0,2},{1,3},{2,0},{3,1},{4,6},{5,7},{6,4},{7,5},{8,10},{9,11},{10,... | collective-permute-start | bytes 147464 | tf_op jit(solution)/shard_map/ppermute | solution.py:383
  18.3 0.3 collective-permute-start.5
  18.8 1.9 %collective-permute-done.3 = f32[96,128]{1,0:T(8,128)S(1)} collective-permute-done((f32[96,128]{1,0:T(8,128)S(1)}, f32[96,128]{1,0:T(8,128)S(1)}, u32[]{:S(2)}, u32[]{:S(2)}) %collective-permute-start.3) | collective-permute-done | bytes 49184 | tf_op jit(solution)/shard_map/ppermute | solution.py:383
  20.8 0.9 %collective-permute-done.4 = f32[96,128]{1,0:T(8,128)S(1)} collective-permute-done((f32[96,128]{1,0:T(8,128)S(1)}, f32[96,128]{1,0:T(8,128)S(1)}, u32[]{:S(2)}, u32[]{:S(2)}) %collective-permute-start.4) | collective-permute-done | bytes 49184 | tf_op jit(solution)/shard_map/ppermute | solution.py:383
  21.7 0.5 %collective-permute-start.6 = (bf16[96,128]{1,0:T(8,128)(2,1)S(1)}, bf16[96,128]{1,0:T(8,128)(2,1)S(1)}, u32[]{:S(2)}, u32[]{:S(2)}) collective-permute-start(bf16[96,128]{1,0:T(8,128)(2,1)S(1)} %add_convert_fusion.refs_0_), channel_id=1, source_target_pairs={{0,12},{4,8},{8,4},{12,0},{1,13},{5,9},{9,5},{13,1},{2,14},{6,10},... | collective-permute-start | bytes 73736 | tf_op jit(solution)/shard_map/ppermute | solution.py:383
  22.2 2.8 %collective-permute-start.7 = (bf16[96,128]{1,0:T(8,128)(2,1)S(1)}, bf16[96,128]{1,0:T(8,128)(2,1)S(1)}, u32[]{:S(2)}, u32[]{:S(2)}) collective-permute-start(bf16[96,128]{1,0:T(8,128)(2,1)S(1)} %add_convert_fusion.refs_0_), channel_id=1, source_target_pairs={{0,8},{4,12},{8,0},{12,4},{1,9},{5,13},{9,1},{13,5},{2,10},{6,14},... | collective-permute-start | bytes 73736 | tf_op jit(solution)/shard_map/ppermute | solution.py:383
  25.3 0.3 collective-permute-done.6.refs_1_
  25.6 1.6 %collective-permute-done.7.refs_2_ = bf16[96,128]{1,0:T(8,128)(2,1)S(1)} collective-permute-done((bf16[96,128]{1,0:T(8,128)(2,1)S(1)}, bf16[96,128]{1,0:T(8,128)(2,1)S(1)}, u32[]{:S(2)}, u32[]{:S(2)}) %collective-permute-start.7) | collective-permute-done | bytes 24608 | tf_op jit(solution)/shard_map/ppermute | solution.py:383
  27.2 1.6 %collective-permute-done.8.refs_3_ = bf16[96,128]{1,0:T(8,128)(2,1)S(1)} collective-permute-done((bf16[96,128]{1,0:T(8,128)(2,1)S(1)}, bf16[96,128]{1,0:T(8,128)(2,1)S(1)}, u32[]{:S(2)}, u32[]{:S(2)}) %collective-permute-start.8) | collective-permute-done | bytes 24608 | tf_op jit(solution)/shard_map/ppermute | solution.py:383
  28.8 1.1 %up.1 = (f32[32,1408]{1,0:T(8,128)S(1)}, f32[32,1408]{1,0:T(8,128)S(1)}) custom-call(f32[128,128]{1,0:T(8,128)S(1)} %get-tuple-element.22.ids_ref, bf16[96,128]{1,0:T(8,128)(2,1)S(1)} %add_convert_fusion.refs_0_, bf16[96,128]{1,0:T(8,128)(2,1)S(1)} %collective-permute-done.6.refs_1_, bf16[96,128]{1,0:T(8,128)(2,1)S(1)} %collective-permute-done.7.refs_2_, ...), custom_call_target="tpu_custom_call" | custom-call | tf_op jit(solution)/shard_map/up/pallas_call | solution.py:371
  29.9 1.0 %collective-permute-start.12 = (f16[32,1408]{1,0:T(8,128)(2,1)S(1)}, f16[32,1408]{1,0:T(8,128)(2,1)S(1)}, u32[]{:S(2)}, u32[]{:S(2)}) collective-permute-start(f16[32,1408]{1,0:T(8,128)(2,1)S(1)} %convert_element_type.22), channel_id=1, source_target_pairs={{0,8},{1,12},{2,4},{3,0},{4,5},{5,13},{6,9},{7,1},{8,6},{9,10},{10... | collective-permute-start | bytes 270344 | tf_op jit(solution)/shard_map/ppermute | solution.py:474
  30.9 1.8 %collective-permute-start.11 = (f16[32,1408]{1,0:T(8,128)(2,1)S(1)}, f16[32,1408]{1,0:T(8,128)(2,1)S(1)}, u32[]{:S(2)}, u32[]{:S(2)}) collective-permute-start(f16[32,1408]{1,0:T(8,128)(2,1)S(1)} %convert_element_type.19), channel_id=1, source_target_pairs={{0,4},{1,0},{2,8},{3,12},{4,9},{5,1},{6,5},{7,13},{8,2},{9,14},{10... | collective-permute-start | bytes 270344 | tf_op jit(solution)/shard_map/ppermute | solution.py:474
  32.8 2.8 %collective-permute-done.12 = f16[32,1408]{1,0:T(8,128)(2,1)S(1)} collective-permute-done((f16[32,1408]{1,0:T(8,128)(2,1)S(1)}, f16[32,1408]{1,0:T(8,128)(2,1)S(1)}, u32[]{:S(2)}, u32[]{:S(2)}) %collective-permute-start.12) | collective-permute-done | bytes 90144 | tf_op jit(solution)/shard_map/ppermute | solution.py:474
  35.6 1.5 %attend.2 = (bf16[32,2048]{1,0:T(8,128)(2,1)}, bf16[32,256]{1,0:T(8,128)(2,1)}, bf16[32,256]{1,0:T(8,128)(2,1)}) custom-call(f32[32,1408]{1,0:T(8,128)S(1)} %convert_element_type.23.refs_0_, bf16[32,2048]{1,0:T(8,128)(2,1)S(1)} %get-tuple-element.28.refs_1_, bf16[32,256]{1,0:T(8,128)(2,1)S(1)} %get-tuple-element.29.refs_2_, ...), custom_call_target="tpu_custom_call" | custom-call | tf_op jit(solution)/shard_map/attend/pallas_call | solution.py:319
  37.1 0.3 collective-permute-done.11
  37.5 1.5 %attend.3 = (bf16[32,2048]{1,0:T(8,128)(2,1)}, bf16[32,256]{1,0:T(8,128)(2,1)}, bf16[32,256]{1,0:T(8,128)(2,1)}) custom-call(f32[32,1408]{1,0:T(8,128)S(1)} %convert_element_type.20.refs_0_, bf16[32,2048]{1,0:T(8,128)(2,1)S(1)} %get-tuple-element.28.refs_1_, ...), custom_call_target="tpu_custom_call", output_to_operand_aliasing={{0}: (9, {}), {1}: (10, {}), {2}: (11, {})} | custom-call | tf_op jit(solution)/shard_map/attend/pallas_call | solution.py:319
  (20 shorter events, 0.9 us)
Async XLA Ops:
  1.5 27.3 %collective-permute-start.9 = (bf16[32,32,512]{2,1,0:T(8,128)(2,1)}, bf16[32,32,512]{2,1,0:T(8,128)(2,1)S(1)}, u32[]{:S(2)}, u32[]{:S(2)}) collective-permute-start(bf16[32,32,512]{2,1,0:T(8,128)(2,1)} %refs_1_.1), channel_id=1, source_target_pairs={{0,1},{1,0},{2,3},{3,2},{4,5},{5,4},{6,7},{7,6},{8,9},{9,8},{10,11... | collective-permute-start | bytes 3145736 | tf_op jit(solution)/shard_map/ppermute | solution.py:383
  1.6 8.9 %collective-permute-start = (bf16[16,4224]{1,0:T(8,128)(2,1)S(1)}, bf16[16,4224]{1,0:T(8,128)(2,1)S(1)}, u32[]{:S(2)}, u32[]{:S(2)}) collective-permute-start(bf16[16,4224]{1,0:T(8,128)(2,1)S(1)} %pack.1.refs_0_), channel_id=1, source_target_pairs={{0,12},{4,8},{8,4},{12,0},{1,13},{5,9},{9,5},{13,1},{2,14},{6,10},... | collective-permute-start | bytes 405512 | tf_op jit(solution)/shard_map/ppermute | solution.py:383
  2.1 13.2 %collective-permute-start.2 = (bf16[16,4224]{1,0:T(8,128)(2,1)S(1)}, bf16[16,4224]{1,0:T(8,128)(2,1)S(1)}, u32[]{:S(2)}, u32[]{:S(2)}) collective-permute-start(bf16[16,4224]{1,0:T(8,128)(2,1)S(1)} %pack.1.refs_0_), channel_id=1, source_target_pairs={{0,4},{4,0},{8,12},{12,8},{1,5},{5,1},{9,13},{13,9},{2,6},{6,2},{1... | collective-permute-start | bytes 405512 | tf_op jit(solution)/shard_map/ppermute | solution.py:383
  10.5 5.2 %collective-permute-start.1 = (bf16[16,4224]{1,0:T(8,128)(2,1)S(1)}, bf16[16,4224]{1,0:T(8,128)(2,1)S(1)}, u32[]{:S(2)}, u32[]{:S(2)}) collective-permute-start(bf16[16,4224]{1,0:T(8,128)(2,1)S(1)} %collective-permute-done.refs_1_), channel_id=1, source_target_pairs={{0,4},{4,0},{8,12},{12,8},{1,5},{5,1},{9,13},{13,9},{2,6},{6,2},{1... | collective-permute-start | bytes 405512 | tf_op jit(solution)/shard_map/ppermute | solution.py:383
  15.3 3.4 %copy-start.1 = (bf16[32,2,32,64]{3,2,1,0:T(8,128)(2,1)S(1)}, bf16[32,2,32,64]{3,2,1,0:T(8,128)(2,1)}, u32[]{:S(2)}) copy-start(bf16[32,2,32,64]{3,2,1,0:T(8,128)(2,1)} %refs_2_.1) | copy-start | bytes 786436
  15.3 10.0 %copy-start = (s32[32]{0:T(128)S(1)}, s32[32]{0:T(128)}, u32[]{:S(2)}) copy-start(s32[32]{0:T(128)} %param.21) | copy-start | bytes 388
  16.7 4.1 %collective-permute-start.3 = (f32[96,128]{1,0:T(8,128)S(1)}, f32[96,128]{1,0:T(8,128)S(1)}, u32[]{:S(2)}, u32[]{:S(2)}) collective-permute-start(f32[96,128]{1,0:T(8,128)S(1)} %get-tuple-element.23), channel_id=1, source_target_pairs={{0,3},{1,2},{2,1},{3,0},{4,7},{5,6},{6,5},{7,4},{8,11},{9,10},{10,... | collective-permute-start | bytes 147464 | tf_op jit(solution)/shard_map/ppermute | solution.py:383
  16.8 4.9 %collective-permute-start.4 = (f32[96,128]{1,0:T(8,128)S(1)}, f32[96,128]{1,0:T(8,128)S(1)}, u32[]{:S(2)}, u32[]{:S(2)}) collective-permute-start(f32[96,128]{1,0:T(8,128)S(1)} %get-tuple-element.23), channel_id=1, source_target_pairs={{0,2},{1,3},{2,0},{3,1},{4,6},{5,7},{6,4},{7,5},{8,10},{9,11},{10,... | collective-permute-start | bytes 147464 | tf_op jit(solution)/shard_map/ppermute | solution.py:383
  18.3 3.3 %collective-permute-start.5 = (f32[96,128]{1,0:T(8,128)S(1)}, f32[96,128]{1,0:T(8,128)S(1)}, u32[]{:S(2)}, u32[]{:S(2)}) collective-permute-start(f32[96,128]{1,0:T(8,128)S(1)} %get-tuple-element.23), channel_id=1, source_target_pairs={{0,1},{1,0},{2,3},{3,2},{4,5},{5,4},{6,7},{7,6},{8,9},{9,8},{10,11... | collective-permute-start | bytes 147464 | tf_op jit(solution)/shard_map/ppermute | solution.py:383
  18.6 6.7 %collective-permute-start.10 = (bf16[32,2,32,64]{3,2,1,0:T(8,128)(2,1)S(1)}, bf16[32,2,32,64]{3,2,1,0:T(8,128)(2,1)S(1)}, u32[]{:S(2)}, u32[]{:S(2)}) collective-permute-start(bf16[32,2,32,64]{3,2,1,0:T(8,128)(2,1)S(1)} %copy-done.1), channel_id=1, source_target_pairs={{0,1},{1,0},{2,3},{3,2},{4,5},{5,4},{6,7},{7,6},{8,9},{9,8},{10,11... | collective-permute-start | bytes 786440 | tf_op jit(solution)/shard_map/ppermute | solution.py:383
  21.7 3.9 %collective-permute-start.6 = (bf16[96,128]{1,0:T(8,128)(2,1)S(1)}, bf16[96,128]{1,0:T(8,128)(2,1)S(1)}, u32[]{:S(2)}, u32[]{:S(2)}) collective-permute-start(bf16[96,128]{1,0:T(8,128)(2,1)S(1)} %add_convert_fusion.refs_0_), channel_id=1, source_target_pairs={{0,12},{4,8},{8,4},{12,0},{1,13},{5,9},{9,5},{13,1},{2,14},{6,10},... | collective-permute-start | bytes 73736 | tf_op jit(solution)/shard_map/ppermute | solution.py:383
  22.2 5.0 %collective-permute-start.7 = (bf16[96,128]{1,0:T(8,128)(2,1)S(1)}, bf16[96,128]{1,0:T(8,128)(2,1)S(1)}, u32[]{:S(2)}, u32[]{:S(2)}) collective-permute-start(bf16[96,128]{1,0:T(8,128)(2,1)S(1)} %add_convert_fusion.refs_0_), channel_id=1, source_target_pairs={{0,8},{4,12},{8,0},{12,4},{1,9},{5,13},{9,1},{13,5},{2,10},{6,14},... | collective-permute-start | bytes 73736 | tf_op jit(solution)/shard_map/ppermute | solution.py:383
  25.0 3.8 %collective-permute-start.8 = (bf16[96,128]{1,0:T(8,128)(2,1)S(1)}, bf16[96,128]{1,0:T(8,128)(2,1)S(1)}, u32[]{:S(2)}, u32[]{:S(2)}) collective-permute-start(bf16[96,128]{1,0:T(8,128)(2,1)S(1)} %add_convert_fusion.refs_0_), channel_id=1, source_target_pairs={{0,4},{4,0},{8,12},{12,8},{1,5},{5,1},{9,13},{13,9},{2,6},{6,2},{1... | collective-permute-start | bytes 73736 | tf_op jit(solution)/shard_map/ppermute | solution.py:383
  29.9 5.7 %collective-permute-start.12 = (f16[32,1408]{1,0:T(8,128)(2,1)S(1)}, f16[32,1408]{1,0:T(8,128)(2,1)S(1)}, u32[]{:S(2)}, u32[]{:S(2)}) collective-permute-start(f16[32,1408]{1,0:T(8,128)(2,1)S(1)} %convert_element_type.22), channel_id=1, source_target_pairs={{0,8},{1,12},{2,4},{3,0},{4,5},{5,13},{6,9},{7,1},{8,6},{9,10},{10... | collective-permute-start | bytes 270344 | tf_op jit(solution)/shard_map/ppermute | solution.py:474
  30.9 6.5 %collective-permute-start.11 = (f16[32,1408]{1,0:T(8,128)(2,1)S(1)}, f16[32,1408]{1,0:T(8,128)(2,1)S(1)}, u32[]{:S(2)}, u32[]{:S(2)}) collective-permute-start(f16[32,1408]{1,0:T(8,128)(2,1)S(1)} %convert_element_type.19), channel_id=1, source_target_pairs={{0,4},{1,0},{2,8},{3,12},{4,9},{5,1},{6,5},{7,13},{8,2},{9,14},{10... | collective-permute-start | bytes 270344 | tf_op jit(solution)/shard_map/ppermute | solution.py:474
